TPU v7x, 128 devices: a whole 4x4x4 slice. The times are simulated.
128 devices in a mesh: ctx: 16 (over y, z), tp: 8 (over x, core).
Axes of the slice: x: 4, y: 4, z: 4, core: 2. Of those that a mesh axis runs over, the one named last changes fastest.
Arguments:
- projected: bfloat16 [8192, 5, 8192], P('ctx', None, 'tp'), may hold values from -6 to 6
- route: int32 [8192], P('ctx'), may hold values from 0 to 15, as said below
- contig_len: int32 [8], replicated, may hold values from 1 to 4096, 8192 in all
- mr_filter: float32 [128, 8192], P(None, 'tp'), may hold values from -0.5 to 0.5
- out_weight: bfloat16 [8192, 8192], P('tp'), may hold values from -0.0625 to 0.0625
- li_rate: float32 [16, 8192], P(None, 'tp'), may hold values from 6.1035157e-06 to 0.033
- li_residue: float32 [16, 8192], P(None, 'tp'), may hold values from -1.5 to 1.5
Outputs:
- mixed: bfloat16 [8192, 8192], P('ctx', 'tp')
Inputs may be any that keep to these rules, and one draw needn't show every extreme that they name: `route`: of the 512 rows of one ctx index, at most 48 name the same context shard, and some do in every draw; every context shard is named by exactly 512 rows in all.
All inputs are finite; a program needn't handle non-finite values.
Results may differ from a plain program's by a relative error of at most 0.02.
Values may be sent and summed in bfloat16 or wider, within the bound.
No kernel may reach another device: no remote copies, remote signals or barrier semaphores. Data moves between devices by JAX's collectives and lax.ppermute only.
A program may use at most 192 MiB of HBM per device.

v0:
```python
import jax
import jax.numpy as jnp
from jax import lax
from jax.sharding import PartitionSpec as P


def from_behind(shard, axis, by):
    count = lax.axis_size(axis)
    pairs = [(i, i + by) for i in range(count) if 0 <= i + by < count]
    return lax.ppermute(shard, axis, pairs)


def pair_combine(first_pair, second_pair):
    return (first_pair[0] * second_pair[0], second_pair[0] * first_pair[1] + second_pair[1])


def tap_filter(padded, taps, rows):
    tap_total = taps.shape[0]
    channels = padded.shape[1]
    kernel = taps[::-1].reshape(tap_total, 1, channels)
    result = lax.conv_general_dilated(
        padded[None],
        kernel,
        window_strides=(1,),
        padding="VALID",
        dimension_numbers=("NWC", "WIO", "NWC"),
        feature_group_count=channels,
        precision=lax.Precision.HIGHEST,
        preferred_element_type=jnp.float32,
    )
    return result[0, :rows]


def on_device(projected, route, contig_len, mr_filter, out_weight, li_rate, li_residue):
    tok_rows = projected.shape[0]
    channels = projected.shape[2]
    ctx_count = lax.axis_size("ctx")
    slot_count = 3 * tok_rows // (2 * ctx_count)
    ctx_index = lax.axis_index("ctx")
    peer_ids = jnp.arange(ctx_count, dtype=jnp.int32)
    row_ids = jnp.arange(tok_rows, dtype=jnp.int32)
    every_route = lax.all_gather(route, "ctx", axis=0, tiled=True)
    one_hot = (route[:, None] == peer_ids[None, :]).astype(jnp.int32)
    row_rank = jnp.sum((jnp.cumsum(one_hot, axis=0) - one_hot) * one_hot, axis=1)
    send_slot = route * slot_count + row_rank
    source_row = jnp.full((ctx_count * slot_count,), tok_rows, jnp.int32).at[send_slot].set(row_ids)
    flat_rows = projected.reshape(tok_rows, 5 * channels)
    outgoing = jnp.take(flat_rows, source_row, axis=0, mode="fill", fill_value=0)
    to_here = (every_route.reshape(ctx_count, tok_rows) == ctx_index).astype(jnp.int32)
    counts = jnp.sum(to_here, axis=1)
    run_ends = jnp.cumsum(counts)
    offsets = run_ends - counts
    source = jnp.sum((run_ends[None, :] <= row_ids[:, None]).astype(jnp.int32), axis=1)
    source_hot = (source[:, None] == peer_ids[None, :]).astype(jnp.int32)
    flat_slot = source * slot_count + row_ids - jnp.sum(source_hot * offsets[None, :], axis=1)
    received = lax.all_to_all(outgoing, "ctx", split_axis=0, concat_axis=0, tiled=True)
    ordered = jnp.take(received, flat_slot, axis=0).reshape(tok_rows, 5, channels)
    mr_part = ordered[:, :3]
    li_part = ordered[:, 3:]
    tap_count = mr_filter.shape[0]
    rim_rows = from_behind(mr_part[tok_rows - (tap_count - 1) :, 1:3], "ctx", 1)
    extended = jnp.concatenate([rim_rows, mr_part[:, 1:3]], axis=0)
    u_mr = extended[:, 0].astype(jnp.float32) * extended[:, 1].astype(jnp.float32)
    filtered = tap_filter(u_mr, mr_filter, tok_rows)
    gated = (mr_part[:, 0].astype(jnp.float32) * filtered).astype(jnp.bfloat16)
    partial_value = jnp.dot(gated, out_weight, preferred_element_type=jnp.float32)
    mr_out = lax.psum_scatter(
        partial_value.astype(jnp.bfloat16), "tp", scatter_dimension=1, tiled=True
    ).astype(jnp.float32)
    span_len = 16
    groups = tok_rows // span_len
    mode_weight = li_residue * jnp.sqrt(-jnp.expm1(-2.0 * li_rate))
    u_li = li_part[:, 1].astype(jnp.float32) * mr_out
    starts = jnp.cumsum(contig_len) - contig_len
    seq_pos = ctx_index * tok_rows + row_ids
    is_start = jnp.any(seq_pos[:, None] == starts[None, :], axis=1).astype(jnp.int32)
    segment = jnp.sum((seq_pos[:, None] >= starts[None, :]).astype(jnp.int32), axis=1)
    u_spans = u_li.reshape(groups, span_len, channels)
    seg_spans = segment.reshape(groups, span_len)
    lag_steps = jnp.arange(span_len, dtype=jnp.float32)
    powers = jnp.exp(-li_rate[None, :, :] * lag_steps[:, None, None])
    kernel = jnp.sum(mode_weight[None] * powers, axis=1)
    within = jnp.zeros((groups, span_len, channels), jnp.float32)
    for lag_step in range(span_len):
        shifted = jnp.pad(u_spans[:, : span_len - lag_step], ((0, 0), (lag_step, 0), (0, 0)))
        earlier_seg = jnp.pad(
            seg_spans[:, : span_len - lag_step], ((0, 0), (lag_step, 0)), constant_values=-1
        )
        same_seg = (seg_spans == earlier_seg).astype(jnp.float32)
        within = within + kernel[lag_step][None, None, :] * shifted * same_seg[:, :, None]
    last_same = (seg_spans == seg_spans[:, -1:]).astype(jnp.float32)
    tail_powers = powers[::-1]
    span_state = jnp.einsum(
        "gjc,jnc->gnc",
        u_spans * last_same[:, :, None],
        tail_powers,
        precision=lax.Precision.HIGHEST,
    )
    start_spans = is_start.reshape(groups, span_len)
    clear_span = jnp.sum(start_spans, axis=1) == 0
    step_decay = jnp.exp(-li_rate * float(span_len))
    span_factor = jnp.where(clear_span[:, None, None], step_decay[None], 0.0)
    total_factor, total_state = lax.associative_scan(
        pair_combine, (span_factor, span_state), axis=0
    )
    dev_factor = total_factor[-1]
    dev_state = total_state[-1]

    def hand_on(hop_step, carry_pair):
        incoming_now = from_behind(carry_pair[1].astype(jnp.bfloat16), "ctx", 1).astype(jnp.float32)
        return (incoming_now, dev_factor * incoming_now + dev_state)

    incoming, _ = lax.fori_loop(0, ctx_count - 1, hand_on, (jnp.zeros_like(dev_state), dev_state))
    entering = jnp.concatenate(
        [incoming[None], total_factor[:-1] * incoming[None] + total_state[:-1]], axis=0
    )
    lead_powers = jnp.exp(-li_rate[None] * (lag_steps[:, None, None] + 1.0)) * mode_weight[None]
    carried = jnp.einsum("gnc,inc->gic", entering, lead_powers, precision=lax.Precision.HIGHEST)
    open_rows = (jnp.cumsum(start_spans, axis=1) == 0).astype(jnp.float32)
    li_out = (within + carried * open_rows[:, :, None]).reshape(tok_rows, channels)
    y_seq = (li_part[:, 0].astype(jnp.float32) * li_out).astype(jnp.bfloat16)
    back_row = jnp.full((ctx_count * slot_count,), tok_rows, jnp.int32).at[flat_slot].set(row_ids)
    homeward = jnp.take(y_seq, back_row, axis=0, mode="fill", fill_value=0)
    returned = lax.all_to_all(homeward, "ctx", split_axis=0, concat_axis=0, tiled=True)
    return jnp.take(returned, send_slot, axis=0)


def solution(mesh):
    return jax.shard_map(
        on_device,
        mesh=mesh,
        in_specs=(
            P("ctx", None, "tp"),
            P("ctx"),
            P(),
            P(None, "tp"),
            P("tp", None),
            P(None, "tp"),
            P(None, "tp"),
        ),
        out_specs=P("ctx", "tp"),
        check_vma=False,
    )
```

profile of v0, /device:TPU:0, one launch (start us, length us, event | category | flops | bytes accessed | tf_op | source)
XLA Modules:
  0.0 752.0 jit_solution(10146862001931184243)
XLA Ops:
  13.2 7.8 %copy.391 = bf16[512,5,1024]{0,2,1:T(8,128)(2,1)} copy(bf16[512,5,1024]{2,0,1:T(8,128)(2,1)} %param.9) | data formatting | bytes 10485760 | tf_op args[0]
  21.0 8.0 %copy.392 = bf16[512,5120]{1,0:T(8,128)(2,1)} copy(bf16[512,5120]{0,1:T(8,128)(2,1)} %bitcast.111) | data formatting | bytes 10485760 | tf_op jit(solution)/shard_map/reshape | solution.py:47
  29.1 17.9 %gather_fusion = bf16[768,5120]{1,0:T(8,128)(2,1)} fusion(bf16[512,5120]{1,0:T(8,128)(2,1)} %copy.392, s32[1024]{0:T(1024)S(1)} %pad_clamp_fusion.3), kind=kCustom, calls=%fused_computation | custom fusion | bytes 15731712 | tf_op jit(solution)/shard_map/jit(_take)/gather | solution.py:48
  47.0 6.9 broadcast_select_fusion
  53.8 8.3 %all-to-all-start = ((bf16[16,48,5120]{2,1,0:T(8,128)(2,1)}), bf16[16,48,5120]{2,1,0:T(8,128)(2,1)}, u32[]{:S(2)}, u32[]{:S(2)}) async-start(bf16[16,48,5120]{2,1,0:T(8,128)(2,1)} %broadcast_select_fusion), calls=%async_computation | async-start | bytes 15728640 | tf_op jit(solution)/shard_map/all_to_all | solution.py:56
  62.2 153.5 %all-gather = s32[16,1,512]{2,1,0:T(1,128)S(1)} all-gather(s32[1,1,512]{2,1,0:T(1,128)S(1)} %bitcast.134), channel_id=1, replica_groups=mesh['ctx'=16,'tp'=8] {'ctx'}, dimensions={0}, use_global_device_ids=true | all-gather | bytes 34816 | tf_op jit(solution)/shard_map/all_gather | solution.py:42
  216.6 14.7 %gather_fusion.1 = bf16[512,5120]{1,0:T(8,128)(2,1)} fusion(bf16[768,5120]{1,0:T(8,128)(2,1)} %bitcast.9, s32[1024]{0:T(1024)S(1)} %pad_clamp_fusion.2), kind=kCustom, calls=%fused_computation.1 | custom fusion | bytes 10487808 | tf_op jit(solution)/shard_map/jit(_take)/gather | solution.py:57
  231.3 7.9 %copy.393 = bf16[512,5120]{0,1:T(8,128)(2,1)} copy(bf16[512,5120]{1,0:T(8,128)(2,1)} %gather_fusion.1) | data formatting | bytes 10485760 | tf_op jit(solution)/shard_map/jit(_take)/gather | solution.py:57
  239.2 8.0 %copy.394 = bf16[512,5,1024]{2,0,1:T(8,128)(2,1)} copy(bf16[512,5,1024]{0,2,1:T(8,128)(2,1)} %bitcast.110) | data formatting | bytes 10485760 | tf_op jit(solution)/shard_map/jit(_take)/gather | solution.py:57
  263.1 22.5 %fusion.11 = f32[1,512,1024]{2,0,1:T(1,128)S(1)} fusion(f32[1,639,1024]{2,1,0:T(8,128)S(1)} %multiply_bitcast_fusion, f32[128,1,1024]{2,0,1:T(8,128)S(1)} %bitcast.131), kind=kOutput, calls=%fused_computation.27 | convolution fusion | flops 805306368 | bytes 5238784 | tf_op jit(solution)/shard_map/conv_general_dilated | solution.py:21
  285.6 14.7 %convolution_convert_fusion = bf16[512,8192]{1,0:T(8,128)(2,1)} fusion(bf16[1024,8192]{1,0:T(8,128)(2,1)} %param.13, f32[1,512,1024]{2,0,1:T(1,128)S(1)} %fusion.11, bf16[512,5,1024]{2,0,1:T(8,128)(2,1)} %copy-done), kind=kOutput, calls=%fused_computation.7 | convolution fusion | flops 8595701760 | bytes 28311552 | tf_op jit(solution)/shard_map/dot_general | solution.py:66
  307.1 12.0 %rev.7 = f32[16,16,1024]{1,0,2:T(8,128)} reverse(f32[16,16,1024]{1,0,2:T(8,128)} %get-tuple-element.81), dimensions={0} | reverse | bytes 2097152 | tf_op jit(solution)/shard_map/rev | solution.py:92
  338.6 15.8 %reduce-scatter.2.cloned.1.call-done = bf16[512,1024]{1,0:T(8,128)(2,1)} async-done(((bf16[512,8192]{1,0:T(8,128)(2,1)}), bf16[512,1024]{1,0:T(8,128)(2,1)}) %reduce-scatter.2.cloned.1.call-update) | async-done | bytes 1048592 | tf_op jit(solution)/shard_map/reduce_scatter | solution.py:67
  356.4 6.8 copy.399
  363.1 17.3 %fusion.1 = f32[1024,16,32]{2,1,0:T(8,128)} fusion(f32[16,16,1024]{1,0,2:T(8,128)} %rev.7, f32[32,16,1024]{0,1,2:T(8,128)} %copy.399, f32[32,16]{0,1:T(8,128)S(1)} %copy.430), kind=kOutput, calls=%fused_computation.10 | convolution fusion | flops 101187584 | bytes 5244928 | tf_op jit(solution)/shard_map/gjc,jnc->gnc/dot_general | solution.py:93
  470.7 6.5 pad.230
  503.2 10.2 %pad.381 = f32[32,16,1024]{2,1,0:T(8,128)} pad(f32[16,16,1024]{2,1,0:T(8,128)} %add.331, f32[]{:T(128)} %constant.101.clone.1), padding=1_0_1x0_0_0x0_0_0 | pad | bytes 3145732
  515.1 116.4 %while.12 = (s32[]{:T(128)}, f32[16,1024]{1,0:T(8,128)}, bf16[16,1024]{1,0:T(8,128)(2,1)S(1)}, f32[16,1024]{1,0:T(8,128)S(1)}, f32[16,1024]{1,0:T(8,128)S(1)}, /*index=5*/s32[]{:T(128)}) while((s32[]{:T(128)}, f32[16,1024]{1,0:T(8,128)}, bf16[16,1024]{1,0:T(8,128)(2,1)S(1)}, f32[16,1024]{1,0:T(8,128)S(1)}, f32[16,1024]{1,0:T(8,128)S(1)}, ...), condition=%wide.region_16.17_spmd, body=%wide.region_15.16_spmd.sunk | while | flops 65538 | bytes 393325 | solution.py:113
  571.2 6.5 collective-permute-start
  579.9 6.5 collective-permute-start
  635.8 6.5 copy.434
  642.7 54.7 %fusion = f32[32,16,1024]{0,1,2:T(8,128)} fusion(f32[32,1,1024]{0,1,2:T(1,128)} %slice.494, f32[32,2,1024]{0,1,2:T(2,128)} %slice.491, f32[32,3,1024]{0,1,2:T(4,128)} %slice.488, f32[32,4,1024]{0,1,2:T(4,128)} %slice.485, f32[32,5,1024]{0,1,2:T(8,128)} %slice.482, f32[32,6,1024]{0,1,2:T(8,128)} %slice.479, f32[32,7,1024]{0,1,2:T(8,128)} %slice.476, ...), kind=kOutput, calls=%fused_computation.9 | convolution fusion | flops 126353408 | bytes 22249536 | tf_op jit(solution)/shard_map/gnc,inc->gic/dot_general | solution.py:118
  709.1 16.5 %all-to-all-start.1 = ((bf16[16,48,1024]{2,1,0:T(8,128)(2,1)}), bf16[16,48,1024]{2,1,0:T(8,128)(2,1)S(1)}, u32[]{:S(2)}, u32[]{:S(2)}) async-start(bf16[16,48,1024]{2,1,0:T(8,128)(2,1)} %broadcast_select_fusion.2), calls=%async_computation.2 | async-start | bytes 3145728 | tf_op jit(solution)/shard_map/all_to_all | solution.py:124
  725.6 16.1 %all-to-all-done.1 = bf16[16,48,1024]{2,1,0:T(8,128)(2,1)S(1)} async-done(((bf16[16,48,1024]{2,1,0:T(8,128)(2,1)}), bf16[16,48,1024]{2,1,0:T(8,128)(2,1)S(1)}, u32[]{:S(2)}, u32[]{:S(2)}) %all-to-all-start.1) | async-done | bytes 1572896 | tf_op jit(solution)/shard_map/all_to_all | solution.py:124
  (302 shorter events, 291.5 us)
Async XLA Ops:
  53.8 162.7 %all-to-all-start = ((bf16[16,48,5120]{2,1,0:T(8,128)(2,1)}), bf16[16,48,5120]{2,1,0:T(8,128)(2,1)}, u32[]{:S(2)}, u32[]{:S(2)}) async-start(bf16[16,48,5120]{2,1,0:T(8,128)(2,1)} %broadcast_select_fusion), calls=%async_computation | async-start | bytes 15728640 | tf_op jit(solution)/shard_map/all_to_all | solution.py:56
  62.1 292.3 %reduce-scatter.2.cloned.1.call-start = ((), (), s32[]{:S(2)}) async-start(), calls=%async_computation.3 | async-start | bytes 9437184 | tf_op jit(solution)/shard_map/reduce_scatter | solution.py:67
  252.8 9.8 %collective-permute-start.1 = (bf16[127,2,1024]{2,0,1:T(8,128)(2,1)S(1)}, bf16[127,2,1024]{2,0,1:T(8,128)(2,1)S(1)}, u32[]{:S(2)}, u32[]{:S(2)}) collective-permute-start(bf16[127,2,1024]{2,0,1:T(8,128)(2,1)S(1)} %slice.447), channel_id=1, source_target_pairs={{0,8},{8,16},{16,24},{24,32},{32,40},{40,48},{48,56},{56,64},{64,7... | collective-permute-start | bytes 1560584 | tf_op jit(solution)/shard_map/ppermute | solution.py:10
  302.4 16.7 %copy-start.9 = (f32[16,1024]{0,1:T(8,128)}, f32[16,1024]{0,1:T(8,128)S(1)}, u32[]{:S(2)}) copy-start(f32[16,1024]{0,1:T(8,128)S(1)} %copy.395) | copy-start | bytes 196612
  302.7 16.5 %copy-start.11 = (f32[16,1024]{0,1:T(8,128)}, f32[16,1024]{0,1:T(8,128)S(1)}, u32[]{:S(2)}) copy-start(f32[16,1024]{0,1:T(8,128)S(1)} %copy.396) | copy-start | bytes 196612
  452.9 17.8 %slice-start.2 = ((f32[32,16,1024]{2,1,0:T(8,128)}), f32[1,16,1024]{2,1,0:T(8,128)S(1)}, s32[]{:S(2)}) async-start(f32[32,16,1024]{2,1,0:T(8,128)} %copy-done.1), calls=%async_computation.6 | async-start | bytes 131072 | tf_op jit(solution)/shard_map/slice | solution.py:103
  515.1 5.0 collective-permute-start
  520.7 5.8 collective-permute-start
  527.2 5.8 collective-permute-start
  533.6 5.8 collective-permute-start
  540.0 5.9 collective-permute-start
  546.6 6.9 collective-permute-start
  554.1 7.9 %collective-permute-start = (bf16[16,1024]{1,0:T(8,128)(2,1)S(1)}, bf16[16,1024]{1,0:T(8,128)(2,1)S(1)}, u32[]{:S(2)}, u32[]{:S(2)}) collective-permute-start(bf16[16,1024]{1,0:T(8,128)(2,1)S(1)} %get-tuple-element.159), channel_id=1, source_target_pairs={{0,8},{8,16},{16,24},{24,32},{32,40},{40,48},{48,56},{56,64},{64,7... | collective-permute-start | bytes 98312 | tf_op jit(solution)/shard_map/while/body/eval_jaxpr/ppermute | solution.py:10
  562.7 7.9 %collective-permute-start = (bf16[16,1024]{1,0:T(8,128)(2,1)S(1)}, bf16[16,1024]{1,0:T(8,128)(2,1)S(1)}, u32[]{:S(2)}, u32[]{:S(2)}) collective-permute-start(bf16[16,1024]{1,0:T(8,128)(2,1)S(1)} %get-tuple-element.159), channel_id=1, source_target_pairs={{0,8},{8,16},{16,24},{24,32},{32,40},{40,48},{48,56},{56,64},{64,7... | collective-permute-start | bytes 98312 | tf_op jit(solution)/shard_map/while/body/eval_jaxpr/ppermute | solution.py:10
  571.2 8.0 %collective-permute-start = (bf16[16,1024]{1,0:T(8,128)(2,1)S(1)}, bf16[16,1024]{1,0:T(8,128)(2,1)S(1)}, u32[]{:S(2)}, u32[]{:S(2)}) collective-permute-start(bf16[16,1024]{1,0:T(8,128)(2,1)S(1)} %get-tuple-element.159), channel_id=1, source_target_pairs={{0,8},{8,16},{16,24},{24,32},{32,40},{40,48},{48,56},{56,64},{64,7... | collective-permute-start | bytes 98312 | tf_op jit(solution)/shard_map/while/body/eval_jaxpr/ppermute | solution.py:10
  579.9 8.1 %collective-permute-start = (bf16[16,1024]{1,0:T(8,128)(2,1)S(1)}, bf16[16,1024]{1,0:T(8,128)(2,1)S(1)}, u32[]{:S(2)}, u32[]{:S(2)}) collective-permute-start(bf16[16,1024]{1,0:T(8,128)(2,1)S(1)} %get-tuple-element.159), channel_id=1, source_target_pairs={{0,8},{8,16},{16,24},{24,32},{32,40},{40,48},{48,56},{56,64},{64,7... | collective-permute-start | bytes 98312 | tf_op jit(solution)/shard_map/while/body/eval_jaxpr/ppermute | solution.py:10
  588.5 7.9 %collective-permute-start = (bf16[16,1024]{1,0:T(8,128)(2,1)S(1)}, bf16[16,1024]{1,0:T(8,128)(2,1)S(1)}, u32[]{:S(2)}, u32[]{:S(2)}) collective-permute-start(bf16[16,1024]{1,0:T(8,128)(2,1)S(1)} %get-tuple-element.159), channel_id=1, source_target_pairs={{0,8},{8,16},{16,24},{24,32},{32,40},{40,48},{48,56},{56,64},{64,7... | collective-permute-start | bytes 98312 | tf_op jit(solution)/shard_map/while/body/eval_jaxpr/ppermute | solution.py:10
  597.1 7.9 %collective-permute-start = (bf16[16,1024]{1,0:T(8,128)(2,1)S(1)}, bf16[16,1024]{1,0:T(8,128)(2,1)S(1)}, u32[]{:S(2)}, u32[]{:S(2)}) collective-permute-start(bf16[16,1024]{1,0:T(8,128)(2,1)S(1)} %get-tuple-element.159), channel_id=1, source_target_pairs={{0,8},{8,16},{16,24},{24,32},{32,40},{40,48},{48,56},{56,64},{64,7... | collective-permute-start | bytes 98312 | tf_op jit(solution)/shard_map/while/body/eval_jaxpr/ppermute | solution.py:10
  605.6 7.9 %collective-permute-start = (bf16[16,1024]{1,0:T(8,128)(2,1)S(1)}, bf16[16,1024]{1,0:T(8,128)(2,1)S(1)}, u32[]{:S(2)}, u32[]{:S(2)}) collective-permute-start(bf16[16,1024]{1,0:T(8,128)(2,1)S(1)} %get-tuple-element.159), channel_id=1, source_target_pairs={{0,8},{8,16},{16,24},{24,32},{32,40},{40,48},{48,56},{56,64},{64,7... | collective-permute-start | bytes 98312 | tf_op jit(solution)/shard_map/while/body/eval_jaxpr/ppermute | solution.py:10
  614.1 7.9 %collective-permute-start = (bf16[16,1024]{1,0:T(8,128)(2,1)S(1)}, bf16[16,1024]{1,0:T(8,128)(2,1)S(1)}, u32[]{:S(2)}, u32[]{:S(2)}) collective-permute-start(bf16[16,1024]{1,0:T(8,128)(2,1)S(1)} %get-tuple-element.159), channel_id=1, source_target_pairs={{0,8},{8,16},{16,24},{24,32},{32,40},{40,48},{48,56},{56,64},{64,7... | collective-permute-start | bytes 98312 | tf_op jit(solution)/shard_map/while/body/eval_jaxpr/ppermute | solution.py:10
  622.7 8.0 %collective-permute-start = (bf16[16,1024]{1,0:T(8,128)(2,1)S(1)}, bf16[16,1024]{1,0:T(8,128)(2,1)S(1)}, u32[]{:S(2)}, u32[]{:S(2)}) collective-permute-start(bf16[16,1024]{1,0:T(8,128)(2,1)S(1)} %get-tuple-element.159), channel_id=1, source_target_pairs={{0,8},{8,16},{16,24},{24,32},{32,40},{40,48},{48,56},{56,64},{64,7... | collective-permute-start | bytes 98312 | tf_op jit(solution)/shard_map/while/body/eval_jaxpr/ppermute | solution.py:10
  704.9 20.7 %copy-start.34 = (s32[512]{0:T(512)S(1)}, s32[512]{0:T(512)}, u32[]{:S(2)}) copy-start(s32[512]{0:T(512)} %copy-done.33) | copy-start | bytes 6148
  707.7 36.1 %copy-start.51 = (pred[512]{0:T(512)(128)(4,1)S(1)}, pred[512]{0:T(512)(128)(4,1)}, u32[]{:S(2)}) copy-start(pred[512]{0:T(512)(128)(4,1)} %get-tuple-element.65) | copy-start | bytes 1540
  709.1 32.6 %all-to-all-start.1 = ((bf16[16,48,1024]{2,1,0:T(8,128)(2,1)}), bf16[16,48,1024]{2,1,0:T(8,128)(2,1)S(1)}, u32[]{:S(2)}, u32[]{:S(2)}) async-start(bf16[16,48,1024]{2,1,0:T(8,128)(2,1)} %broadcast_select_fusion.2), calls=%async_computation.2 | async-start | bytes 3145728 | tf_op jit(solution)/shard_map/all_to_all | solution.py:124
  (52 other events, 332.7 us)
Sparse Core Ops, SparseCore 0:
  300.4 53.9 reduce-scatter.1
where the time goes:
time: 763 us; the launch traced here: 752 us
  local copies, waits for them, and re-layouts  233 us (31%)
  blocking collectives  153 us (20%)
  starting transfers between devices  111 us (15%)
  matrix products  109 us (14%)
  other arithmetic  70.2 us (9%)
  waiting for transfers between devices  59.9 us (8%)
  between operations  14.7 us (2%)
    all_gather x1, blocking collectives, on_device(): every_route = lax.all_gather(route, 'ctx', axis=0, tiled=True)  153 us
    ppermute x16, starting transfers between devices, from_behind(): return lax.ppermute(shard, axis, pairs)  86.6 us
    dot_general x1, matrix products, on_device(): jnp.einsum('gnc,inc->gic', entering, lead_powers, precision=lax.Precision...  54.7 us
    pad x14, local copies, waits for them, and re-layouts, on_device(): lax.associative_scan(pair_combine, (span_factor, span_state), axis=0)  51.9 us
    gather x3, local copies, waits for them, and re-layouts, on_device(): jnp.take(received, flat_slot, axis=0).reshape(tok_rows, 5, channels)  30.7 us
    ppermute x16, waiting for transfers between devices, from_behind(): return lax.ppermute(shard, axis, pairs)  27.9 us
    unnamed x115, local copies, waits for them, and re-layouts  24.4 us
    conv_general_dilated x1, matrix products, tap_filter(): lax.conv_general_dilated(padded[None], kernel, window_strides=(1,), paddi...  22.5 us
  transfers between devices with their start and end apart: 19, of which 18 were waited for; matrix products, arithmetic and copies ran while one was open for 5% of the time, Pallas kernels for 0%

commit v1 on v0

v1 whole, which is shorter than its diff:
```python
import functools

import jax
import jax.numpy as jnp
import ml_dtypes
import numpy as np
from jax import lax
from jax.experimental import pallas as pl
from jax.experimental.pallas import tpu as pltpu
from jax.sharding import PartitionSpec as P

f32 = jnp.float32
bf16 = jnp.bfloat16
i32 = jnp.int32
SEGS = 8
CHUNKS = 2
ORDER = 16


def dot(a, b):
    return jnp.dot(a, b, preferred_element_type=f32)


def dot_t(a, b):
    return lax.dot_general(a, b, (((0,), (0,)), ((), ())), preferred_element_type=f32)


def iota(shape, dim):
    return lax.broadcasted_iota(i32, shape, dim)


def ones_where(mask):
    return jnp.where(mask, 1.0, 0.0).astype(bf16)


def params(mib=48):
    return pltpu.CompilerParams(vmem_limit_bytes=mib * 2**20)


def cost(flops, nbytes):
    return pl.CostEstimate(flops=int(flops), bytes_accessed=int(nbytes), transcendentals=0)


def whole(shape):
    return pl.BlockSpec(shape, lambda *_: (0,) * len(shape))


def cols(shape):
    return pl.BlockSpec(shape, lambda j, *_: (0,) * (len(shape) - 1) + (j,))


def send_matrix(route, slots, slot_count):
    rows = route.shape[1]
    peers = slots // slot_count
    hot = iota((peers, rows), 0) == route
    earlier = ones_where(iota((rows, rows), 0) < iota((rows, rows), 1))
    rank = dot(ones_where(hot), earlier)
    rank = jnp.sum(jnp.where(hot, rank, 0.0), axis=0, keepdims=True)
    slot = route * slot_count + rank.astype(i32)
    return ones_where(iota((slots, rows), 0) == slot)


def place_matrix(every_route, me, slots, slot_count):
    peers, rows = every_route.shape
    count = jnp.sum(jnp.where(every_route == me, 1.0, 0.0), axis=1, keepdims=True)
    lane = iota((peers, slots), 1)
    low = iota((peers, slots), 0) * slot_count
    mine = (lane >= low) & (lane < low + slot_count)
    before = jnp.sum(jnp.where(lane >= low + slot_count, count, 0.0), axis=0, keepdims=True)
    held = jnp.sum(jnp.where(mine, count, 0.0), axis=0, keepdims=True)
    within = jnp.sum(jnp.where(mine, (lane - low).astype(f32), 0.0), axis=0, keepdims=True)
    at = jnp.where(within < held, before + within, -1.0).astype(i32)
    return ones_where(iota((rows, slots), 0) == at)


def pack_product(planes, route, first, second, slot_count, peers, tile=512):
    _, rows, channels = planes.shape
    slots = peers * slot_count

    def body(route_ref, a_ref, *rest):
        out_ref, hot_ref = rest[-2:]

        @pl.when(pl.program_id(0) == 0)
        def _():
            hot_ref[...] = send_matrix(route_ref[...], slots, slot_count)

        x = a_ref[0]
        if second is not None:
            x = (x.astype(f32) * rest[0][0].astype(f32)).astype(bf16)
        out_ref[...] = dot(hot_ref[...], x).astype(bf16)

    picks = [first] if second is None else [first, second]
    return pl.pallas_call(
        body,
        grid=(channels // tile,),
        in_specs=[whole((1, rows))]
        + [pl.BlockSpec((1, rows, tile), functools.partial(lambda s, j: (s, 0, j), s)) for s in picks],
        out_specs=cols((slots, tile)),
        out_shape=jax.ShapeDtypeStruct((slots, channels), bf16),
        scratch_shapes=[pltpu.VMEM((slots, rows), bf16)],
        compiler_params=params(),
        cost_estimate=cost(2 * slots * rows * channels, 2 * (rows * len(picks) + slots) * channels),
        name="pack",
    )(route, *([planes] * len(picks)))


def unpack(received, every_route, me, slot_count, tile=512):
    slots, channels = received.shape
    rows = every_route.shape[1]

    def body(me_ref, every_ref, in_ref, out_ref, hot_ref):
        @pl.when(pl.program_id(0) == 0)
        def _():
            hot_ref[...] = place_matrix(every_ref[...], me_ref[0], slots, slot_count)

        out_ref[...] = dot(hot_ref[...], in_ref[...]).astype(bf16)

    return pl.pallas_call(
        body,
        grid_spec=pltpu.PrefetchScalarGridSpec(
            num_scalar_prefetch=1,
            grid=(channels // tile,),
            in_specs=[whole(every_route.shape), cols((slots, tile))],
            out_specs=cols((rows, tile)),
            scratch_shapes=[pltpu.VMEM((rows, slots), bf16)],
        ),
        out_shape=jax.ShapeDtypeStruct((rows, channels), bf16),
        compiler_params=params(),
        cost_estimate=cost(2 * slots * rows * channels, 2 * (rows + slots) * channels),
        name="unpack",
    )(me, every_route, received)


def finish(returned, planes, plane, route, slot_count):
    slots, width = returned[0].shape
    _, rows, channels = planes.shape

    def body(route_ref, gate_ref, *rest):
        out_ref = rest[-1]
        hot = send_matrix(route_ref[...], slots, slot_count)
        for h in range(len(returned)):
            at = slice(h * width, (h + 1) * width)
            out_ref[:, at] = (gate_ref[0, :, at].astype(f32) * dot_t(hot, rest[h][...])).astype(bf16)

    return pl.pallas_call(
        body,
        grid=(1,),
        in_specs=[whole((1, rows)), pl.BlockSpec((1, rows, channels), lambda j: (plane, 0, 0))]
        + [whole((slots, width))] * len(returned),
        out_specs=whole((rows, channels)),
        out_shape=jax.ShapeDtypeStruct((rows, channels), bf16),
        compiler_params=params(),
        cost_estimate=cost(2 * slots * rows * channels, 2 * (2 * rows + slots) * channels),
        name="finish",
    )(route, planes, *returned)


def two_parts(table):
    high = table.astype(ml_dtypes.bfloat16)
    return high, (table - high.astype(np.float64)).astype(ml_dtypes.bfloat16)


def dft_tables(taps):
    points = 2 * taps
    k = np.arange(taps)[:, None].astype(np.float64)
    t = np.arange(points)[None, :].astype(np.float64)
    forward = np.concatenate(
        [np.cos(2 * np.pi * k * t / points), np.cos(np.pi * t), -np.sin(2 * np.pi * k[1:] * t / points)]
    )
    inverse = forward.T[taps:] * (2.0 / points)
    inverse[:, 0] *= 0.5
    inverse[:, taps] *= 0.5
    return np.concatenate(two_parts(forward)), np.concatenate(two_parts(inverse))


def forward_dft(table, x):
    both = dot(table, x)
    half = both.shape[0] // 2
    return both[:half] + both[half:]


def inverse_dft(table, y):
    half = table.shape[0] // 2
    high = y.astype(bf16)
    low = (y - high.astype(f32)).astype(bf16)
    both = dot(table, high)
    return both[:half] + both[half:] + dot(table[:half], low)


def through_filter(spectrum, filter_ref, inverse_table):
    taps = spectrum.shape[0] // 2
    a, b = spectrum[:taps], spectrum[taps:]
    re, im, re_last = filter_ref[0], filter_ref[1], filter_ref[2]
    return inverse_dft(inverse_table, jnp.concatenate([a * re - b * im, a * im + b * re_last]))


def filter_spectrum(mr_filter, forward, tile=512):
    taps, channels = mr_filter.shape

    def body(taps_ref, fwd_ref, out_ref):
        fwd = fwd_ref[:, :taps]
        x = taps_ref[...]
        high = x.astype(bf16)
        low = (x - high.astype(f32)).astype(bf16)
        h = forward_dft(fwd, high) + dot(fwd[: 2 * taps], low)
        first = iota((taps, tile), 0) == 0
        out_ref[0] = h[:taps]
        out_ref[1] = jnp.where(first, 0.0, h[taps:])
        out_ref[2] = jnp.where(first, h[taps:], h[:taps])

    return pl.pallas_call(
        body,
        grid=(channels // tile,),
        in_specs=[cols((taps, tile)), whole(forward.shape)],
        out_specs=cols((3, taps, tile)),
        out_shape=jax.ShapeDtypeStruct((3, taps, channels), f32),
        compiler_params=params(),
        cost_estimate=cost(6 * 2 * taps * taps * channels, 16 * taps * channels),
        name="spectrum",
    )(mr_filter, forward)


def filter_rows(u, spectrum, forward, inverse, tile=512):
    rows, channels = u.shape
    taps = spectrum.shape[1]

    def body(u_ref, h_ref, fwd_ref, inv_ref, out_ref):
        for b in range(rows // taps):
            at = slice(b * taps, (b + 1) * taps)
            if b == 0:
                x = forward_dft(fwd_ref[:, taps:], u_ref[at])
            else:
                x = forward_dft(fwd_ref[...], u_ref[(b - 1) * taps : (b + 1) * taps])
            out_ref[at] = through_filter(x, h_ref, inv_ref[...])

    return pl.pallas_call(
        body,
        grid=(channels // tile,),
        in_specs=[cols((rows, tile)), cols((3, taps, tile)), whole(forward.shape), whole(inverse.shape)],
        out_specs=cols((rows, tile)),
        out_shape=jax.ShapeDtypeStruct((rows, channels), f32),
        compiler_params=params(),
        cost_estimate=cost(14 * taps * rows * channels, 8 * rows * channels),
        name="taps",
    )(u, spectrum, forward, inverse)


def gate(received, every_route, me, filtered, rim, spectrum, forward, inverse, slot_count, tile=512):
    slots, channels = received.shape
    rows = every_route.shape[1]
    taps = spectrum.shape[1]

    def body(me_ref, every_ref, in_ref, filt_ref, rim_ref, h_ref, fwd_ref, inv_ref, out_ref, hot_ref):
        @pl.when(pl.program_id(0) == 0)
        def _():
            hot_ref[...] = place_matrix(every_ref[...], me_ref[0], slots, slot_count)

        q = dot(hot_ref[...], in_ref[...])
        early = through_filter(forward_dft(fwd_ref[:, :taps], rim_ref[...]), h_ref, inv_ref[...])
        out_ref[:taps] = (q[:taps] * (filt_ref[:taps] + early)).astype(bf16)
        out_ref[taps:] = (q[taps:] * filt_ref[taps:]).astype(bf16)

    return pl.pallas_call(
        body,
        grid_spec=pltpu.PrefetchScalarGridSpec(
            num_scalar_prefetch=1,
            grid=(channels // tile,),
            in_specs=[
                whole(every_route.shape),
                cols((slots, tile)),
                cols((rows, tile)),
                cols((taps, tile)),
                cols((3, taps, tile)),
                whole(forward.shape),
                whole(inverse.shape),
            ],
            out_specs=cols((rows, tile)),
            scratch_shapes=[pltpu.VMEM((rows, slots), bf16)],
        ),
        out_shape=jax.ShapeDtypeStruct((rows, channels), bf16),
        compiler_params=params(),
        cost_estimate=cost(2 * slots * rows * channels, (6 * rows + 2 * slots) * channels),
        name="gate",
    )(me, every_route, received, filtered, rim, spectrum, forward, inverse)


def project(tasks, chunk, blocks, own, other, weight, other_weights, adds, out_type, tile=256):
    rows, depth = own.shape
    width = depth // CHUNKS
    steps = width // tile
    count = len(tasks)

    def body(blocks_ref, own_ref, other_ref, *rest):
        for n, (_, low, take) in enumerate(tasks):
            at = slice(low, low + take)
            total = dot(own_ref[at], rest[2 * n][...]) + dot(other_ref[at], rest[2 * n + 1][...])
            if adds:
                total = total + rest[2 * count + n][...].astype(f32)
            rest[2 * count + len(adds) + n][...] = total.astype(out_type)

    specs = [whole((rows, depth))] * 2
    operands = [own, other]
    for dx, _, _ in tasks:
        specs.append(
            pl.BlockSpec(
                (depth, tile),
                functools.partial(lambda d, j, b: (0, (b[d] * CHUNKS + chunk) * steps + j), dx),
            )
        )
        specs.append(pl.BlockSpec((depth, tile), lambda j, b: (0, chunk * steps + j)))
        operands += [weight, other_weights[dx]]
    for arrived in adds:
        specs.append(cols((arrived.shape[0], tile)))
        operands.append(arrived)
    total_rows = sum(take for _, _, take in tasks)
    return pl.pallas_call(
        body,
        grid_spec=pltpu.PrefetchScalarGridSpec(
            num_scalar_prefetch=1,
            grid=(steps,),
            in_specs=specs,
            out_specs=[cols((take, tile)) for _, _, take in tasks],
        ),
        out_shape=[jax.ShapeDtypeStruct((take, width), out_type) for _, _, take in tasks],
        compiler_params=params(),
        cost_estimate=cost(
            4 * depth * width * total_rows, 4 * depth * width * count + 4 * rows * depth + 4 * total_rows * width
        ),
        name="project",
    )(blocks, *operands)


def end_states(chunk, table, own, arrived, k_li, last, coef):
    rows, width = own.shape
    half = rows // 2
    steps = rows // SEGS

    def body(table_ref, own_ref, a0_ref, a1_ref, b0_ref, b1_ref, k_ref, last_ref, coef_ref, u_ref, seg_ref, end_ref):
        top = own_ref[:half] + a0_ref[...].astype(f32) + a1_ref[...].astype(f32)
        top = top * k_ref[:half].astype(f32)
        bottom = own_ref[half:] + b0_ref[...].astype(f32) + b1_ref[...].astype(f32)
        bottom = bottom * k_ref[half:].astype(f32)
        for cb in range(width // 128):
            lanes = slice(cb * 128, (cb + 1) * 128)
            u_ref[cb, :half] = top[:, lanes]
            u_ref[cb, half:] = bottom[:, lanes]
            decay = [jnp.broadcast_to(coef_ref[0, n : n + 1, lanes], (SEGS, 128)) for n in range(ORDER)]

            def step(t, state):
                u = u_ref[cb, pl.ds(t, SEGS, stride=steps), :] * last_ref[pl.ds(t, SEGS, stride=steps), :]
                return tuple(d * s + u for d, s in zip(decay, state))

            state = lax.fori_loop(0, steps, step, (jnp.zeros((SEGS, 128), f32),) * ORDER, unroll=4)
            for n in range(ORDER):
                seg_ref[cb, n * SEGS : (n + 1) * SEGS] = state[n]
            total = jnp.zeros((ORDER, 128), f32)
            for s in range(SEGS):
                keep = jnp.where(table_ref[s] == 0, coef_ref[1, :, lanes], 0.0)
                total = keep * total + seg_ref[cb, pl.ds(s, ORDER, stride=SEGS), :]
            end_ref[:, lanes] = total

    piece = whole((half, width))
    return pl.pallas_call(
        body,
        grid_spec=pltpu.PrefetchScalarGridSpec(
            num_scalar_prefetch=1,
            grid=(1,),
            in_specs=[
                whole((rows, width)),
                piece,
                piece,
                piece,
                piece,
                pl.BlockSpec((rows, width), lambda j, b: (0, chunk)),
                whole(last.shape),
                pl.BlockSpec((4, ORDER, width), lambda j, b: (0, 0, chunk)),
            ],
            out_specs=[
                whole((width // 128, rows, 128)),
                whole((width // 128, ORDER * SEGS, 128)),
                whole((ORDER, width)),
            ],
        ),
        out_shape=[
            jax.ShapeDtypeStruct((width // 128, rows, 128), f32),
            jax.ShapeDtypeStruct((width // 128, ORDER * SEGS, 128), f32),
            jax.ShapeDtypeStruct((ORDER, width), f32),
        ],
        compiler_params=params(),
        cost_estimate=cost(2e9, 8 * rows * width),
        name="ends",
    )(table, own, *arrived, k_li, last, coef)


def recur(chunk, table, ends, segs, u, keep, coef, every_route, slot_count):
    blocks, rows, _ = u.shape
    width = 128 * blocks
    steps = rows // SEGS
    peers = every_route.shape[0]
    slots = peers * slot_count

    def body(table_ref, ends_ref, seg_ref, u_ref, keep_ref, coef_ref, every_ref, out_ref, in_ref, li_ref):
        me = table_ref[SEGS + peers]

        def hop(j, carry):
            return jnp.where(table_ref[SEGS + j] == 0, coef_ref[2], 0.0) * carry + ends_ref[j]

        carry = lax.fori_loop(0, me, hop, jnp.zeros((ORDER, width), f32))
        for cb in range(blocks):
            lanes = slice(cb * 128, (cb + 1) * 128)
            enter = carry[:, lanes]
            for s in range(SEGS):
                in_ref[cb, pl.ds(s, ORDER, stride=SEGS), :] = enter
                fade = jnp.where(table_ref[s] == 0, coef_ref[1, :, lanes], 0.0)
                enter = fade * enter + seg_ref[cb, pl.ds(s, ORDER, stride=SEGS), :]
            decay = [jnp.broadcast_to(coef_ref[0, n : n + 1, lanes], (SEGS, 128)) for n in range(ORDER)]
            weigh = [jnp.broadcast_to(coef_ref[3, n : n + 1, lanes], (SEGS, 128)) for n in range(ORDER)]
            state = tuple(in_ref[cb, n * SEGS : (n + 1) * SEGS] for n in range(ORDER))

            def step(t, state):
                u = u_ref[cb, pl.ds(t, SEGS, stride=steps), :]
                kept = keep_ref[pl.ds(t, SEGS, stride=steps), :]
                state = tuple((d * s) * kept + u for d, s in zip(decay, state))
                terms = [w * s for w, s in zip(weigh, state)]
                while len(terms) > 1:
                    terms = [a + b for a, b in zip(terms[::2], terms[1::2])]
                li_ref[cb, pl.ds(t, SEGS, stride=steps), :] = terms[0]
                return state

            lax.fori_loop(0, steps, step, state, unroll=4)
        hot = place_matrix(every_ref[...], me, slots, slot_count)
        li = jnp.concatenate([li_ref[cb].astype(bf16) for cb in range(blocks)], axis=1)
        out_ref[...] = dot_t(hot, li).astype(bf16)

    return pl.pallas_call(
        body,
        grid_spec=pltpu.PrefetchScalarGridSpec(
            num_scalar_prefetch=1,
            grid=(1,),
            in_specs=[
                whole(ends.shape),
                whole(segs.shape),
                whole(u.shape),
                whole(keep.shape),
                pl.BlockSpec((4, ORDER, width), lambda j, b: (0, 0, chunk)),
                whole(every_route.shape),
            ],
            out_specs=whole((slots, width)),
            scratch_shapes=[pltpu.VMEM(segs.shape, f32), pltpu.VMEM(u.shape, f32)],
        ),
        out_shape=jax.ShapeDtypeStruct((slots, width), bf16),
        compiler_params=params(),
        cost_estimate=cost(4e9, 8 * rows * width),
        name="recur",
    )(table, ends, segs, u, keep, coef, every_route)


def along_x(shard, dx, dcore=0):
    count = lax.axis_size("tp") // 2
    pairs = [
        (2 * x + c, 2 * ((x + dx) % count) + (c + dcore) % 2) for x in range(count) for c in range(2)
    ]
    return lax.ppermute(shard, "tp", pairs)


def swap(shard):
    return lax.all_to_all(shard, "ctx", split_axis=0, concat_axis=0, tiled=True)


def together(*arrays):
    return lax.optimization_barrier(arrays)


def on_device(projected, route, contig_len, mr_filter, out_weight, li_rate, li_residue):
    rows, _, channels = projected.shape
    peers = lax.axis_size("ctx")
    slot_count = 3 * rows // (2 * peers)
    taps = mr_filter.shape[0]
    half = rows // 2
    me = lax.axis_index("ctx").astype(i32)
    tp = lax.axis_index("tp").astype(i32)
    chip, core = tp // 2, tp % 2
    chips = lax.axis_size("tp") // 2
    planes = jnp.transpose(projected, (1, 0, 2))
    route_row = route.reshape(1, rows)
    me_row = me.reshape(1)
    forward, inverse = (jnp.asarray(t) for t in dft_tables(taps))

    every_route = lax.all_gather(route, "ctx", axis=0, tiled=False)
    packed_kv = pack_product(planes, route_row, 1, 2, slot_count, peers)
    packed_kv, every_route = together(packed_kv, every_route)
    got_kv = swap(packed_kv)
    packed_q = pack_product(planes, route_row, 0, None, slot_count, peers)
    packed_k = pack_product(planes, route_row, 4, None, slot_count, peers)

    order = jnp.arange(contig_len.shape[0], dtype=i32)
    starts = jnp.sum(jnp.where(order[:, None] < order[None, :], contig_len[:, None], 0), axis=0)
    span = rows // SEGS
    here = me * rows + jnp.arange(rows, dtype=i32)
    seg_last = here - here % span + (span - 1)
    keep = jnp.where(jnp.any(here[:, None] == starts[None, :], axis=1), 0.0, 1.0).astype(f32)
    last = jnp.where(
        jnp.any((starts[None, :] > here[:, None]) & (starts[None, :] <= seg_last[:, None]), axis=1), 0.0, 1.0
    ).astype(f32)
    keep = jnp.broadcast_to(keep[:, None], (rows, 128))
    last = jnp.broadcast_to(last[:, None], (rows, 128))
    seg_ids = me * SEGS + jnp.arange(SEGS, dtype=i32)
    seg_has = jnp.any(seg_ids[:, None] == (starts // span)[None, :], axis=1)
    dev_has = jnp.any(jnp.arange(peers, dtype=i32)[:, None] == (starts // rows)[None, :], axis=1)
    table = jnp.concatenate([seg_has.astype(i32), dev_has.astype(i32), me_row])
    mode_weight = li_residue * jnp.sqrt(-jnp.expm1(-2.0 * li_rate))
    coef = jnp.stack([jnp.exp(-li_rate), jnp.exp(-li_rate * span), jnp.exp(-li_rate * rows), mode_weight])
    spectrum = filter_spectrum(mr_filter, forward)

    blocks = jnp.stack([2 * ((chip + d) % chips) + core for d in range(chips)]).astype(i32)
    depth = out_weight.shape[0]
    other_weights = [
        along_x(lax.dynamic_slice(out_weight, (0, (2 * ((chip + d) % chips) + 1 - core) * depth), (depth, depth)), 0, 1)
        for d in range(chips)
    ]

    got_kv, packed_q = together(got_kv, packed_q)
    got_q = swap(packed_q)
    u_mr = unpack(got_kv, every_route, me_row, slot_count)
    rim = lax.ppermute(u_mr[rows - taps :], "ctx", [(i, i + 1) for i in range(peers - 1)])
    filtered = filter_rows(u_mr, spectrum, forward, inverse)
    got_q, packed_k = together(got_q, packed_k)
    gated = gate(got_q, every_route, me_row, filtered, rim, spectrum, forward, inverse, slot_count)
    got_k = swap(packed_k)
    other = along_x(gated, 0, 1)
    mm = functools.partial(project, blocks=blocks, own=gated, other=other, weight=out_weight, other_weights=other_weights)

    k_li = None
    returned = []
    for h in range(CHUNKS):
        far_a, far_b = mm([(2, 0, half), (2, half, half)], h, adds=[], out_type=bf16)
        pass_a, pass_b = along_x(far_a, 1), along_x(far_b, -1)
        up_b, down_a = mm([(1, half, half), (3, 0, half)], h, adds=[], out_type=bf16)
        from_low_b, from_high_a = along_x(up_b, 1), along_x(down_a, -1)
        [mine] = mm([(0, 0, rows)], h, adds=[], out_type=f32)
        up_a, down_b = mm([(1, 0, half), (3, half, half)], h, adds=[pass_a, pass_b], out_type=bf16)
        from_low_a, from_high_b = along_x(up_a, 1), along_x(down_b, -1)
        if k_li is None:
            k_li = unpack(got_k, every_route, me_row, slot_count)
        u, segs, end = end_states(
            h, table, mine, [from_low_a, from_high_a, from_low_b, from_high_b], k_li, last, coef
        )
        ends = lax.all_gather(end, "ctx", axis=0, tiled=False)
        homeward = recur(h, table, ends, segs, u, keep, coef, every_route, slot_count)
        returned.append(swap(homeward))
    return finish(returned, planes, 3, route_row, slot_count)


def solution(mesh):
    return jax.shard_map(
        on_device,
        mesh=mesh,
        in_specs=(
            P("ctx", None, "tp"),
            P("ctx"),
            P(),
            P(None, "tp"),
            P("tp", None),
            P(None, "tp"),
            P(None, "tp"),
        ),
        out_specs=P("ctx", "tp"),
        check_vma=False,
    )
```

time: 763 us -> 243 us (0.32); the launches traced: 752 us -> 242 us
  local copies, waits for them, and re-layouts: 233 us -> 14.3 us
  matrix products: 109 us -> 0 us
  Pallas kernels: 0 us -> 78.6 us
  other arithmetic: 70.2 us -> 0.74 us
  starting transfers between devices: 111 us -> 43.4 us
  blocking collectives: 153 us -> 89.7 us
  waiting for transfers between devices: 59.9 us -> 14.4 us
  between operations: 14.7 us -> 0.7 us
    dot_general x3 -> x0, matrix products: 86.7 us -> none  [the longest x1 54.7 us: on_device(): jnp.einsum('gnc,inc->gic', entering, lead_powers, precision=lax.Precision...]
    all_gather x1 -> x3, blocking collectives: 153 us -> 73.6 us  [the longest x2 48.8 us: on_device(): ends = lax.all_gather(end, 'ctx', axis=0, tiled=False)]
    pallas_call x0 -> x21, Pallas kernels: none -> 78.6 us  [the longest x8 31.5 us: project(): pl.pallas_call(body, grid_spec=pltpu.PrefetchScalarGridSpec(num_scalar_pr...]
    ppermute x16 -> x18, starting transfers between devices: 86.6 us -> 22.4 us  [the longest x17 18.7 us: along_x(): return lax.ppermute(shard, 'tp', pairs)]
    gather x6 -> x0, local copies, waits for them, and re-layouts: 53.4 us -> none  [the longest x3 30.7 us: on_device(): jnp.take(received, flat_slot, axis=0).reshape(tok_rows, 5, channels)]
    pad x14 -> x0, local copies, waits for them, and re-layouts: 51.9 us -> none  [on_device(): lax.associative_scan(pair_combine, (span_factor, span_state), axis=0)]
    slice x22 -> x1, local copies, waits for them, and re-layouts: 42.2 us -> 0.02 us  [on_device(): u_mr[rows - taps:]]
    add x33 -> x2, other arithmetic: 36 us -> 0.02 us  [the longest x1 0.01 us: on_device(): seg_last = here - here % span + (span - 1)]
  transfers between devices with their start and end apart: 19 -> 22, of which waited for: 18 -> 1; matrix products, arithmetic and copies ran while one was open for 5% -> 3% of each run, Pallas kernels for 0% -> 29%
where the time goes in v1:
time: 243 us; the launch traced here: 242 us
  blocking collectives  89.7 us (37%)
  Pallas kernels  78.6 us (32%)
  starting transfers between devices  43.4 us (18%)
  waiting for transfers between devices  14.4 us (6%)
  local copies, waits for them, and re-layouts  14.3 us (6%)
    all_gather x2, blocking collectives, on_device(): ends = lax.all_gather(end, 'ctx', axis=0, tiled=False)  48.8 us
    pallas_call x8, Pallas kernels, project(): pl.pallas_call(body, grid_spec=pltpu.PrefetchScalarGridSpec(num_scalar_pr...  31.5 us
    all_gather x1, blocking collectives, on_device(): every_route = lax.all_gather(route, 'ctx', axis=0, tiled=False)  24.9 us
    all_to_all x4, starting transfers between devices, swap(): return lax.all_to_all(shard, 'ctx', split_axis=0, concat_axis=0, tiled=True)  21.1 us
    ppermute x17, starting transfers between devices, along_x(): return lax.ppermute(shard, 'tp', pairs)  18.7 us
    all_to_all x1, blocking collectives, swap(): return lax.all_to_all(shard, 'ctx', split_axis=0, concat_axis=0, tiled=True)  16.1 us
    all_to_all x4, waiting for transfers between devices, swap(): return lax.all_to_all(shard, 'ctx', split_axis=0, concat_axis=0, tiled=True)  14.3 us
    pallas_call x2, Pallas kernels, recur(): pl.pallas_call(body, grid_spec=pltpu.PrefetchScalarGridSpec(num_scalar_pr...  11.2 us
  transfers between devices with their start and end apart: 22, of which 1 were waited for; matrix products, arithmetic and copies ran while one was open for 3% of the time, Pallas kernels for 29%

profile of v1, /device:TPU:0, one launch (start us, length us, event | category | flops | bytes accessed | tf_op | source)
XLA Modules:
  0.0 241.9 jit_solution(10420783233106280862)
XLA Ops:
  0.0 24.9 %all-gather.3 = s32[16,1,512]{2,1,0:T(1,128)S(1)} all-gather(s32[1,1,512]{2,1,0:T(1,128)} %bitcast.44), channel_id=2, replica_groups=mesh['ctx'=16,'tp'=8] {'ctx'}, dimensions={0}, use_global_device_ids=true | all-gather | bytes 34816 | tf_op jit(solution)/shard_map/all_gather | solution.py:489
  25.6 3.9 %pack.3 = bf16[768,1024]{1,0:T(8,128)(2,1)} custom-call(s32[1,512]{1,0:T(1,128)S(1)} %bitcast.45, bf16[5,512,1024]{2,1,0:T(8,128)(2,1)} %bitcast.49, bf16[5,512,1024]{2,1,0:T(8,128)(2,1)} %bitcast.50), custom_call_target="tpu_custom_call" | custom-call | flops 805306368 | bytes 3670016 | tf_op jit(solution)/shard_map/pack/pallas_call | solution.py:93
  29.5 5.1 %all-to-all-start = ((bf16[16,48,1024]{2,1,0:T(8,128)(2,1)}), bf16[16,48,1024]{2,1,0:T(8,128)(2,1)S(1)}, u32[]{:S(2)}, u32[]{:S(2)}) async-start(bf16[16,48,1024]{2,1,0:T(8,128)(2,1)} %bitcast.8), calls=%async_computation | async-start | bytes 3145728 | tf_op jit(solution)/shard_map/all_to_all | solution.py:467
  38.3 14.3 %all-to-all-done = bf16[16,48,1024]{2,1,0:T(8,128)(2,1)S(1)} async-done(((bf16[16,48,1024]{2,1,0:T(8,128)(2,1)}), bf16[16,48,1024]{2,1,0:T(8,128)(2,1)S(1)}, u32[]{:S(2)}, u32[]{:S(2)}) %all-to-all-start) | async-done | bytes 1572896 | tf_op jit(solution)/shard_map/all_to_all | solution.py:467
  52.6 4.4 %all-to-all-start.1 = ((bf16[16,48,1024]{2,1,0:T(8,128)(2,1)}), bf16[16,48,1024]{2,1,0:T(8,128)(2,1)}, u32[]{:S(2)}, u32[]{:S(2)}) async-start(bf16[16,48,1024]{2,1,0:T(8,128)(2,1)} %bitcast.10), calls=%async_computation.1 | async-start | bytes 3145728 | tf_op jit(solution)/shard_map/all_to_all | solution.py:467
  57.1 7.1 %constant_dynamic-slice_fusion = (bf16[1024,1024]{1,0:T(8,128)(2,1)}, bf16[1024,1024]{1,0:T(8,128)(2,1)}, bf16[1024,1024]{1,0:T(8,128)(2,1)}, bf16[1024,1024]{1,0:T(8,128)(2,1)}) fusion(bf16[1024,8192]{1,0:T(8,128)(2,1)} %rest_2_.11, s32[]{:T(128)S(6)} %select_n.104, s32[]{:T(128)S(6)} %select_n.103, s32[]{:T(128)S(6)} %select_n.102, s32[]{:T(128)S(6)} %select_n.101), kind=kLoop, calls=%fused_computation.24 | loop fusion | bytes 16777232 | tf_op jit(solution)/shard_map/dynamic_slice | solution.py:518
  69.6 3.7 %collective-permute-start = (bf16[128,1024]{1,0:T(8,128)(2,1)S(1)}, bf16[128,1024]{1,0:T(8,128)(2,1)S(1)}, u32[]{:S(2)}, u32[]{:S(2)}) collective-permute-start(bf16[128,1024]{1,0:T(8,128)(2,1)S(1)} %slice.4), channel_id=1, source_target_pairs={{0,8},{8,16},{16,24},{24,32},{32,40},{40,48},{48,56},{56,64},{64,7... | collective-permute-start | bytes 786440 | tf_op jit(solution)/shard_map/ppermute | solution.py:525
  77.4 4.1 %taps.1.filt_ref = f32[512,1024]{1,0:T(8,128)S(1)} custom-call(bf16[512,1024]{1,0:T(8,128)(2,1)S(1)} %unpack.2.u_ref, f32[3,128,1024]{2,1,0:T(8,128)S(1)} %spectrum.1.h_ref, bf16[512,256]{1,0:T(8,128)(2,1)S(1)} %copy-done.2, bf16[256,256]{1,0:T(8,128)(2,1)S(1)} %copy-done.6), custom_call_target="tpu_custom_call" | custom-call | flops 939524096 | bytes 4194304 | tf_op jit(solution)/shard_map/taps/pallas_call | solution.py:236
  84.4 4.0 %gate.1.own_ref = bf16[512,1024]{1,0:T(8,128)(2,1)S(1)} custom-call(s32[1]{0:T(128)} %bitcast.2.me_ref, s32[16,512]{1,0:T(8,128)S(1)} %bitcast.40, bf16[768,1024]{1,0:T(8,128)(2,1)} %bitcast.11.in_ref, f32[512,1024]{1,0:T(8,128)} %copy-done, bf16[128,1024]{1,0:T(8,128)(2,1)S(1)} %copy-done.9, f32[3,128,1024]{2,1,0:T(8,128)S(1)} %spectrum.1.h_ref, ...), custom_call_target="tpu_custom_call" | custom-call | flops 805306368 | bytes 4718592 | tf_op jit(solution)/shard_map/gate/pallas_call | solution.py:263
  88.8 6.6 %all-to-all-start.2 = ((bf16[16,48,1024]{2,1,0:T(8,128)(2,1)}), bf16[16,48,1024]{2,1,0:T(8,128)(2,1)}, u32[]{:S(2)}, u32[]{:S(2)}) async-start(bf16[16,48,1024]{2,1,0:T(8,128)(2,1)} %bitcast.31), calls=%async_computation.2 | async-start | bytes 3145728 | tf_op jit(solution)/shard_map/all_to_all | solution.py:467
  95.5 3.7 %project.9 = (bf16[256,512]{1,0:T(8,128)(2,1)S(1)}, bf16[256,512]{1,0:T(8,128)(2,1)S(1)}) custom-call(s32[4]{0:T(128)S(1)} %pad_add_fusion.1.blocks_ref, bf16[512,1024]{1,0:T(8,128)(2,1)S(1)} %gate.1.own_ref, bf16[512,1024]{1,0:T(8,128)(2,1)S(1)} %collective-permute-done.1.other_ref, bf16[1024,8192]{1,0:T(8,128)(2,1)} %rest_2_.11, ...), custom_call_target="tpu_custom_call" | custom-call | flops 1073741824 | bytes 7340032 | tf_op jit(solution)/shard_map/project/pallas_call | solution.py:316
  102.5 3.7 %project.13 = (bf16[256,512]{1,0:T(8,128)(2,1)S(1)}, bf16[256,512]{1,0:T(8,128)(2,1)S(1)}) custom-call(s32[4]{0:T(128)S(1)} %pad_add_fusion.1.blocks_ref, bf16[512,1024]{1,0:T(8,128)(2,1)S(1)} %gate.1.own_ref, bf16[512,1024]{1,0:T(8,128)(2,1)S(1)} %collective-permute-done.1.other_ref, bf16[1024,8192]{1,0:T(8,128)(2,1)} %rest_2_.11, ...), custom_call_target="tpu_custom_call" | custom-call | flops 1073741824 | bytes 7340032 | tf_op jit(solution)/shard_map/project/pallas_call | solution.py:316
  109.8 4.3 %project.15 = (bf16[256,512]{1,0:T(8,128)(2,1)}, bf16[256,512]{1,0:T(8,128)(2,1)}) custom-call(s32[4]{0:T(128)S(1)} %pad_add_fusion.1.blocks_ref, bf16[512,1024]{1,0:T(8,128)(2,1)S(1)} %gate.1.own_ref, bf16[512,1024]{1,0:T(8,128)(2,1)S(1)} %collective-permute-done.1.other_ref, bf16[1024,8192]{1,0:T(8,128)(2,1)} %rest_2_.11, ...), custom_call_target="tpu_custom_call" | custom-call | flops 1073741824 | bytes 7340032 | tf_op jit(solution)/shard_map/project/pallas_call | solution.py:316
  114.1 4.3 %project.11 = (bf16[256,512]{1,0:T(8,128)(2,1)}, bf16[256,512]{1,0:T(8,128)(2,1)}) custom-call(s32[4]{0:T(128)S(1)} %pad_add_fusion.1.blocks_ref, bf16[512,1024]{1,0:T(8,128)(2,1)S(1)} %gate.1.own_ref, bf16[512,1024]{1,0:T(8,128)(2,1)S(1)} %collective-permute-done.1.other_ref, bf16[1024,8192]{1,0:T(8,128)(2,1)} %rest_2_.11, ...), custom_call_target="tpu_custom_call" | custom-call | flops 1073741824 | bytes 7340032 | tf_op jit(solution)/shard_map/project/pallas_call | solution.py:316
  120.6 4.4 %project.10 = (bf16[256,512]{1,0:T(8,128)(2,1)}, bf16[256,512]{1,0:T(8,128)(2,1)}) custom-call(s32[4]{0:T(128)S(1)} %pad_add_fusion.1.blocks_ref, bf16[512,1024]{1,0:T(8,128)(2,1)S(1)} %gate.1.own_ref, bf16[512,1024]{1,0:T(8,128)(2,1)S(1)} %collective-permute-done.1.other_ref, bf16[1024,8192]{1,0:T(8,128)(2,1)} %rest_2_.11, ...), custom_call_target="tpu_custom_call" | custom-call | flops 1073741824 | bytes 7340032 | tf_op jit(solution)/shard_map/project/pallas_call | solution.py:316
  132.1 4.4 %project.14 = (bf16[256,512]{1,0:T(8,128)(2,1)}, bf16[256,512]{1,0:T(8,128)(2,1)}) custom-call(s32[4]{0:T(128)S(1)} %pad_add_fusion.1.blocks_ref, bf16[512,1024]{1,0:T(8,128)(2,1)S(1)} %gate.1.own_ref, bf16[512,1024]{1,0:T(8,128)(2,1)S(1)} %collective-permute-done.1.other_ref, bf16[1024,8192]{1,0:T(8,128)(2,1)} %rest_2_.11, ...), custom_call_target="tpu_custom_call" | custom-call | flops 1073741824 | bytes 7340032 | tf_op jit(solution)/shard_map/project/pallas_call | solution.py:316
  144.3 4.2 %ends.2 = (f32[4,512,128]{2,1,0:T(8,128)S(1)}, f32[4,128,128]{2,1,0:T(8,128)S(1)}, f32[16,512]{1,0:T(8,128)S(1)}) custom-call(s32[25]{0:T(128)S(1)} %pad_add_fusion.table_ref, f32[512,512]{1,0:T(8,128)S(1)} %project.8.own_ref, bf16[256,512]{1,0:T(8,128)(2,1)} %collective-permute-done.8.a0_ref, bf16[256,512]{1,0:T(8,128)(2,1)} %collective-permute-done.9.a1_ref, ...), custom_call_target="tpu_custom_call" | custom-call | flops 2000000000 | bytes 2097152 | tf_op jit(solution)/shard_map/ends/pallas_call | solution.py:363
  148.6 24.4 %all-gather.1 = f32[256,512]{1,0:T(8,128)S(1)} all-gather(f32[16,512]{1,0:T(8,128)S(1)} %get-tuple-element.41), channel_id=3, replica_groups=mesh['ctx'=16,'tp'=8] {'ctx'}, dimensions={0}, use_global_device_ids=true | all-gather | bytes 557056 | tf_op jit(solution)/shard_map/all_gather | solution.py:548
  173.1 5.6 %recur.2 = bf16[768,512]{1,0:T(8,128)(2,1)S(1)} custom-call(s32[25]{0:T(128)S(1)} %pad_add_fusion.table_ref, f32[16,16,512]{2,1,0:T(8,128)S(1)} %bitcast.38, f32[4,128,128]{2,1,0:T(8,128)S(1)} %get-tuple-element.42.seg_ref, f32[4,512,128]{2,1,0:T(8,128)S(1)} %get-tuple-element.43.u_ref, f32[512,128]{1,0:T(8,128)S(1)} %broadcast_in_dim.31.keep_ref, ...), custom_call_target="tpu_custom_call" | custom-call | flops 4000000000 | bytes 2097152 | tf_op jit(solution)/shard_map/recur/pallas_call | solution.py:435
  179.6 5.0 %all-to-all-start.3 = ((bf16[16,48,512]{2,1,0:T(8,128)(2,1)}), bf16[16,48,512]{2,1,0:T(8,128)(2,1)S(1)}, u32[]{:S(2)}, u32[]{:S(2)}) async-start(bf16[16,48,512]{2,1,0:T(8,128)(2,1)} %bitcast.35), calls=%async_computation.3 | async-start | bytes 1572864 | tf_op jit(solution)/shard_map/all_to_all | solution.py:467
  188.1 4.2 %ends.3 = (f32[4,512,128]{2,1,0:T(8,128)S(1)}, f32[4,128,128]{2,1,0:T(8,128)S(1)}, f32[16,512]{1,0:T(8,128)S(1)}) custom-call(s32[25]{0:T(128)S(1)} %pad_add_fusion.table_ref, f32[512,512]{1,0:T(8,128)S(1)} %project.12.own_ref, bf16[256,512]{1,0:T(8,128)(2,1)} %collective-permute-done.14.a0_ref, bf16[256,512]{1,0:T(8,128)(2,1)} %collective-permute-done.15.a1_ref, ...), custom_call_target="tpu_custom_call" | custom-call | flops 2000000000 | bytes 2097152 | tf_op jit(solution)/shard_map/ends/pallas_call | solution.py:363
  192.3 24.4 %all-gather.2 = f32[256,512]{1,0:T(8,128)S(1)} all-gather(f32[16,512]{1,0:T(8,128)S(1)} %get-tuple-element.50), channel_id=4, replica_groups=mesh['ctx'=16,'tp'=8] {'ctx'}, dimensions={0}, use_global_device_ids=true | all-gather | bytes 557056 | tf_op jit(solution)/shard_map/all_gather | solution.py:548
  216.7 5.6 %recur.3 = bf16[768,512]{1,0:T(8,128)(2,1)S(1)} custom-call(s32[25]{0:T(128)S(1)} %pad_add_fusion.table_ref, f32[16,16,512]{2,1,0:T(8,128)S(1)} %bitcast.37, f32[4,128,128]{2,1,0:T(8,128)S(1)} %get-tuple-element.51.seg_ref, f32[4,512,128]{2,1,0:T(8,128)S(1)} %get-tuple-element.52.u_ref, f32[512,128]{1,0:T(8,128)S(1)} %copy-done.13, ...), custom_call_target="tpu_custom_call" | custom-call | flops 4000000000 | bytes 2097152 | tf_op jit(solution)/shard_map/recur/pallas_call | solution.py:435
  222.3 16.1 %all_to_all.57 = bf16[16,48,512]{2,1,0:T(8,128)(2,1)S(1)} all-to-all(bf16[16,48,512]{2,1,0:T(8,128)(2,1)S(1)} %bitcast.36), channel_id=1, replica_groups=mesh['ctx'=16,'tp'=8] {'ctx'}, dimensions={0} | all-to-all | bytes 1572864 | tf_op jit(solution)/shard_map/all_to_all | solution.py:467
  (113 shorter events, 48.7 us)
Async XLA Ops:
  24.9 42.8 %copy-start.14 = (s32[16,1,512]{2,0,1:T(8,128)}, s32[16,1,512]{2,0,1:T(8,128)S(1)}, u32[]{:S(2)}) copy-start(s32[16,1,512]{2,0,1:T(8,128)S(1)} %copy.12) | copy-start | bytes 98308
  29.5 23.1 %all-to-all-start = ((bf16[16,48,1024]{2,1,0:T(8,128)(2,1)}), bf16[16,48,1024]{2,1,0:T(8,128)(2,1)S(1)}, u32[]{:S(2)}, u32[]{:S(2)}) async-start(bf16[16,48,1024]{2,1,0:T(8,128)(2,1)} %bitcast.8), calls=%async_computation | async-start | bytes 3145728 | tf_op jit(solution)/shard_map/all_to_all | solution.py:467
  52.6 30.2 %all-to-all-start.1 = ((bf16[16,48,1024]{2,1,0:T(8,128)(2,1)}), bf16[16,48,1024]{2,1,0:T(8,128)(2,1)}, u32[]{:S(2)}, u32[]{:S(2)}) async-start(bf16[16,48,1024]{2,1,0:T(8,128)(2,1)} %bitcast.10), calls=%async_computation.1 | async-start | bytes 3145728 | tf_op jit(solution)/shard_map/all_to_all | solution.py:467
  64.2 31.3 %collective-permute-start.5 = (bf16[1024,1024]{1,0:T(8,128)(2,1)}, bf16[1024,1024]{1,0:T(8,128)(2,1)}, u32[]{:S(2)}, u32[]{:S(2)}) collective-permute-start(bf16[1024,1024]{1,0:T(8,128)(2,1)} %get-tuple-element.55), channel_id=1, source_target_pairs={{0,1},{1,0},{2,3},{3,2},{4,5},{5,4},{6,7},{7,6},{8,9},{9,8},{10,11... | collective-permute-start | bytes 6291464 | tf_op jit(solution)/shard_map/ppermute | solution.py:463
  64.2 42.1 %collective-permute-start.4 = (bf16[1024,1024]{1,0:T(8,128)(2,1)}, bf16[1024,1024]{1,0:T(8,128)(2,1)}, u32[]{:S(2)}, u32[]{:S(2)}) collective-permute-start(bf16[1024,1024]{1,0:T(8,128)(2,1)} %get-tuple-element.56), channel_id=1, source_target_pairs={{0,1},{1,0},{2,3},{3,2},{4,5},{5,4},{6,7},{7,6},{8,9},{9,8},{10,11... | collective-permute-start | bytes 6291464 | tf_op jit(solution)/shard_map/ppermute | solution.py:463
  64.7 42.1 %collective-permute-start.3 = (bf16[1024,1024]{1,0:T(8,128)(2,1)}, bf16[1024,1024]{1,0:T(8,128)(2,1)}, u32[]{:S(2)}, u32[]{:S(2)}) collective-permute-start(bf16[1024,1024]{1,0:T(8,128)(2,1)} %get-tuple-element.57), channel_id=1, source_target_pairs={{0,1},{1,0},{2,3},{3,2},{4,5},{5,4},{6,7},{7,6},{8,9},{9,8},{10,11... | collective-permute-start | bytes 6291464 | tf_op jit(solution)/shard_map/ppermute | solution.py:463
  64.8 60.1 %collective-permute-start.2 = (bf16[1024,1024]{1,0:T(8,128)(2,1)}, bf16[1024,1024]{1,0:T(8,128)(2,1)}, u32[]{:S(2)}, u32[]{:S(2)}) collective-permute-start(bf16[1024,1024]{1,0:T(8,128)(2,1)} %get-tuple-element.58), channel_id=1, source_target_pairs={{0,1},{1,0},{2,3},{3,2},{4,5},{5,4},{6,7},{7,6},{8,9},{9,8},{10,11... | collective-permute-start | bytes 6291464 | tf_op jit(solution)/shard_map/ppermute | solution.py:463
  69.6 13.2 %collective-permute-start = (bf16[128,1024]{1,0:T(8,128)(2,1)S(1)}, bf16[128,1024]{1,0:T(8,128)(2,1)S(1)}, u32[]{:S(2)}, u32[]{:S(2)}) collective-permute-start(bf16[128,1024]{1,0:T(8,128)(2,1)S(1)} %slice.4), channel_id=1, source_target_pairs={{0,8},{8,16},{16,24},{24,32},{32,40},{40,48},{48,56},{56,64},{64,7... | collective-permute-start | bytes 786440 | tf_op jit(solution)/shard_map/ppermute | solution.py:525
  88.5 7.0 %collective-permute-start.1 = (bf16[512,1024]{1,0:T(8,128)(2,1)S(1)}, bf16[512,1024]{1,0:T(8,128)(2,1)S(1)}, u32[]{:S(2)}, u32[]{:S(2)}) collective-permute-start(bf16[512,1024]{1,0:T(8,128)(2,1)S(1)} %gate.1.own_ref), channel_id=1, source_target_pairs={{0,1},{1,0},{2,3},{3,2},{4,5},{5,4},{6,7},{7,6},{8,9},{9,8},{10,11... | collective-permute-start | bytes 3145736 | tf_op jit(solution)/shard_map/ppermute | solution.py:463
  88.8 47.7 %all-to-all-start.2 = ((bf16[16,48,1024]{2,1,0:T(8,128)(2,1)}), bf16[16,48,1024]{2,1,0:T(8,128)(2,1)}, u32[]{:S(2)}, u32[]{:S(2)}) async-start(bf16[16,48,1024]{2,1,0:T(8,128)(2,1)} %bitcast.31), calls=%async_computation.2 | async-start | bytes 3145728 | tf_op jit(solution)/shard_map/all_to_all | solution.py:467
  99.2 19.2 %collective-permute-start.6 = (bf16[256,512]{1,0:T(8,128)(2,1)S(1)}, bf16[256,512]{1,0:T(8,128)(2,1)S(1)}, u32[]{:S(2)}, u32[]{:S(2)}) collective-permute-start(bf16[256,512]{1,0:T(8,128)(2,1)S(1)} %get-tuple-element.34), channel_id=1, source_target_pairs={{0,2},{1,3},{2,4},{3,5},{4,6},{5,7},{6,0},{7,1},{8,10},{9,11},{10,... | collective-permute-start | bytes 786440 | tf_op jit(solution)/shard_map/ppermute | solution.py:463
  100.8 18.2 %collective-permute-start.7 = (bf16[256,512]{1,0:T(8,128)(2,1)S(1)}, bf16[256,512]{1,0:T(8,128)(2,1)S(1)}, u32[]{:S(2)}, u32[]{:S(2)}) collective-permute-start(bf16[256,512]{1,0:T(8,128)(2,1)S(1)} %get-tuple-element.35), channel_id=1, source_target_pairs={{0,6},{1,7},{2,0},{3,1},{4,2},{5,3},{6,4},{7,5},{8,14},{9,15},{10,... | collective-permute-start | bytes 786440 | tf_op jit(solution)/shard_map/ppermute | solution.py:463
  106.3 18.7 %collective-permute-start.12 = (bf16[256,512]{1,0:T(8,128)(2,1)S(1)}, bf16[256,512]{1,0:T(8,128)(2,1)S(1)}, u32[]{:S(2)}, u32[]{:S(2)}) collective-permute-start(bf16[256,512]{1,0:T(8,128)(2,1)S(1)} %get-tuple-element.44), channel_id=1, source_target_pairs={{0,2},{1,3},{2,4},{3,5},{4,6},{5,7},{6,0},{7,1},{8,10},{9,11},{10,... | collective-permute-start | bytes 786440 | tf_op jit(solution)/shard_map/ppermute | solution.py:463
  106.8 24.7 %collective-permute-start.13 = (bf16[256,512]{1,0:T(8,128)(2,1)S(1)}, bf16[256,512]{1,0:T(8,128)(2,1)S(1)}, u32[]{:S(2)}, u32[]{:S(2)}) collective-permute-start(bf16[256,512]{1,0:T(8,128)(2,1)S(1)} %get-tuple-element.45), channel_id=1, source_target_pairs={{0,6},{1,7},{2,0},{3,1},{4,2},{5,3},{6,4},{7,5},{8,14},{9,15},{10,... | collective-permute-start | bytes 786440 | tf_op jit(solution)/shard_map/ppermute | solution.py:463
  118.5 20.9 %collective-permute-start.9 = (bf16[256,512]{1,0:T(8,128)(2,1)}, bf16[256,512]{1,0:T(8,128)(2,1)}, u32[]{:S(2)}, u32[]{:S(2)}) collective-permute-start(bf16[256,512]{1,0:T(8,128)(2,1)} %get-tuple-element.37), channel_id=1, source_target_pairs={{0,6},{1,7},{2,0},{3,1},{4,2},{5,3},{6,4},{7,5},{8,14},{9,15},{10,... | collective-permute-start | bytes 786440 | tf_op jit(solution)/shard_map/ppermute | solution.py:463
  119.0 21.9 %collective-permute-start.10 = (bf16[256,512]{1,0:T(8,128)(2,1)}, bf16[256,512]{1,0:T(8,128)(2,1)}, u32[]{:S(2)}, u32[]{:S(2)}) collective-permute-start(bf16[256,512]{1,0:T(8,128)(2,1)} %get-tuple-element.38), channel_id=1, source_target_pairs={{0,2},{1,3},{2,4},{3,5},{4,6},{5,7},{6,0},{7,1},{8,10},{9,11},{10,... | collective-permute-start | bytes 786440 | tf_op jit(solution)/shard_map/ppermute | solution.py:463
  125.0 16.1 %collective-permute-start.8 = (bf16[256,512]{1,0:T(8,128)(2,1)}, bf16[256,512]{1,0:T(8,128)(2,1)}, u32[]{:S(2)}, u32[]{:S(2)}) collective-permute-start(bf16[256,512]{1,0:T(8,128)(2,1)} %get-tuple-element.36), channel_id=1, source_target_pairs={{0,2},{1,3},{2,4},{3,5},{4,6},{5,7},{6,0},{7,1},{8,10},{9,11},{10,... | collective-permute-start | bytes 786440 | tf_op jit(solution)/shard_map/ppermute | solution.py:463
  125.0 19.2 %collective-permute-start.11 = (bf16[256,512]{1,0:T(8,128)(2,1)}, bf16[256,512]{1,0:T(8,128)(2,1)}, u32[]{:S(2)}, u32[]{:S(2)}) collective-permute-start(bf16[256,512]{1,0:T(8,128)(2,1)} %get-tuple-element.39), channel_id=1, source_target_pairs={{0,6},{1,7},{2,0},{3,1},{4,2},{5,3},{6,4},{7,5},{8,14},{9,15},{10,... | collective-permute-start | bytes 786440 | tf_op jit(solution)/shard_map/ppermute | solution.py:463
  131.6 56.4 %collective-permute-start.15 = (bf16[256,512]{1,0:T(8,128)(2,1)}, bf16[256,512]{1,0:T(8,128)(2,1)}, u32[]{:S(2)}, u32[]{:S(2)}) collective-permute-start(bf16[256,512]{1,0:T(8,128)(2,1)} %get-tuple-element.47), channel_id=1, source_target_pairs={{0,6},{1,7},{2,0},{3,1},{4,2},{5,3},{6,4},{7,5},{8,14},{9,15},{10,... | collective-permute-start | bytes 786440 | tf_op jit(solution)/shard_map/ppermute | solution.py:463
  139.3 48.7 %collective-permute-start.16 = (bf16[256,512]{1,0:T(8,128)(2,1)}, bf16[256,512]{1,0:T(8,128)(2,1)}, u32[]{:S(2)}, u32[]{:S(2)}) collective-permute-start(bf16[256,512]{1,0:T(8,128)(2,1)} %get-tuple-element.48), channel_id=1, source_target_pairs={{0,2},{1,3},{2,4},{3,5},{4,6},{5,7},{6,0},{7,1},{8,10},{9,11},{10,... | collective-permute-start | bytes 786440 | tf_op jit(solution)/shard_map/ppermute | solution.py:463
  140.9 47.1 %collective-permute-start.14 = (bf16[256,512]{1,0:T(8,128)(2,1)}, bf16[256,512]{1,0:T(8,128)(2,1)}, u32[]{:S(2)}, u32[]{:S(2)}) collective-permute-start(bf16[256,512]{1,0:T(8,128)(2,1)} %get-tuple-element.46), channel_id=1, source_target_pairs={{0,2},{1,3},{2,4},{3,5},{4,6},{5,7},{6,0},{7,1},{8,10},{9,11},{10,... | collective-permute-start | bytes 786440 | tf_op jit(solution)/shard_map/ppermute | solution.py:463
  141.0 47.0 %collective-permute-start.17 = (bf16[256,512]{1,0:T(8,128)(2,1)}, bf16[256,512]{1,0:T(8,128)(2,1)}, u32[]{:S(2)}, u32[]{:S(2)}) collective-permute-start(bf16[256,512]{1,0:T(8,128)(2,1)} %get-tuple-element.49), channel_id=1, source_target_pairs={{0,6},{1,7},{2,0},{3,1},{4,2},{5,3},{6,4},{7,5},{8,14},{9,15},{10,... | collective-permute-start | bytes 786440 | tf_op jit(solution)/shard_map/ppermute | solution.py:463
  179.6 42.7 %all-to-all-start.3 = ((bf16[16,48,512]{2,1,0:T(8,128)(2,1)}), bf16[16,48,512]{2,1,0:T(8,128)(2,1)S(1)}, u32[]{:S(2)}, u32[]{:S(2)}) async-start(bf16[16,48,512]{2,1,0:T(8,128)(2,1)} %bitcast.35), calls=%async_computation.3 | async-start | bytes 1572864 | tf_op jit(solution)/shard_map/all_to_all | solution.py:467
  188.0 28.7 %copy-start.13 = (f32[512,128]{1,0:T(8,128)S(1)}, f32[512,128]{1,0:T(8,128)}, u32[]{:S(2)}) copy-start(f32[512,128]{1,0:T(8,128)} %copy-done.12) | copy-start | bytes 786436
  (22 other events, 100.9 us)

commit v2 on v1

v2 whole, which is shorter than its diff:
```python
import functools

import jax
import jax.numpy as jnp
import ml_dtypes
import numpy as np
from jax import lax
from jax.experimental import pallas as pl
from jax.experimental.pallas import tpu as pltpu
from jax.sharding import PartitionSpec as P

f32 = jnp.float32
bf16 = jnp.bfloat16
i32 = jnp.int32
SEGS = 8
ORDER = 16
EMPTY = 64.0
MIB = 48


def dot(a, b):
    return jnp.dot(a, b, preferred_element_type=f32)


def iota(shape, dim):
    return lax.broadcasted_iota(i32, shape, dim)


def ones_where(mask):
    return jnp.where(mask, 1.0, 0.0).astype(bf16)


def params(mib=MIB):
    return pltpu.CompilerParams(vmem_limit_bytes=mib * 2**20)


def cost(flops, nbytes):
    return pl.CostEstimate(flops=int(flops) // 10, bytes_accessed=int(nbytes) // 10, transcendentals=0)


def whole(shape):
    return pl.BlockSpec(shape, lambda *_: (0,) * len(shape))


def cols(shape):
    return pl.BlockSpec(shape, lambda j, *_: (0,) * (len(shape) - 1) + (j,))


def leading(shape):
    return pl.BlockSpec(shape, lambda j, *_: (j,) + (0,) * (len(shape) - 1))


def as_column(row):
    return jnp.transpose(jnp.broadcast_to(row.astype(f32), (128, row.shape[1])))[:, :1].astype(i32)


def send_slots(route, peers, slot_count):
    rows = route.shape[1]
    hot = iota((peers, rows), 0) == route
    earlier = ones_where(iota((rows, rows), 0) < iota((rows, rows), 1))
    rank = dot(ones_where(hot), earlier)
    rank = jnp.sum(jnp.where(hot, rank, 0.0), axis=0, keepdims=True)
    return route * slot_count + rank.astype(i32)


def place_rows(count, slots):
    peers = count.shape[0]
    per = slots // peers
    lane = iota((peers, slots), 1)
    low = iota((peers, slots), 0) * per
    mine = (lane >= low) & (lane < low + per)
    before = jnp.sum(jnp.where(lane >= low + per, count, 0.0), axis=0, keepdims=True)
    held = jnp.sum(jnp.where(mine, count, 0.0), axis=0, keepdims=True)
    within = jnp.sum(jnp.where(mine, (lane - low).astype(f32), 0.0), axis=0, keepdims=True)
    return jnp.where(within < held, before + within, -1.0).astype(i32)


def pack_product(planes, route, first, second, slot_count, peers, tile=256):
    _, rows, channels = planes.shape
    slots = peers * slot_count

    def body(route_ref, a_ref, b_ref, out_ref, hot_ref, fill_ref):
        @pl.when(pl.program_id(0) == 0)
        def _():
            hot = ones_where(iota((slots, rows), 0) == send_slots(route_ref[...], peers, slot_count))
            hot_ref[...] = hot
            fill_ref[...] = EMPTY * (1.0 - dot(hot, jnp.ones((rows, 128), bf16)))

        x = (a_ref[0].astype(f32) * b_ref[0].astype(f32)).astype(bf16)
        out_ref[...] = (dot(hot_ref[...], x) + fill_ref[:, :1]).astype(bf16)

    return pl.pallas_call(
        body,
        grid=(channels // tile,),
        in_specs=[whole((1, rows))]
        + [pl.BlockSpec((1, rows, tile), functools.partial(lambda s, j: (s, 0, j), s)) for s in (first, second)],
        out_specs=cols((slots, tile)),
        out_shape=jax.ShapeDtypeStruct((slots, channels), bf16),
        scratch_shapes=[pltpu.VMEM((slots, rows), bf16), pltpu.VMEM((slots, 128), f32)],
        compiler_params=params(),
        cost_estimate=cost(2 * slots * rows * channels, 2 * (2 * rows + slots) * channels),
        name="pack_kv",
    )(route, planes, planes)


def pack_two(planes, route, first, second, slot_count, peers, tile=512):
    _, rows, channels = planes.shape
    slots = peers * slot_count

    def body(route_ref, a_ref, b_ref, out_a_ref, out_b_ref, back_ref, hot_ref):
        @pl.when(pl.program_id(0) == 0)
        def _():
            slot = send_slots(route_ref[...], peers, slot_count)
            hot_ref[...] = ones_where(iota((slots, rows), 0) == slot)
            back_ref[...] = ones_where(iota((rows, slots), 1) == as_column(slot))

        out_a_ref[...] = dot(hot_ref[...], a_ref[0]).astype(bf16)
        out_b_ref[...] = dot(hot_ref[...], b_ref[0]).astype(bf16)

    return pl.pallas_call(
        body,
        grid=(channels // tile,),
        in_specs=[whole((1, rows))]
        + [pl.BlockSpec((1, rows, tile), functools.partial(lambda s, j: (s, 0, j), s)) for s in (first, second)],
        out_specs=[cols((slots, tile)), cols((slots, tile)), whole((rows, slots))],
        out_shape=[
            jax.ShapeDtypeStruct((slots, channels), bf16),
            jax.ShapeDtypeStruct((slots, channels), bf16),
            jax.ShapeDtypeStruct((rows, slots), bf16),
        ],
        scratch_shapes=[pltpu.VMEM((slots, rows), bf16)],
        compiler_params=params(),
        cost_estimate=cost(4 * slots * rows * channels, 4 * (rows + slots) * channels),
        name="pack_two",
    )(route, planes, planes)


def place_matrices(received, rows, slot_count, peers):
    slots = received.shape[0]

    def body(in_ref, to_ref, steps_ref, back_ref):
        used = ones_where(in_ref[...].astype(f32) < 0.75 * EMPTY)
        lane = iota((peers, slots), 1)
        low = iota((peers, slots), 0) * slot_count
        at = place_rows(dot(ones_where((lane >= low) & (lane < low + slot_count)), used)[:, :1], slots)
        to_ref[...] = ones_where(iota((rows, slots), 0) == at)
        span = rows // SEGS
        at = jnp.where(at < 0, at, (at % span) * SEGS + at // span)
        steps_ref[...] = ones_where(iota((rows, slots), 0) == at)
        back_ref[...] = ones_where(iota((slots, rows), 1) == as_column(at))

    return pl.pallas_call(
        body,
        grid=(1,),
        in_specs=[pl.BlockSpec((slots, 128), lambda j: (0, 0))],
        out_specs=[whole((rows, slots)), whole((rows, slots)), whole((slots, rows))],
        out_shape=[
            jax.ShapeDtypeStruct((rows, slots), bf16),
            jax.ShapeDtypeStruct((rows, slots), bf16),
            jax.ShapeDtypeStruct((slots, rows), bf16),
        ],
        compiler_params=params(),
        cost_estimate=cost(1e6, 6 * rows * slots),
        name="place",
    )(received)


def unpack(received, to_rows, tile=512):
    slots, channels = received.shape
    rows = to_rows.shape[0]

    def body(hot_ref, in_ref, out_ref):
        out_ref[...] = dot(hot_ref[...], in_ref[...]).astype(bf16)

    return pl.pallas_call(
        body,
        grid=(channels // tile,),
        in_specs=[whole(to_rows.shape), cols((slots, tile))],
        out_specs=cols((rows, tile)),
        out_shape=jax.ShapeDtypeStruct((rows, channels), bf16),
        compiler_params=params(),
        cost_estimate=cost(2 * slots * rows * channels, 2 * (rows + slots) * channels),
        name="unpack",
    )(to_rows, received)


def finish(returned, planes, plane, back, tile=512):
    slots, channels = returned.shape
    _, rows, _ = planes.shape

    def body(back_ref, gate_ref, in_ref, out_ref):
        out_ref[...] = (gate_ref[0].astype(f32) * dot(back_ref[...], in_ref[...])).astype(bf16)

    return pl.pallas_call(
        body,
        grid=(channels // tile,),
        in_specs=[
            whole((rows, slots)),
            pl.BlockSpec((1, rows, tile), lambda j: (plane, 0, j)),
            cols((slots, tile)),
        ],
        out_specs=cols((rows, tile)),
        out_shape=jax.ShapeDtypeStruct((rows, channels), bf16),
        compiler_params=params(),
        cost_estimate=cost(2 * slots * rows * channels, 2 * (2 * rows + slots) * channels),
        name="finish",
    )(back, planes, returned)


def two_parts(table):
    high = table.astype(ml_dtypes.bfloat16)
    return high, (table - high.astype(np.float64)).astype(ml_dtypes.bfloat16)


def dft_tables(taps):
    points = 2 * taps
    k = np.arange(taps)[:, None].astype(np.float64)
    t = np.arange(points)[None, :].astype(np.float64)
    forward = np.concatenate(
        [np.cos(2 * np.pi * k * t / points), np.cos(np.pi * t), -np.sin(2 * np.pi * k[1:] * t / points)]
    )
    inverse = forward.T[taps:] * (2.0 / points)
    inverse[:, 0] *= 0.5
    inverse[:, taps] *= 0.5
    return np.concatenate(two_parts(forward)), np.concatenate(two_parts(inverse))


def side_by_side(rows):
    p = np.arange(rows)
    t = (p % SEGS) * (rows // SEGS) + p // SEGS
    return (t[:, None] == p[None, :]).astype(ml_dtypes.bfloat16)


def forward_dft(table, x):
    both = dot(table, x)
    half = both.shape[0] // 2
    return both[:half] + both[half:]


def inverse_dft(table, y):
    half = table.shape[0] // 2
    high = y.astype(bf16)
    low = (y - high.astype(f32)).astype(bf16)
    both = dot(table, high)
    return both[:half] + both[half:] + dot(table[:half], low)


def through_filter(spectrum, filter_ref, inverse_table):
    taps = spectrum.shape[0] // 2
    a, b = spectrum[:taps], spectrum[taps:]
    re, im, re_last = filter_ref[0], filter_ref[1], filter_ref[2]
    return inverse_dft(inverse_table, jnp.concatenate([a * re - b * im, a * im + b * re_last]))


def filter_spectrum(mr_filter, forward, tile=512):
    taps, channels = mr_filter.shape

    def body(taps_ref, fwd_ref, out_ref):
        fwd = fwd_ref[:, :taps]
        x = taps_ref[...]
        high = x.astype(bf16)
        low = (x - high.astype(f32)).astype(bf16)
        h = forward_dft(fwd, high) + dot(fwd[: 2 * taps], low)
        first = iota((taps, tile), 0) == 0
        out_ref[0] = h[:taps]
        out_ref[1] = jnp.where(first, 0.0, h[taps:])
        out_ref[2] = jnp.where(first, h[taps:], h[:taps])

    return pl.pallas_call(
        body,
        grid=(channels // tile,),
        in_specs=[cols((taps, tile)), whole(forward.shape)],
        out_specs=cols((3, taps, tile)),
        out_shape=jax.ShapeDtypeStruct((3, taps, channels), f32),
        compiler_params=params(),
        cost_estimate=cost(6 * 2 * taps * taps * channels, 16 * taps * channels),
        name="spectrum",
    )(mr_filter, forward)


def filter_rows(u, spectrum, forward, inverse, tile=512):
    rows, channels = u.shape
    taps = spectrum.shape[1]

    def body(u_ref, h_ref, fwd_ref, inv_ref, out_ref):
        for b in range(rows // taps):
            if b == 0:
                x = forward_dft(fwd_ref[:, taps:], u_ref[:taps])
            else:
                x = forward_dft(fwd_ref[...], u_ref[(b - 1) * taps : (b + 1) * taps])
            out_ref[b * taps : (b + 1) * taps] = through_filter(x, h_ref, inv_ref[...])

    return pl.pallas_call(
        body,
        grid=(channels // tile,),
        in_specs=[cols((rows, tile)), cols((3, taps, tile)), whole(forward.shape), whole(inverse.shape)],
        out_specs=cols((rows, tile)),
        out_shape=jax.ShapeDtypeStruct((rows, channels), f32),
        compiler_params=params(),
        cost_estimate=cost(14 * taps * rows * channels, 8 * rows * channels),
        name="taps",
    )(u, spectrum, forward, inverse)


def gate(received, to_rows, filtered, rim, spectrum, forward, inverse, beside, tile=512):
    slots, channels = received.shape
    rows = to_rows.shape[0]
    taps = spectrum.shape[1]

    def body(hot_ref, in_ref, filt_ref, rim_ref, h_ref, fwd_ref, inv_ref, beside_ref, out_ref):
        q = dot(hot_ref[...], in_ref[...])
        early = through_filter(forward_dft(fwd_ref[:, :taps], rim_ref[...]), h_ref, inv_ref[...])
        first = (q[:taps] * (filt_ref[:taps] + early)).astype(bf16)
        rest = (q[taps:] * filt_ref[taps:]).astype(bf16)
        out_ref[...] = dot(beside_ref[...], jnp.concatenate([first, rest])).astype(bf16)

    return pl.pallas_call(
        body,
        grid=(channels // tile,),
        in_specs=[
            whole(to_rows.shape),
            cols((slots, tile)),
            cols((rows, tile)),
            cols((taps, tile)),
            cols((3, taps, tile)),
            whole(forward.shape),
            whole(inverse.shape),
            whole((rows, rows)),
        ],
        out_specs=cols((rows, tile)),
        out_shape=jax.ShapeDtypeStruct((rows, channels), bf16),
        compiler_params=params(),
        cost_estimate=cost(2 * slots * rows * channels, (6 * rows + 2 * slots) * channels),
        name="gate",
    )(to_rows, received, filtered, rim, spectrum, forward, inverse, beside)


def project(tasks, blocks, own, other, weight, other_weight, tile=512):
    rows, depth = own.shape
    width = depth
    steps = width // tile
    adds = [add for _, _, _, add, _ in tasks if add is not None]
    shapes = [jax.ShapeDtypeStruct((take, width), kind) for _, _, splits, _, kind in tasks for take in splits]

    def body(blocks_ref, own_ref, other_ref, *rest):
        arrived = iter(rest[2 * len(tasks) : 2 * len(tasks) + len(adds)])
        outs = iter(rest[2 * len(tasks) + len(adds) :])
        for n, (_, low, splits, add, kind) in enumerate(tasks):
            at = slice(low, low + sum(splits))
            total = dot(own_ref[at], rest[2 * n][...]) + dot(other_ref[at], rest[2 * n + 1][...])
            if add is not None:
                total = total + next(arrived)[...].astype(f32)
            start = 0
            for take in splits:
                next(outs)[...] = total[start : start + take].astype(kind)
                start += take

    specs = [whole((rows, depth))] * 2
    operands = [own, other]
    for dx, *_ in tasks:
        spec = pl.BlockSpec(
            (depth, tile), functools.partial(lambda d, j, b: (0, b[d] * steps + j), dx)
        )
        specs += [spec, spec]
        operands += [weight, other_weight]
    for add in adds:
        specs.append(cols((add.shape[0], tile)))
        operands.append(add)
    total_rows = sum(shape.shape[0] for shape in shapes)
    return pl.pallas_call(
        body,
        grid_spec=pltpu.PrefetchScalarGridSpec(
            num_scalar_prefetch=1,
            grid=(steps,),
            in_specs=specs,
            out_specs=[cols((shape.shape[0], tile)) for shape in shapes],
        ),
        out_shape=shapes,
        compiler_params=params(),
        cost_estimate=cost(
            4 * depth * width * total_rows, 4 * depth * width * len(tasks) + 4 * rows * depth + 4 * total_rows * width
        ),
        name="project",
    )(blocks, *operands)


def rows_of(t):
    return pl.ds(pl.multiple_of(t * SEGS, SEGS), SEGS)


def spread(ref, which, lanes):
    return [jnp.broadcast_to(ref[which, n : n + 1, lanes], (SEGS, 128)) for n in range(ORDER)]


def total_of(terms):
    while len(terms) > 1:
        terms = [a + b for a, b in zip(terms[::2], terms[1::2])]
    return terms[0]


def end_states(table, own, arrived, k_li, last, coef, peers, tile=256):
    rows, width = own.shape
    half = rows // 2
    blocks = tile // 128

    def body(table_ref, own_ref, a0_ref, a1_ref, b0_ref, b1_ref, k_ref, last_ref, coef_ref, u_ref, seg_ref, end_ref):
        top = own_ref[:half] + a0_ref[...].astype(f32) + a1_ref[...].astype(f32)
        top = top * k_ref[:half].astype(f32)
        bottom = own_ref[half:] + b0_ref[...].astype(f32) + b1_ref[...].astype(f32)
        bottom = bottom * k_ref[half:].astype(f32)
        for cb in range(blocks):
            lanes = slice(cb * 128, (cb + 1) * 128)
            u_ref[cb, :half] = top[:, lanes]
            u_ref[cb, half:] = bottom[:, lanes]
        for cb in range(blocks):
            lanes = slice(cb * 128, (cb + 1) * 128)
            decay = spread(coef_ref, 0, lanes)

            def step(t, state):
                u = u_ref[cb, rows_of(t), :] * last_ref[rows_of(t), :]
                return tuple(d * s + u for d, s in zip(decay, state))

            state = lax.fori_loop(0, rows // SEGS, step, (jnp.zeros((SEGS, 128), f32),) * ORDER, unroll=8)
            for n in range(ORDER):
                seg_ref[cb, n * SEGS : (n + 1) * SEGS] = state[n]
            total = jnp.zeros((ORDER, 128), f32)
            for s in range(SEGS):
                keep = jnp.where(table_ref[s] == 0, coef_ref[1, :, lanes], 0.0)
                total = keep * total + seg_ref[cb, pl.ds(s, ORDER, stride=SEGS), :]
            for p in range(peers):
                end_ref[p * ORDER : (p + 1) * ORDER, lanes] = total.astype(bf16)

    return pl.pallas_call(
        body,
        grid_spec=pltpu.PrefetchScalarGridSpec(
            num_scalar_prefetch=1,
            grid=(width // tile,),
            in_specs=[
                cols((rows, tile)),
                cols((half, tile)),
                cols((half, tile)),
                cols((half, tile)),
                cols((half, tile)),
                cols((rows, tile)),
                whole(last.shape),
                cols((4, ORDER, tile)),
            ],
            out_specs=[
                leading((blocks, rows, 128)),
                leading((blocks, ORDER * SEGS, 128)),
                cols((peers * ORDER, tile)),
            ],
        ),
        out_shape=[
            jax.ShapeDtypeStruct((width // 128, rows, 128), f32),
            jax.ShapeDtypeStruct((width // 128, ORDER * SEGS, 128), f32),
            jax.ShapeDtypeStruct((peers * ORDER, width), bf16),
        ],
        compiler_params=params(),
        cost_estimate=cost(4e9, 12 * rows * width),
        name="ends",
    )(table, own, *arrived, k_li, last, coef)


def recur(table, segs, u, keep, coef, step_blocks=2):
    count, rows, _ = u.shape

    def body(table_ref, seg_ref, u_ref, keep_ref, coef_ref, li_ref, in_ref):
        for cb in range(step_blocks):
            lanes = slice(cb * 128, (cb + 1) * 128)
            enter = jnp.zeros((ORDER, 128), f32)
            for s in range(SEGS):
                in_ref[pl.ds(s, ORDER, stride=SEGS), :] = enter
                fade = jnp.where(table_ref[s] == 0, coef_ref[1, :, lanes], 0.0)
                enter = fade * enter + seg_ref[cb, pl.ds(s, ORDER, stride=SEGS), :]
            decay, weigh = spread(coef_ref, 0, lanes), spread(coef_ref, 3, lanes)

            def step(t, state):
                u, kept = u_ref[cb, rows_of(t), :], keep_ref[rows_of(t), :]
                state = tuple((d * s) * kept + u for d, s in zip(decay, state))
                li_ref[cb, rows_of(t), :] = total_of([w * s for w, s in zip(weigh, state)])
                return state

            state = tuple(in_ref[n * SEGS : (n + 1) * SEGS] for n in range(ORDER))
            lax.fori_loop(0, rows // SEGS, step, state, unroll=8)

    return pl.pallas_call(
        body,
        grid_spec=pltpu.PrefetchScalarGridSpec(
            num_scalar_prefetch=1,
            grid=(count // step_blocks,),
            in_specs=[
                leading((step_blocks, ORDER * SEGS, 128)),
                leading((step_blocks, rows, 128)),
                whole(keep.shape),
                cols((4, ORDER, step_blocks * 128)),
            ],
            out_specs=leading((step_blocks, rows, 128)),
            scratch_shapes=[pltpu.VMEM((ORDER * SEGS, 128), f32)],
        ),
        out_shape=jax.ShapeDtypeStruct(u.shape, f32),
        compiler_params=params(),
        cost_estimate=cost(8e9, 8 * count * rows * 128),
        name="recur",
    )(table, segs, u, keep, coef)


def carry_in(table, ends, li, unbroken, coef, back, peers, step_blocks=2):
    count, rows, _ = li.shape
    slots = back.shape[0]
    tile = step_blocks * 128

    def body(table_ref, ends_ref, li_ref, unbroken_ref, coef_ref, back_ref, out_ref, in_ref, sum_ref):
        def hop(j, carry):
            return jnp.where(table_ref[SEGS + j] == 0, coef_ref[2], 0.0) * carry + ends_ref[j].astype(f32)

        carry = lax.fori_loop(0, table_ref[SEGS + peers], hop, jnp.zeros((ORDER, tile), f32))
        for cb in range(step_blocks):
            lanes = slice(cb * 128, (cb + 1) * 128)
            enter = carry[:, lanes] * coef_ref[3, :, lanes]
            for s in range(SEGS):
                in_ref[pl.ds(s, ORDER, stride=SEGS), :] = enter
                enter = coef_ref[1, :, lanes] * enter
            decay = spread(coef_ref, 0, lanes)

            def step(t, state):
                state = tuple(d * s for d, s in zip(decay, state))
                more = total_of(list(state)) * unbroken_ref[rows_of(t), :]
                sum_ref[rows_of(t), lanes] = li_ref[cb, rows_of(t), :] + more
                return state

            state = tuple(in_ref[n * SEGS : (n + 1) * SEGS] for n in range(ORDER))
            lax.fori_loop(0, rows // SEGS, step, state, unroll=8)
        out_ref[...] = dot(back_ref[...], sum_ref[...].astype(bf16)).astype(bf16)

    return pl.pallas_call(
        body,
        grid_spec=pltpu.PrefetchScalarGridSpec(
            num_scalar_prefetch=1,
            grid=(count // step_blocks,),
            in_specs=[
                cols((peers, ORDER, tile)),
                leading((step_blocks, rows, 128)),
                whole(unbroken.shape),
                cols((4, ORDER, tile)),
                whole(back.shape),
            ],
            out_specs=cols((slots, tile)),
            scratch_shapes=[pltpu.VMEM((ORDER * SEGS, 128), f32), pltpu.VMEM((rows, tile), f32)],
        ),
        out_shape=jax.ShapeDtypeStruct((slots, count * 128), bf16),
        compiler_params=params(),
        cost_estimate=cost(4e9, 8 * count * rows * 128),
        name="carry",
    )(table, ends, li, unbroken, coef, back)


def along_x(shard, dx, dcore=0):
    count = lax.axis_size("tp") // 2
    pairs = [
        (2 * x + c, 2 * ((x + dx) % count) + (c + dcore) % 2) for x in range(count) for c in range(2)
    ]
    return lax.ppermute(shard, "tp", pairs)


def lane_mask(hit):
    return jnp.broadcast_to(jnp.where(hit, 0.0, 1.0).astype(f32)[:, None], (hit.shape[0], 128))


def swap(shard):
    return lax.all_to_all(shard, "ctx", split_axis=0, concat_axis=0, tiled=True)


def together(*arrays):
    return lax.optimization_barrier(arrays)


def on_device(projected, route, contig_len, mr_filter, out_weight, li_rate, li_residue):
    rows, _, channels = projected.shape
    peers = lax.axis_size("ctx")
    slot_count = 3 * rows // (2 * peers)
    taps = mr_filter.shape[0]
    half = rows // 2
    me = lax.axis_index("ctx").astype(i32)
    tp = lax.axis_index("tp").astype(i32)
    chip, core = tp // 2, tp % 2
    chips = lax.axis_size("tp") // 2
    planes = jnp.transpose(projected, (1, 0, 2))
    route_row = route.reshape(1, rows)
    me_row = me.reshape(1)
    span = rows // SEGS
    forward, inverse = (jnp.asarray(t) for t in dft_tables(taps))
    beside = jnp.asarray(side_by_side(rows))

    packed_kv = pack_product(planes, route_row, 1, 2, slot_count, peers)
    packed_kv, other_source = together(packed_kv, out_weight)
    other_weight = along_x(other_source, 0, 1)
    got_kv = swap(packed_kv)
    packed_q, packed_k, to_loader = pack_two(planes, route_row, 0, 4, slot_count, peers)

    order = jnp.arange(contig_len.shape[0], dtype=i32)
    starts = jnp.sum(jnp.where(order[:, None] < order[None, :], contig_len[:, None], 0), axis=0)
    here = me * rows + jnp.arange(SEGS, dtype=i32)[None, :] * span + jnp.arange(span, dtype=i32)[:, None]
    here = here.reshape(rows, 1)
    seg_last = here - here % span + (span - 1)
    seen, behind = starts[None, :] <= here, starts[None, :] > here
    keep = lane_mask(jnp.any(starts[None, :] == here, axis=1))
    last = lane_mask(jnp.any(behind & (starts[None, :] <= seg_last), axis=1))
    unbroken = lane_mask(jnp.any(seen & (starts[None, :] >= me * rows), axis=1))
    seg_ids = me * SEGS + jnp.arange(SEGS, dtype=i32)
    seg_has = jnp.any(seg_ids[:, None] == (starts // span)[None, :], axis=1)
    dev_has = jnp.any(jnp.arange(peers, dtype=i32)[:, None] == (starts // rows)[None, :], axis=1)
    table = jnp.concatenate([seg_has.astype(i32), dev_has.astype(i32), me_row])
    mode_weight = li_residue * jnp.sqrt(-jnp.expm1(-2.0 * li_rate))
    coef = jnp.stack([jnp.exp(-li_rate), jnp.exp(-li_rate * span), jnp.exp(-li_rate * rows), mode_weight])
    spectrum = filter_spectrum(mr_filter, forward)

    blocks = jnp.stack([2 * ((chip + d) % chips) + core for d in range(chips)]).astype(i32)

    got_kv, packed_q, coef, spectrum = together(got_kv, packed_q, coef, spectrum)
    got_q = swap(packed_q)
    to_rows, to_steps, to_slots = place_matrices(got_kv, rows, slot_count, peers)
    u_mr = unpack(got_kv, to_rows)
    rim = lax.ppermute(u_mr[rows - taps :], "ctx", [(i, i + 1) for i in range(peers - 1)])
    filtered = filter_rows(u_mr, spectrum, forward, inverse)
    got_q, filtered, packed_k = together(got_q, filtered, packed_k)
    got_k = swap(packed_k)
    gated = gate(got_q, to_rows, filtered, rim, spectrum, forward, inverse, beside)
    other = along_x(gated, 0, 1)
    mm = functools.partial(project, own=gated, weight=out_weight, other_weight=other_weight)
    far_a, far_b = mm([(2, 0, (half, half), None, bf16)], blocks, other=other)
    blocks, far_a, far_b = together(blocks, far_a, far_b)
    pass_a, pass_b = along_x(far_a, 1), along_x(far_b, -1)
    up_b, down_a = mm([(1, half, (half,), None, bf16), (3, 0, (half,), None, bf16)], blocks, other=other)
    up_b, down_a, blocks = together(up_b, down_a, blocks)
    from_low_b, from_high_a = along_x(up_b, 1), along_x(down_a, -1)
    [mine] = mm([(0, 0, (rows,), None, f32)], blocks, other=other)
    got_k, pass_a, pass_b, mine = together(got_k, pass_a, pass_b, mine)
    k_li = unpack(got_k, to_steps)
    up_a, down_b = mm([(1, 0, (half,), pass_a, bf16), (3, half, (half,), pass_b, bf16)], blocks, other=other)
    from_low_a, from_high_b = along_x(up_a, 1), along_x(down_b, -1)
    u, segs, end = end_states(
        table, mine, [from_low_a, from_high_a, from_low_b, from_high_b], k_li, last, coef, peers
    )
    ends = swap(end).reshape(peers, ORDER, channels)
    li = recur(table, segs, u, keep, coef)
    returned = swap(carry_in(table, ends, li, unbroken, coef, to_slots, peers))
    return finish(returned, planes, 3, to_loader)


def solution(mesh):
    return jax.shard_map(
        on_device,
        mesh=mesh,
        in_specs=(
            P("ctx", None, "tp"),
            P("ctx"),
            P(),
            P(None, "tp"),
            P("tp", None),
            P(None, "tp"),
            P(None, "tp"),
        ),
        out_specs=P("ctx", "tp"),
        check_vma=False,
    )
```

time: 243 us -> 186 us (0.77)
  blocking collectives: 89.7 us -> 26.5 us
  waiting for transfers between devices: 14.4 us -> 38.4 us
  Pallas kernels: 78.6 us -> 66.5 us
  starting transfers between devices: 43.4 us -> 38.7 us
    all_gather x3 -> x0, blocking collectives: 73.6 us -> none  [the longest x2 48.8 us: on_device(): ends = lax.all_gather(end, 'ctx', axis=0, tiled=False)]
    all_to_all x4, waiting for transfers between devices: 14.3 us -> 30.1 us  [swap(): return lax.all_to_all(shard, 'ctx', split_axis=0, concat_axis=0, tiled=True)]
    all_to_all x1, blocking collectives: 16.1 us -> 26.5 us  [swap(): return lax.all_to_all(shard, 'ctx', split_axis=0, concat_axis=0, tiled=True)]
    ppermute x17 -> x8, starting transfers between devices: 18.7 us -> 8.66 us  [along_x(): return lax.ppermute(shard, 'tp', pairs)]
    pallas_call x8 -> x4, Pallas kernels: 31.5 us -> 21.7 us  [project(): pl.pallas_call(body, grid_spec=pltpu.PrefetchScalarGridSpec(num_scalar_pr...]
    pallas_call x4 -> x7, Pallas kernels: 12.1 us -> 21.9 us  [the longest x1 5.24 us: carry_in(): pl.pallas_call(body, grid_spec=pltpu.PrefetchScalarGridSpec(num_scalar_pr...]
    ppermute x17 -> x8, waiting for transfers between devices: 0.04 us -> 8.28 us  [along_x(): return lax.ppermute(shard, 'tp', pairs)]
    dynamic_slice x1 -> x0, local copies, waits for them, and re-layouts: 7.08 us -> none  [on_device(): lax.dynamic_slice(out_weight, (0, (2 * ((chip + d) % chips) + 1 - core) *...]
  transfers between devices with their start and end apart: 22 -> 13, of which waited for: 1 -> 5; matrix products, arithmetic and copies ran while one was open for 3% -> 1% of each run, Pallas kernels for 29% -> 25%
where the time goes in v2:
time: 186 us; the launch traced here: 185 us
  Pallas kernels  66.5 us (36%)
  starting transfers between devices  38.7 us (21%)
  waiting for transfers between devices  38.4 us (21%)
  blocking collectives  26.5 us (14%)
  local copies, waits for them, and re-layouts  13.3 us (7%)
    all_to_all x4, waiting for transfers between devices, swap(): return lax.all_to_all(shard, 'ctx', split_axis=0, concat_axis=0, tiled=True)  30.1 us
    all_to_all x1, blocking collectives, swap(): return lax.all_to_all(shard, 'ctx', split_axis=0, concat_axis=0, tiled=True)  26.5 us
    all_to_all x4, starting transfers between devices, swap(): return lax.all_to_all(shard, 'ctx', split_axis=0, concat_axis=0, tiled=True)  26.2 us
    pallas_call x4, Pallas kernels, project(): pl.pallas_call(body, grid_spec=pltpu.PrefetchScalarGridSpec(num_scalar_pr...  21.7 us
    unnamed x48, local copies, waits for them, and re-layouts  12.8 us
    ppermute x8, starting transfers between devices, along_x(): return lax.ppermute(shard, 'tp', pairs)  8.66 us
    ppermute x8, waiting for transfers between devices, along_x(): return lax.ppermute(shard, 'tp', pairs)  8.28 us
    pallas_call x1, Pallas kernels, recur(): pl.pallas_call(body, grid_spec=pltpu.PrefetchScalarGridSpec(num_scalar_pr...  6.52 us
  transfers between devices with their start and end apart: 13, of which 5 were waited for; matrix products, arithmetic and copies ran while one was open for 1% of the time, Pallas kernels for 25%

profile of v2, /device:TPU:0, one launch (start us, length us, event | category | flops | bytes accessed | tf_op | source)
XLA Modules:
  0.0 184.7 jit_solution(2225112329185995167)
XLA Ops:
  0.7 5.2 %pack_kv.1 = bf16[768,1024]{1,0:T(8,128)(2,1)} custom-call(s32[1,512]{1,0:T(1,128)S(1)} %bitcast.30, bf16[5,512,1024]{2,1,0:T(8,128)(2,1)} %bitcast.32, bf16[5,512,1024]{2,1,0:T(8,128)(2,1)} %bitcast.33), custom_call_target="tpu_custom_call" | custom-call | flops 80530640 | bytes 367001 | tf_op jit(solution)/shard_map/pack_kv/pallas_call | solution.py:92
  5.8 8.3 %all-to-all-start = ((bf16[16,48,1024]{2,1,0:T(8,128)(2,1)}), bf16[16,48,1024]{2,1,0:T(8,128)(2,1)S(1)}, u32[]{:S(2)}, u32[]{:S(2)}) async-start(bf16[16,48,1024]{2,1,0:T(8,128)(2,1)} %bitcast.3), calls=%async_computation | async-start | bytes 3145728 | tf_op jit(solution)/shard_map/all_to_all | solution.py:571
  16.1 4.3 %pack_two.1 = (bf16[768,1024]{1,0:T(8,128)(2,1)S(1)}, bf16[768,1024]{1,0:T(8,128)(2,1)S(1)}, bf16[512,768]{1,0:T(8,128)(2,1)S(1)}) custom-call(s32[1,512]{1,0:T(1,128)S(1)} %bitcast.31, bf16[5,512,1024]{2,1,0:T(8,128)(2,1)} %bitcast.34, bf16[5,512,1024]{2,1,0:T(8,128)(2,1)} %bitcast.35), custom_call_target="tpu_custom_call" | custom-call | flops 161061280 | bytes 524288 | tf_op jit(solution)/shard_map/pack_two/pallas_call | solution.py:120
  23.0 16.4 %all-to-all-done = bf16[16,48,1024]{2,1,0:T(8,128)(2,1)S(1)} async-done(((bf16[16,48,1024]{2,1,0:T(8,128)(2,1)}), bf16[16,48,1024]{2,1,0:T(8,128)(2,1)S(1)}, u32[]{:S(2)}, u32[]{:S(2)}) %all-to-all-start) | async-done | bytes 1572896 | tf_op jit(solution)/shard_map/all_to_all | solution.py:571
  39.4 4.4 %all-to-all-start.1 = ((bf16[16,48,1024]{2,1,0:T(8,128)(2,1)}), bf16[16,48,1024]{2,1,0:T(8,128)(2,1)}, u32[]{:S(2)}, u32[]{:S(2)}) async-start(bf16[16,48,1024]{2,1,0:T(8,128)(2,1)} %bitcast.29), calls=%async_computation.1 | async-start | bytes 3145728 | tf_op jit(solution)/shard_map/all_to_all | solution.py:571
  47.4 3.8 %collective-permute-start = (bf16[128,1024]{1,0:T(8,128)(2,1)S(1)}, bf16[128,1024]{1,0:T(8,128)(2,1)S(1)}, u32[]{:S(2)}, u32[]{:S(2)}) collective-permute-start(bf16[128,1024]{1,0:T(8,128)(2,1)S(1)} %slice.4), channel_id=1, source_target_pairs={{0,8},{8,16},{16,24},{24,32},{32,40},{40,48},{48,56},{56,64},{64,7... | collective-permute-start | bytes 786440 | tf_op jit(solution)/shard_map/ppermute | solution.py:624
  51.3 4.0 %taps.1.filt_ref = f32[512,1024]{1,0:T(8,128)S(1)} custom-call(bf16[512,1024]{1,0:T(8,128)(2,1)S(1)} %unpack.2.u_ref, f32[3,128,1024]{2,1,0:T(8,128)S(1)} %spectrum.1.h_ref, bf16[512,256]{1,0:T(8,128)(2,1)S(1)} %copy-done.5, bf16[256,256]{1,0:T(8,128)(2,1)S(1)} %copy-done.16), custom_call_target="tpu_custom_call" | custom-call | flops 93952408 | bytes 419430 | tf_op jit(solution)/shard_map/taps/pallas_call | solution.py:293
  56.7 10.0 %all-to-all-done.1 = bf16[16,48,1024]{2,1,0:T(8,128)(2,1)} async-done(((bf16[16,48,1024]{2,1,0:T(8,128)(2,1)}), bf16[16,48,1024]{2,1,0:T(8,128)(2,1)}, u32[]{:S(2)}, u32[]{:S(2)}) %all-to-all-start.1) | async-done | bytes 1572896 | tf_op jit(solution)/shard_map/all_to_all | solution.py:571
  68.9 4.4 %gate.1.own_ref = bf16[512,1024]{1,0:T(8,128)(2,1)S(1)} custom-call(bf16[512,768]{1,0:T(8,128)(2,1)S(1)} %copy-done.3, bf16[768,1024]{1,0:T(8,128)(2,1)} %bitcast.10.in_ref, f32[512,1024]{1,0:T(8,128)} %copy-done.1, bf16[128,1024]{1,0:T(8,128)(2,1)S(1)} %collective-permute-done.rim_ref, f32[3,128,1024]{2,1,0:T(8,128)S(1)} %spectrum.1.h_ref, ...), custom_call_target="tpu_custom_call" | custom-call | flops 80530640 | bytes 471859 | tf_op jit(solution)/shard_map/gate/pallas_call | solution.py:317
  73.4 7.3 %all-to-all-start.2 = ((bf16[16,48,1024]{2,1,0:T(8,128)(2,1)}), bf16[16,48,1024]{2,1,0:T(8,128)(2,1)}, u32[]{:S(2)}, u32[]{:S(2)}) async-start(bf16[16,48,1024]{2,1,0:T(8,128)(2,1)} %bitcast.28), calls=%async_computation.2 | async-start | bytes 3145728 | tf_op jit(solution)/shard_map/all_to_all | solution.py:571
  81.4 5.4 %project.4 = (bf16[256,1024]{1,0:T(8,128)(2,1)}, bf16[256,1024]{1,0:T(8,128)(2,1)}) custom-call(s32[4]{0:T(128)S(1)} %pad_add_fusion.1.blocks_ref, bf16[512,1024]{1,0:T(8,128)(2,1)S(1)} %gate.1.own_ref, bf16[512,1024]{1,0:T(8,128)(2,1)S(1)} %collective-permute-done.1.other_ref, bf16[1024,8192]{1,0:T(8,128)(2,1)} %rest_2_.3, ...), custom_call_target="tpu_custom_call" | custom-call | flops 214748368 | bytes 838860 | tf_op jit(solution)/shard_map/project/pallas_call | solution.py:370
  88.2 1.7 collective-permute-start.4
  90.2 6.1 %project.5 = (bf16[256,1024]{1,0:T(8,128)(2,1)}, bf16[256,1024]{1,0:T(8,128)(2,1)}) custom-call(s32[4]{0:T(128)S(1)} %pad_add_fusion.1.blocks_ref, bf16[512,1024]{1,0:T(8,128)(2,1)S(1)} %gate.1.own_ref, bf16[512,1024]{1,0:T(8,128)(2,1)S(1)} %collective-permute-done.1.other_ref, bf16[1024,8192]{1,0:T(8,128)(2,1)} %rest_2_.3, ...), custom_call_target="tpu_custom_call" | custom-call | flops 214748368 | bytes 1258291 | tf_op jit(solution)/shard_map/project/pallas_call | solution.py:370
  98.3 4.8 %project.6.own_ref = f32[512,1024]{1,0:T(8,128)S(1)} custom-call(s32[4]{0:T(128)S(1)} %pad_add_fusion.1.blocks_ref, bf16[512,1024]{1,0:T(8,128)(2,1)S(1)} %gate.1.own_ref, bf16[512,1024]{1,0:T(8,128)(2,1)S(1)} %collective-permute-done.1.other_ref, bf16[1024,8192]{1,0:T(8,128)(2,1)} %rest_2_.3, bf16[1024,8192]{1,0:T(8,128)(2,1)} %collective-permute-done.2.rest_1_.rest_3_), custom_call_target="tpu_custom_call" | custom-call | flops 214748368 | bytes 838860 | tf_op jit(solution)/shard_map/project/pallas_call | solution.py:370
  105.9 5.4 %project.7 = (bf16[256,1024]{1,0:T(8,128)(2,1)S(1)}, bf16[256,1024]{1,0:T(8,128)(2,1)S(1)}) custom-call(s32[4]{0:T(128)S(1)} %pad_add_fusion.1.blocks_ref, bf16[512,1024]{1,0:T(8,128)(2,1)S(1)} %gate.1.own_ref, bf16[512,1024]{1,0:T(8,128)(2,1)S(1)} %collective-permute-done.1.other_ref, bf16[1024,8192]{1,0:T(8,128)(2,1)} %rest_2_.3, ...), custom_call_target="tpu_custom_call" | custom-call | flops 214748368 | bytes 1258291 | tf_op jit(solution)/shard_map/project/pallas_call | solution.py:370
  114.7 2.4 %unpack.3.k_ref = bf16[512,1024]{1,0:T(8,128)(2,1)S(1)} custom-call(bf16[512,768]{1,0:T(8,128)(2,1)S(1)} %copy-done.15, bf16[768,1024]{1,0:T(8,128)(2,1)} %bitcast.12.in_ref), custom_call_target="tpu_custom_call" | custom-call | flops 80530640 | bytes 262144 | tf_op jit(solution)/shard_map/unpack/pallas_call | solution.py:175
  117.1 8.3 %collective-permute-done.5.a0_ref = bf16[256,1024]{1,0:T(8,128)(2,1)S(1)} collective-permute-done((bf16[256,1024]{1,0:T(8,128)(2,1)S(1)}, bf16[256,1024]{1,0:T(8,128)(2,1)S(1)}, u32[]{:S(2)}, u32[]{:S(2)}) %collective-permute-start.5) | collective-permute-done | bytes 524320 | tf_op jit(solution)/shard_map/ppermute | solution.py:563
  125.5 6.4 %ends.1 = (f32[8,512,128]{2,1,0:T(8,128)}, f32[8,128,128]{2,1,0:T(8,128)S(1)}, bf16[256,1024]{1,0:T(8,128)(2,1)}) custom-call(s32[25]{0:T(128)S(1)} %pad_add_fusion.table_ref, f32[512,1024]{1,0:T(8,128)} %copy-done, bf16[256,1024]{1,0:T(8,128)(2,1)S(1)} %collective-permute-done.5.a0_ref, bf16[256,1024]{1,0:T(8,128)(2,1)} %collective-permute-done.6.a1_ref, ...), custom_call_target="tpu_custom_call" | custom-call | flops 400000000 | bytes 629145 | tf_op jit(solution)/shard_map/ends/pallas_call | solution.py:433
  131.9 6.2 %all-to-all-start.3 = ((bf16[16,16,1024]{2,1,0:T(8,128)(2,1)}), bf16[16,16,1024]{2,1,0:T(8,128)(2,1)S(1)}, u32[]{:S(2)}, u32[]{:S(2)}) async-start(bf16[16,16,1024]{2,1,0:T(8,128)(2,1)} %bitcast.17), calls=%async_computation.3 | async-start | bytes 1048576 | tf_op jit(solution)/shard_map/all_to_all | solution.py:571
  139.9 6.5 %recur.1.li_ref = f32[8,512,128]{2,1,0:T(8,128)S(1)} custom-call(s32[25]{0:T(128)S(1)} %pad_add_fusion.table_ref, f32[8,128,128]{2,1,0:T(8,128)S(1)} %get-tuple-element.70.seg_ref, f32[8,512,128]{2,1,0:T(8,128)S(1)} %copy-done.7, f32[512,128]{1,0:T(8,128)S(1)} %broadcast_in_dim.35.keep_ref, f32[4,16,1024]{2,1,0:T(8,128)S(1)} %pad_maximum_fusion.coef_ref), custom_call_target="tpu_custom_call" | custom-call | flops 800000000 | bytes 419430 | tf_op jit(solution)/shard_map/recur/pallas_call | solution.py:487
  146.4 2.2 %all-to-all-done.3.ends_ref = bf16[16,16,1024]{2,1,0:T(8,128)(2,1)S(1)} async-done(((bf16[16,16,1024]{2,1,0:T(8,128)(2,1)}), bf16[16,16,1024]{2,1,0:T(8,128)(2,1)S(1)}, u32[]{:S(2)}, u32[]{:S(2)}) %all-to-all-start.3) | async-done | bytes 524320 | tf_op jit(solution)/shard_map/all_to_all | solution.py:571
  149.9 5.2 %carry.1 = bf16[768,1024]{1,0:T(8,128)(2,1)S(1)} custom-call(s32[25]{0:T(128)S(1)} %pad_add_fusion.table_ref, bf16[16,16,1024]{2,1,0:T(8,128)(2,1)S(1)} %all-to-all-done.3.ends_ref, f32[8,512,128]{2,1,0:T(8,128)S(1)} %recur.1.li_ref, f32[512,128]{1,0:T(8,128)S(1)} %broadcast_in_dim.36.unbroken_ref, f32[4,16,1024]{2,1,0:T(8,128)S(1)} %pad_maximum_fusion.coef_ref, ...), custom_call_target="tpu_custom_call" | custom-call | flops 400000000 | bytes 419430 | tf_op jit(solution)/shard_map/carry/pallas_call | solution.py:536
  155.2 26.5 %all_to_all.56 = bf16[16,48,1024]{2,1,0:T(8,128)(2,1)S(1)} all-to-all(bf16[16,48,1024]{2,1,0:T(8,128)(2,1)S(1)} %bitcast.26), channel_id=1, replica_groups=mesh['ctx'=16,'tp'=8] {'ctx'}, dimensions={0} | all-to-all | bytes 3145728 | tf_op jit(solution)/shard_map/all_to_all | solution.py:571
  181.7 3.0 %finish.1 = bf16[512,1024]{1,0:T(8,128)(2,1)} custom-call(bf16[512,768]{1,0:T(8,128)(2,1)S(1)} %copy-done.11, bf16[5,512,1024]{2,1,0:T(8,128)(2,1)} %bitcast.36, bf16[768,1024]{1,0:T(8,128)(2,1)S(1)} %bitcast.27), custom_call_target="tpu_custom_call" | custom-call | flops 80530640 | bytes 367001 | tf_op jit(solution)/shard_map/finish/pallas_call | solution.py:194
  (90 shorter events, 25.9 us)
Async XLA Ops:
  5.8 75.5 %collective-permute-start.2 = (bf16[1024,8192]{1,0:T(8,128)(2,1)}, bf16[1024,8192]{1,0:T(8,128)(2,1)}, u32[]{:S(2)}, u32[]{:S(2)}) collective-permute-start(bf16[1024,8192]{1,0:T(8,128)(2,1)} %rest_2_.3), channel_id=1, source_target_pairs={{0,1},{1,0},{2,3},{3,2},{4,5},{5,4},{6,7},{7,6},{8,9},{9,8},{10,11... | collective-permute-start | bytes 50331656 | tf_op jit(solution)/shard_map/ppermute | solution.py:563
  5.8 8.3 %copy-start.4 = (bf16[512,256]{1,0:T(8,128)(2,1)S(1)}, bf16[512,256]{1,0:T(8,128)(2,1)}, u32[]{:S(2)}) copy-start(bf16[512,256]{1,0:T(8,128)(2,1)} %constant.117.clone.fwd_ref) | copy-start | bytes 786436
  5.8 33.6 %all-to-all-start = ((bf16[16,48,1024]{2,1,0:T(8,128)(2,1)}), bf16[16,48,1024]{2,1,0:T(8,128)(2,1)S(1)}, u32[]{:S(2)}, u32[]{:S(2)}) async-start(bf16[16,48,1024]{2,1,0:T(8,128)(2,1)} %bitcast.3), calls=%async_computation | async-start | bytes 3145728 | tf_op jit(solution)/shard_map/all_to_all | solution.py:571
  16.1 5.2 %copy-start.21 = (f32[16,1024]{1,0:T(8,128)S(1)}, f32[16,1024]{1,0:T(8,128)}, u32[]{:S(2)}) copy-start(f32[16,1024]{1,0:T(8,128)} %param.15) | copy-start | bytes 196612
  16.1 5.2 %copy-start.22 = (f32[16,1024]{1,0:T(8,128)S(1)}, f32[16,1024]{1,0:T(8,128)}, u32[]{:S(2)}) copy-start(f32[16,1024]{1,0:T(8,128)} %param.16) | copy-start | bytes 196612
  21.3 1.7 copy-start.9
  39.4 27.3 %all-to-all-start.1 = ((bf16[16,48,1024]{2,1,0:T(8,128)(2,1)}), bf16[16,48,1024]{2,1,0:T(8,128)(2,1)}, u32[]{:S(2)}, u32[]{:S(2)}) async-start(bf16[16,48,1024]{2,1,0:T(8,128)(2,1)} %bitcast.29), calls=%async_computation.1 | async-start | bytes 3145728 | tf_op jit(solution)/shard_map/all_to_all | solution.py:571
  46.0 5.2 %copy-start.5 = (bf16[512,256]{1,0:T(8,128)(2,1)S(1)}, bf16[512,256]{1,0:T(8,128)(2,1)}, u32[]{:S(2)}) copy-start(bf16[512,256]{1,0:T(8,128)(2,1)} %constant.117.clone.fwd_ref) | copy-start | bytes 786436
  46.0 5.2 %copy-start.16 = (bf16[256,256]{1,0:T(8,128)(2,1)S(1)}, bf16[256,256]{1,0:T(8,128)(2,1)}, u32[]{:S(2)}) copy-start(bf16[256,256]{1,0:T(8,128)(2,1)} %constant.118.clone.inv_ref) | copy-start | bytes 393220
  47.4 19.3 %copy-start.6 = (bf16[512,256]{1,0:T(8,128)(2,1)S(1)}, bf16[512,256]{1,0:T(8,128)(2,1)}, u32[]{:S(2)}) copy-start(bf16[512,256]{1,0:T(8,128)(2,1)} %constant.117.clone.fwd_ref) | copy-start | bytes 786436
  47.4 19.2 %collective-permute-start = (bf16[128,1024]{1,0:T(8,128)(2,1)S(1)}, bf16[128,1024]{1,0:T(8,128)(2,1)S(1)}, u32[]{:S(2)}, u32[]{:S(2)}) collective-permute-start(bf16[128,1024]{1,0:T(8,128)(2,1)S(1)} %slice.4), channel_id=1, source_target_pairs={{0,8},{8,16},{16,24},{24,32},{32,40},{40,48},{48,56},{56,64},{64,7... | collective-permute-start | bytes 786440 | tf_op jit(solution)/shard_map/ppermute | solution.py:624
  73.3 8.1 %collective-permute-start.1 = (bf16[512,1024]{1,0:T(8,128)(2,1)S(1)}, bf16[512,1024]{1,0:T(8,128)(2,1)S(1)}, u32[]{:S(2)}, u32[]{:S(2)}) collective-permute-start(bf16[512,1024]{1,0:T(8,128)(2,1)S(1)} %gate.1.own_ref), channel_id=1, source_target_pairs={{0,1},{1,0},{2,3},{3,2},{4,5},{5,4},{6,7},{7,6},{8,9},{9,8},{10,11... | collective-permute-start | bytes 3145736 | tf_op jit(solution)/shard_map/ppermute | solution.py:563
  73.4 7.4 %copy-start.23 = (s32[8]{0:T(128)S(1)}, s32[8]{0:T(128)}, u32[]{:S(2)}) copy-start(s32[8]{0:T(128)} %param.12) | copy-start | bytes 100
  73.4 32.5 %all-to-all-start.2 = ((bf16[16,48,1024]{2,1,0:T(8,128)(2,1)}), bf16[16,48,1024]{2,1,0:T(8,128)(2,1)}, u32[]{:S(2)}, u32[]{:S(2)}) async-start(bf16[16,48,1024]{2,1,0:T(8,128)(2,1)} %bitcast.28), calls=%async_computation.2 | async-start | bytes 3145728 | tf_op jit(solution)/shard_map/all_to_all | solution.py:571
  86.8 19.1 %collective-permute-start.3 = (bf16[256,1024]{1,0:T(8,128)(2,1)}, bf16[256,1024]{1,0:T(8,128)(2,1)S(1)}, u32[]{:S(2)}, u32[]{:S(2)}) collective-permute-start(bf16[256,1024]{1,0:T(8,128)(2,1)} %get-tuple-element.53), channel_id=1, source_target_pairs={{0,2},{1,3},{2,4},{3,5},{4,6},{5,7},{6,0},{7,1},{8,10},{9,11},{10,... | collective-permute-start | bytes 1572872 | tf_op jit(solution)/shard_map/ppermute | solution.py:563
  88.2 17.6 %collective-permute-start.4 = (bf16[256,1024]{1,0:T(8,128)(2,1)}, bf16[256,1024]{1,0:T(8,128)(2,1)S(1)}, u32[]{:S(2)}, u32[]{:S(2)}) collective-permute-start(bf16[256,1024]{1,0:T(8,128)(2,1)} %get-tuple-element.54), channel_id=1, source_target_pairs={{0,6},{1,7},{2,0},{3,1},{4,2},{5,3},{6,4},{7,5},{8,14},{9,15},{10,... | collective-permute-start | bytes 1572872 | tf_op jit(solution)/shard_map/ppermute | solution.py:563
  96.2 20.9 %collective-permute-start.6 = (bf16[256,1024]{1,0:T(8,128)(2,1)}, bf16[256,1024]{1,0:T(8,128)(2,1)}, u32[]{:S(2)}, u32[]{:S(2)}) collective-permute-start(bf16[256,1024]{1,0:T(8,128)(2,1)} %get-tuple-element.63), channel_id=1, source_target_pairs={{0,6},{1,7},{2,0},{3,1},{4,2},{5,3},{6,4},{7,5},{8,14},{9,15},{10,... | collective-permute-start | bytes 1572872 | tf_op jit(solution)/shard_map/ppermute | solution.py:563
  97.8 19.3 %collective-permute-start.7 = (bf16[256,1024]{1,0:T(8,128)(2,1)}, bf16[256,1024]{1,0:T(8,128)(2,1)}, u32[]{:S(2)}, u32[]{:S(2)}) collective-permute-start(bf16[256,1024]{1,0:T(8,128)(2,1)} %get-tuple-element.64), channel_id=1, source_target_pairs={{0,2},{1,3},{2,4},{3,5},{4,6},{5,7},{6,0},{7,1},{8,10},{9,11},{10,... | collective-permute-start | bytes 1572872 | tf_op jit(solution)/shard_map/ppermute | solution.py:563
  105.9 8.9 %copy-start.15 = (bf16[512,768]{1,0:T(8,128)(2,1)S(1)}, bf16[512,768]{1,0:T(8,128)(2,1)}, u32[]{:S(2)}) copy-start(bf16[512,768]{1,0:T(8,128)(2,1)} %copy-done.14) | copy-start | bytes 2359300
  111.3 14.1 %collective-permute-start.5 = (bf16[256,1024]{1,0:T(8,128)(2,1)S(1)}, bf16[256,1024]{1,0:T(8,128)(2,1)S(1)}, u32[]{:S(2)}, u32[]{:S(2)}) collective-permute-start(bf16[256,1024]{1,0:T(8,128)(2,1)S(1)} %get-tuple-element.62), channel_id=1, source_target_pairs={{0,2},{1,3},{2,4},{3,5},{4,6},{5,7},{6,0},{7,1},{8,10},{9,11},{10,... | collective-permute-start | bytes 1572872 | tf_op jit(solution)/shard_map/ppermute | solution.py:563
  112.9 12.5 %collective-permute-start.8 = (bf16[256,1024]{1,0:T(8,128)(2,1)S(1)}, bf16[256,1024]{1,0:T(8,128)(2,1)S(1)}, u32[]{:S(2)}, u32[]{:S(2)}) collective-permute-start(bf16[256,1024]{1,0:T(8,128)(2,1)S(1)} %get-tuple-element.65), channel_id=1, source_target_pairs={{0,6},{1,7},{2,0},{3,1},{4,2},{5,3},{6,4},{7,5},{8,14},{9,15},{10,... | collective-permute-start | bytes 1572872 | tf_op jit(solution)/shard_map/ppermute | solution.py:563
  131.9 16.8 %all-to-all-start.3 = ((bf16[16,16,1024]{2,1,0:T(8,128)(2,1)}), bf16[16,16,1024]{2,1,0:T(8,128)(2,1)S(1)}, u32[]{:S(2)}, u32[]{:S(2)}) async-start(bf16[16,16,1024]{2,1,0:T(8,128)(2,1)} %bitcast.17), calls=%async_computation.3 | async-start | bytes 1048576 | tf_op jit(solution)/shard_map/all_to_all | solution.py:571
  138.3 1.6 copy-start.7
  155.2 26.5 %copy-start.11 = (bf16[512,768]{1,0:T(8,128)(2,1)S(1)}, bf16[512,768]{1,0:T(8,128)(2,1)}, u32[]{:S(2)}) copy-start(bf16[512,768]{1,0:T(8,128)(2,1)} %copy-done.10) | copy-start | bytes 2359300
  (13 other events, 14.4 us)

commit v3 on v2

--- a/solution.py
+++ b/solution.py
@@ -75,7 +75,7 @@
     return jnp.where(within < held, before + within, -1.0).astype(i32)
 
 
-def pack_product(planes, route, first, second, slot_count, peers, tile=256):
+def pack_product(planes, route, first, second, slot_count, peers, tile=512):
     _, rows, channels = planes.shape
     slots = peers * slot_count
 
@@ -404,9 +404,9 @@
     blocks = tile // 128
 
     def body(table_ref, own_ref, a0_ref, a1_ref, b0_ref, b1_ref, k_ref, last_ref, coef_ref, u_ref, seg_ref, end_ref):
-        top = own_ref[:half] + a0_ref[...].astype(f32) + a1_ref[...].astype(f32)
+        top = own_ref[:half].astype(f32) + a0_ref[...].astype(f32) + a1_ref[...].astype(f32)
         top = top * k_ref[:half].astype(f32)
-        bottom = own_ref[half:] + b0_ref[...].astype(f32) + b1_ref[...].astype(f32)
+        bottom = own_ref[half:].astype(f32) + b0_ref[...].astype(f32) + b1_ref[...].astype(f32)
         bottom = bottom * k_ref[half:].astype(f32)
         for cb in range(blocks):
             lanes = slice(cb * 128, (cb + 1) * 128)
@@ -505,7 +505,7 @@
     )(table, segs, u, keep, coef)
 
 
-def carry_in(table, ends, li, unbroken, coef, back, peers, step_blocks=2):
+def carry_in(table, ends, li, unbroken, coef, back, peers, step_blocks=4):
     count, rows, _ = li.shape
     slots = back.shape[0]
     tile = step_blocks * 128
@@ -634,11 +634,11 @@
     up_b, down_a = mm([(1, half, (half,), None, bf16), (3, 0, (half,), None, bf16)], blocks, other=other)
     up_b, down_a, blocks = together(up_b, down_a, blocks)
     from_low_b, from_high_a = along_x(up_b, 1), along_x(down_a, -1)
-    [mine] = mm([(0, 0, (rows,), None, f32)], blocks, other=other)
-    got_k, pass_a, pass_b, mine = together(got_k, pass_a, pass_b, mine)
+    up_a, down_b = mm([(1, 0, (half,), pass_a, bf16), (3, half, (half,), pass_b, bf16)], blocks, other=other)
+    up_a, down_b, blocks, got_k = together(up_a, down_b, blocks, got_k)
+    from_low_a, from_high_b = along_x(up_a, 1), along_x(down_b, -1)
+    [mine] = mm([(0, 0, (rows,), None, bf16)], blocks, other=other)
     k_li = unpack(got_k, to_steps)
-    up_a, down_b = mm([(1, 0, (half,), pass_a, bf16), (3, half, (half,), pass_b, bf16)], blocks, other=other)
-    from_low_a, from_high_b = along_x(up_a, 1), along_x(down_b, -1)
     u, segs, end = end_states(
         table, mine, [from_low_a, from_high_a, from_low_b, from_high_b], k_li, last, coef, peers
     )

time: 186 us -> 182 us (0.978)
    all_to_all x4, waiting for transfers between devices: 30.1 us -> 28.2 us  [swap(): return lax.all_to_all(shard, 'ctx', split_axis=0, concat_axis=0, tiled=True)]
    unnamed x48 -> x50, local copies, waits for them, and re-layouts: 12.8 us -> 13.1 us
  transfers between devices with their start and end apart: 13 -> 13, of which waited for: 5 -> 6; matrix products, arithmetic and copies ran while one was open for 1% -> 1% of each run, Pallas kernels for 25% -> 26%
where the time goes in v3:
time: 182 us; the launch traced here: 181 us
  Pallas kernels  65 us (36%)
  starting transfers between devices  39.2 us (22%)
  waiting for transfers between devices  36.8 us (20%)
  blocking collectives  25.3 us (14%)
  local copies, waits for them, and re-layouts  13.5 us (7%)
    all_to_all x4, waiting for transfers between devices, swap(): return lax.all_to_all(shard, 'ctx', split_axis=0, concat_axis=0, tiled=True)  28.2 us
    all_to_all x4, starting transfers between devices, swap(): return lax.all_to_all(shard, 'ctx', split_axis=0, concat_axis=0, tiled=True)  26.8 us
    all_to_all x1, blocking collectives, swap(): return lax.all_to_all(shard, 'ctx', split_axis=0, concat_axis=0, tiled=True)  25.3 us
    pallas_call x4, Pallas kernels, project(): pl.pallas_call(body, grid_spec=pltpu.PrefetchScalarGridSpec(num_scalar_pr...  21.8 us
    unnamed x50, local copies, waits for them, and re-layouts  13.1 us
    ppermute x8, starting transfers between devices, along_x(): return lax.ppermute(shard, 'tp', pairs)  8.59 us
    ppermute x8, waiting for transfers between devices, along_x(): return lax.ppermute(shard, 'tp', pairs)  8.54 us
    pallas_call x1, Pallas kernels, recur(): pl.pallas_call(body, grid_spec=pltpu.PrefetchScalarGridSpec(num_scalar_pr...  6.52 us
  transfers between devices with their start and end apart: 13, of which 6 were waited for; matrix products, arithmetic and copies ran while one was open for 1% of the time, Pallas kernels for 26%

profile of v3, /device:TPU:0, one launch (start us, length us, event | category | flops | bytes accessed | tf_op | source)
XLA Modules:
  0.0 181.2 jit_solution(439239896448911299)
XLA Ops:
  0.7 4.1 %pack_kv.1 = bf16[768,1024]{1,0:T(8,128)(2,1)} custom-call(s32[1,512]{1,0:T(1,128)S(1)} %bitcast.30, bf16[5,512,1024]{2,1,0:T(8,128)(2,1)} %bitcast.32, bf16[5,512,1024]{2,1,0:T(8,128)(2,1)} %bitcast.33), custom_call_target="tpu_custom_call" | custom-call | flops 80530640 | bytes 367001 | tf_op jit(solution)/shard_map/pack_kv/pallas_call | solution.py:92
  4.8 8.3 %all-to-all-start = ((bf16[16,48,1024]{2,1,0:T(8,128)(2,1)}), bf16[16,48,1024]{2,1,0:T(8,128)(2,1)S(1)}, u32[]{:S(2)}, u32[]{:S(2)}) async-start(bf16[16,48,1024]{2,1,0:T(8,128)(2,1)} %bitcast.7), calls=%async_computation | async-start | bytes 3145728 | tf_op jit(solution)/shard_map/all_to_all | solution.py:571
  15.0 4.3 %pack_two.1 = (bf16[768,1024]{1,0:T(8,128)(2,1)S(1)}, bf16[768,1024]{1,0:T(8,128)(2,1)S(1)}, bf16[512,768]{1,0:T(8,128)(2,1)S(1)}) custom-call(s32[1,512]{1,0:T(1,128)S(1)} %bitcast.31, bf16[5,512,1024]{2,1,0:T(8,128)(2,1)} %bitcast.34, bf16[5,512,1024]{2,1,0:T(8,128)(2,1)} %bitcast.35), custom_call_target="tpu_custom_call" | custom-call | flops 161061280 | bytes 524288 | tf_op jit(solution)/shard_map/pack_two/pallas_call | solution.py:120
  22.0 16.4 %all-to-all-done = bf16[16,48,1024]{2,1,0:T(8,128)(2,1)S(1)} async-done(((bf16[16,48,1024]{2,1,0:T(8,128)(2,1)}), bf16[16,48,1024]{2,1,0:T(8,128)(2,1)S(1)}, u32[]{:S(2)}, u32[]{:S(2)}) %all-to-all-start) | async-done | bytes 1572896 | tf_op jit(solution)/shard_map/all_to_all | solution.py:571
  38.4 4.4 %all-to-all-start.1 = ((bf16[16,48,1024]{2,1,0:T(8,128)(2,1)}), bf16[16,48,1024]{2,1,0:T(8,128)(2,1)}, u32[]{:S(2)}, u32[]{:S(2)}) async-start(bf16[16,48,1024]{2,1,0:T(8,128)(2,1)} %bitcast.29), calls=%async_computation.1 | async-start | bytes 3145728 | tf_op jit(solution)/shard_map/all_to_all | solution.py:571
  46.4 3.8 %collective-permute-start = (bf16[128,1024]{1,0:T(8,128)(2,1)S(1)}, bf16[128,1024]{1,0:T(8,128)(2,1)S(1)}, u32[]{:S(2)}, u32[]{:S(2)}) collective-permute-start(bf16[128,1024]{1,0:T(8,128)(2,1)S(1)} %slice.4), channel_id=1, source_target_pairs={{0,8},{8,16},{16,24},{24,32},{32,40},{40,48},{48,56},{56,64},{64,7... | collective-permute-start | bytes 786440 | tf_op jit(solution)/shard_map/ppermute | solution.py:624
  50.2 4.0 %taps.1.filt_ref = f32[512,1024]{1,0:T(8,128)S(1)} custom-call(bf16[512,1024]{1,0:T(8,128)(2,1)S(1)} %unpack.2.u_ref, f32[3,128,1024]{2,1,0:T(8,128)S(1)} %spectrum.1.h_ref, bf16[512,256]{1,0:T(8,128)(2,1)S(1)} %copy-done.4, bf16[256,256]{1,0:T(8,128)(2,1)S(1)} %copy-done.15), custom_call_target="tpu_custom_call" | custom-call | flops 93952408 | bytes 419430 | tf_op jit(solution)/shard_map/taps/pallas_call | solution.py:293
  55.6 10.0 %all-to-all-done.1 = bf16[16,48,1024]{2,1,0:T(8,128)(2,1)} async-done(((bf16[16,48,1024]{2,1,0:T(8,128)(2,1)}), bf16[16,48,1024]{2,1,0:T(8,128)(2,1)}, u32[]{:S(2)}, u32[]{:S(2)}) %all-to-all-start.1) | async-done | bytes 1572896 | tf_op jit(solution)/shard_map/all_to_all | solution.py:571
  67.8 4.4 %gate.1.own_ref = bf16[512,1024]{1,0:T(8,128)(2,1)S(1)} custom-call(bf16[512,768]{1,0:T(8,128)(2,1)S(1)} %copy-done.2, bf16[768,1024]{1,0:T(8,128)(2,1)} %bitcast.14.in_ref, f32[512,1024]{1,0:T(8,128)} %copy-done, bf16[128,1024]{1,0:T(8,128)(2,1)S(1)} %collective-permute-done.rim_ref, f32[3,128,1024]{2,1,0:T(8,128)S(1)} %spectrum.1.h_ref, ...), custom_call_target="tpu_custom_call" | custom-call | flops 80530640 | bytes 471859 | tf_op jit(solution)/shard_map/gate/pallas_call | solution.py:317
  72.3 7.3 %all-to-all-start.2 = ((bf16[16,48,1024]{2,1,0:T(8,128)(2,1)}), bf16[16,48,1024]{2,1,0:T(8,128)(2,1)}, u32[]{:S(2)}, u32[]{:S(2)}) async-start(bf16[16,48,1024]{2,1,0:T(8,128)(2,1)} %bitcast.28), calls=%async_computation.2 | async-start | bytes 3145728 | tf_op jit(solution)/shard_map/all_to_all | solution.py:571
  80.0 5.4 %project.4 = (bf16[256,1024]{1,0:T(8,128)(2,1)}, bf16[256,1024]{1,0:T(8,128)(2,1)}) custom-call(s32[4]{0:T(128)S(1)} %pad_add_fusion.1.blocks_ref, bf16[512,1024]{1,0:T(8,128)(2,1)S(1)} %gate.1.own_ref, bf16[512,1024]{1,0:T(8,128)(2,1)S(1)} %collective-permute-done.1.other_ref, bf16[1024,8192]{1,0:T(8,128)(2,1)} %rest_0_.7, ...), custom_call_target="tpu_custom_call" | custom-call | flops 214748368 | bytes 838860 | tf_op jit(solution)/shard_map/project/pallas_call | solution.py:370
  89.0 6.1 %project.5 = (bf16[256,1024]{1,0:T(8,128)(2,1)}, bf16[256,1024]{1,0:T(8,128)(2,1)}) custom-call(s32[4]{0:T(128)S(1)} %pad_add_fusion.1.blocks_ref, bf16[512,1024]{1,0:T(8,128)(2,1)S(1)} %gate.1.own_ref, bf16[512,1024]{1,0:T(8,128)(2,1)S(1)} %collective-permute-done.1.other_ref, bf16[1024,8192]{1,0:T(8,128)(2,1)} %rest_0_.7, ...), custom_call_target="tpu_custom_call" | custom-call | flops 214748368 | bytes 1258291 | tf_op jit(solution)/shard_map/project/pallas_call | solution.py:370
  97.1 4.6 %collective-permute-done.3.rest_4_ = bf16[256,1024]{1,0:T(8,128)(2,1)} collective-permute-done((bf16[256,1024]{1,0:T(8,128)(2,1)}, bf16[256,1024]{1,0:T(8,128)(2,1)}, u32[]{:S(2)}, u32[]{:S(2)}) %collective-permute-start.3) | collective-permute-done | bytes 524320 | tf_op jit(solution)/shard_map/ppermute | solution.py:563
  102.0 5.6 %project.6 = (bf16[256,1024]{1,0:T(8,128)(2,1)S(1)}, bf16[256,1024]{1,0:T(8,128)(2,1)S(1)}) custom-call(s32[4]{0:T(128)S(1)} %pad_add_fusion.1.blocks_ref, bf16[512,1024]{1,0:T(8,128)(2,1)S(1)} %gate.1.own_ref, bf16[512,1024]{1,0:T(8,128)(2,1)S(1)} %collective-permute-done.1.other_ref, bf16[1024,8192]{1,0:T(8,128)(2,1)} %rest_0_.7, ...), custom_call_target="tpu_custom_call" | custom-call | flops 214748368 | bytes 1258291 | tf_op jit(solution)/shard_map/project/pallas_call | solution.py:370
  112.8 2.4 %unpack.3.k_ref = bf16[512,1024]{1,0:T(8,128)(2,1)S(1)} custom-call(bf16[512,768]{1,0:T(8,128)(2,1)S(1)} %copy-done.14, bf16[768,1024]{1,0:T(8,128)(2,1)} %bitcast.16.in_ref), custom_call_target="tpu_custom_call" | custom-call | flops 80530640 | bytes 262144 | tf_op jit(solution)/shard_map/unpack/pallas_call | solution.py:175
  115.1 4.7 %project.7.own_ref = bf16[512,1024]{1,0:T(8,128)(2,1)S(1)} custom-call(s32[4]{0:T(128)S(1)} %pad_add_fusion.1.blocks_ref, bf16[512,1024]{1,0:T(8,128)(2,1)S(1)} %gate.1.own_ref, bf16[512,1024]{1,0:T(8,128)(2,1)S(1)} %collective-permute-done.1.other_ref, bf16[1024,8192]{1,0:T(8,128)(2,1)} %rest_0_.7, bf16[1024,8192]{1,0:T(8,128)(2,1)} %collective-permute-done.2.rest_1_.rest_3_), custom_call_target="tpu_custom_call" | custom-call | flops 214748368 | bytes 838860 | tf_op jit(solution)/shard_map/project/pallas_call | solution.py:370
  119.9 3.6 %collective-permute-done.5.a0_ref = bf16[256,1024]{1,0:T(8,128)(2,1)S(1)} collective-permute-done((bf16[256,1024]{1,0:T(8,128)(2,1)}, bf16[256,1024]{1,0:T(8,128)(2,1)S(1)}, u32[]{:S(2)}, u32[]{:S(2)}) %collective-permute-start.5) | collective-permute-done | bytes 524320 | tf_op jit(solution)/shard_map/ppermute | solution.py:563
  123.6 6.2 %ends.1 = (f32[8,512,128]{2,1,0:T(8,128)}, f32[8,128,128]{2,1,0:T(8,128)S(1)}, bf16[256,1024]{1,0:T(8,128)(2,1)}) custom-call(s32[25]{0:T(128)S(1)} %pad_add_fusion.table_ref, bf16[512,1024]{1,0:T(8,128)(2,1)S(1)} %project.7.own_ref, bf16[256,1024]{1,0:T(8,128)(2,1)S(1)} %collective-permute-done.5.a0_ref, bf16[256,1024]{1,0:T(8,128)(2,1)} %collective-permute-done.6.a1_ref, ...), custom_call_target="tpu_custom_call" | custom-call | flops 400000000 | bytes 629145 | tf_op jit(solution)/shard_map/ends/pallas_call | solution.py:433
  129.8 6.8 %all-to-all-start.3 = ((bf16[16,16,1024]{2,1,0:T(8,128)(2,1)}), bf16[16,16,1024]{2,1,0:T(8,128)(2,1)S(1)}, u32[]{:S(2)}, u32[]{:S(2)}) async-start(bf16[16,16,1024]{2,1,0:T(8,128)(2,1)} %bitcast.17), calls=%async_computation.3 | async-start | bytes 1048576 | tf_op jit(solution)/shard_map/all_to_all | solution.py:571
  138.4 6.5 %recur.1.li_ref = f32[8,512,128]{2,1,0:T(8,128)S(1)} custom-call(s32[25]{0:T(128)S(1)} %pad_add_fusion.table_ref, f32[8,128,128]{2,1,0:T(8,128)S(1)} %get-tuple-element.70.seg_ref, f32[8,512,128]{2,1,0:T(8,128)S(1)} %copy-done.6, f32[512,128]{1,0:T(8,128)S(1)} %broadcast_in_dim.35.keep_ref, f32[4,16,1024]{2,1,0:T(8,128)S(1)} %pad_maximum_fusion.coef_ref), custom_call_target="tpu_custom_call" | custom-call | flops 800000000 | bytes 419430 | tf_op jit(solution)/shard_map/recur/pallas_call | solution.py:487
  144.9 1.8 all-to-all-done.3.ends_ref
  148.0 4.8 %carry.1 = bf16[768,1024]{1,0:T(8,128)(2,1)S(1)} custom-call(s32[25]{0:T(128)S(1)} %pad_add_fusion.table_ref, bf16[16,16,1024]{2,1,0:T(8,128)(2,1)S(1)} %all-to-all-done.3.ends_ref, f32[8,512,128]{2,1,0:T(8,128)S(1)} %recur.1.li_ref, f32[512,128]{1,0:T(8,128)S(1)} %broadcast_in_dim.36.unbroken_ref, f32[4,16,1024]{2,1,0:T(8,128)S(1)} %pad_maximum_fusion.coef_ref, ...), custom_call_target="tpu_custom_call" | custom-call | flops 400000000 | bytes 419430 | tf_op jit(solution)/shard_map/carry/pallas_call | solution.py:536
  152.8 25.3 %all_to_all.56 = bf16[16,48,1024]{2,1,0:T(8,128)(2,1)S(1)} all-to-all(bf16[16,48,1024]{2,1,0:T(8,128)(2,1)S(1)} %bitcast.26), channel_id=1, replica_groups=mesh['ctx'=16,'tp'=8] {'ctx'}, dimensions={0} | all-to-all | bytes 3145728 | tf_op jit(solution)/shard_map/all_to_all | solution.py:571
  178.1 3.0 %finish.1 = bf16[512,1024]{1,0:T(8,128)(2,1)} custom-call(bf16[512,768]{1,0:T(8,128)(2,1)S(1)} %copy-done.10, bf16[5,512,1024]{2,1,0:T(8,128)(2,1)} %bitcast.36, bf16[768,1024]{1,0:T(8,128)(2,1)S(1)} %bitcast.27), custom_call_target="tpu_custom_call" | custom-call | flops 80530640 | bytes 367001 | tf_op jit(solution)/shard_map/finish/pallas_call | solution.py:194
  (92 shorter events, 26.7 us)
Async XLA Ops:
  4.8 75.2 %collective-permute-start.2 = (bf16[1024,8192]{1,0:T(8,128)(2,1)}, bf16[1024,8192]{1,0:T(8,128)(2,1)}, u32[]{:S(2)}, u32[]{:S(2)}) collective-permute-start(bf16[1024,8192]{1,0:T(8,128)(2,1)} %rest_0_.7), channel_id=1, source_target_pairs={{0,1},{1,0},{2,3},{3,2},{4,5},{5,4},{6,7},{7,6},{8,9},{9,8},{10,11... | collective-permute-start | bytes 50331656 | tf_op jit(solution)/shard_map/ppermute | solution.py:563
  4.8 8.3 %copy-start.3 = (bf16[512,256]{1,0:T(8,128)(2,1)S(1)}, bf16[512,256]{1,0:T(8,128)(2,1)}, u32[]{:S(2)}) copy-start(bf16[512,256]{1,0:T(8,128)(2,1)} %constant.117.clone.fwd_ref) | copy-start | bytes 786436
  4.8 33.6 %all-to-all-start = ((bf16[16,48,1024]{2,1,0:T(8,128)(2,1)}), bf16[16,48,1024]{2,1,0:T(8,128)(2,1)S(1)}, u32[]{:S(2)}, u32[]{:S(2)}) async-start(bf16[16,48,1024]{2,1,0:T(8,128)(2,1)} %bitcast.7), calls=%async_computation | async-start | bytes 3145728 | tf_op jit(solution)/shard_map/all_to_all | solution.py:571
  15.0 5.2 %copy-start.22 = (f32[16,1024]{1,0:T(8,128)S(1)}, f32[16,1024]{1,0:T(8,128)}, u32[]{:S(2)}) copy-start(f32[16,1024]{1,0:T(8,128)} %param.15) | copy-start | bytes 196612
  15.0 5.2 %copy-start.23 = (f32[16,1024]{1,0:T(8,128)S(1)}, f32[16,1024]{1,0:T(8,128)}, u32[]{:S(2)}) copy-start(f32[16,1024]{1,0:T(8,128)} %param.16) | copy-start | bytes 196612
  20.2 1.7 copy-start.8
  38.4 27.2 %all-to-all-start.1 = ((bf16[16,48,1024]{2,1,0:T(8,128)(2,1)}), bf16[16,48,1024]{2,1,0:T(8,128)(2,1)}, u32[]{:S(2)}, u32[]{:S(2)}) async-start(bf16[16,48,1024]{2,1,0:T(8,128)(2,1)} %bitcast.29), calls=%async_computation.1 | async-start | bytes 3145728 | tf_op jit(solution)/shard_map/all_to_all | solution.py:571
  45.0 5.2 %copy-start.4 = (bf16[512,256]{1,0:T(8,128)(2,1)S(1)}, bf16[512,256]{1,0:T(8,128)(2,1)}, u32[]{:S(2)}) copy-start(bf16[512,256]{1,0:T(8,128)(2,1)} %constant.117.clone.fwd_ref) | copy-start | bytes 786436
  45.0 5.2 %copy-start.15 = (bf16[256,256]{1,0:T(8,128)(2,1)S(1)}, bf16[256,256]{1,0:T(8,128)(2,1)}, u32[]{:S(2)}) copy-start(bf16[256,256]{1,0:T(8,128)(2,1)} %constant.118.clone.inv_ref) | copy-start | bytes 393220
  46.4 19.2 %copy-start.5 = (bf16[512,256]{1,0:T(8,128)(2,1)S(1)}, bf16[512,256]{1,0:T(8,128)(2,1)}, u32[]{:S(2)}) copy-start(bf16[512,256]{1,0:T(8,128)(2,1)} %constant.117.clone.fwd_ref) | copy-start | bytes 786436
  46.4 19.2 %collective-permute-start = (bf16[128,1024]{1,0:T(8,128)(2,1)S(1)}, bf16[128,1024]{1,0:T(8,128)(2,1)S(1)}, u32[]{:S(2)}, u32[]{:S(2)}) collective-permute-start(bf16[128,1024]{1,0:T(8,128)(2,1)S(1)} %slice.4), channel_id=1, source_target_pairs={{0,8},{8,16},{16,24},{24,32},{32,40},{40,48},{48,56},{56,64},{64,7... | collective-permute-start | bytes 786440 | tf_op jit(solution)/shard_map/ppermute | solution.py:624
  72.2 7.7 %collective-permute-start.1 = (bf16[512,1024]{1,0:T(8,128)(2,1)S(1)}, bf16[512,1024]{1,0:T(8,128)(2,1)S(1)}, u32[]{:S(2)}, u32[]{:S(2)}) collective-permute-start(bf16[512,1024]{1,0:T(8,128)(2,1)S(1)} %gate.1.own_ref), channel_id=1, source_target_pairs={{0,1},{1,0},{2,3},{3,2},{4,5},{5,4},{6,7},{7,6},{8,9},{9,8},{10,11... | collective-permute-start | bytes 3145736 | tf_op jit(solution)/shard_map/ppermute | solution.py:563
  72.3 7.5 %copy-start.24 = (s32[8]{0:T(128)S(1)}, s32[8]{0:T(128)}, u32[]{:S(2)}) copy-start(s32[8]{0:T(128)} %param.12) | copy-start | bytes 100
  72.3 36.9 %all-to-all-start.2 = ((bf16[16,48,1024]{2,1,0:T(8,128)(2,1)}), bf16[16,48,1024]{2,1,0:T(8,128)(2,1)}, u32[]{:S(2)}, u32[]{:S(2)}) async-start(bf16[16,48,1024]{2,1,0:T(8,128)(2,1)} %bitcast.28), calls=%async_computation.2 | async-start | bytes 3145728 | tf_op jit(solution)/shard_map/all_to_all | solution.py:571
  85.4 16.3 %collective-permute-start.3 = (bf16[256,1024]{1,0:T(8,128)(2,1)}, bf16[256,1024]{1,0:T(8,128)(2,1)}, u32[]{:S(2)}, u32[]{:S(2)}) collective-permute-start(bf16[256,1024]{1,0:T(8,128)(2,1)} %get-tuple-element.56), channel_id=1, source_target_pairs={{0,2},{1,3},{2,4},{3,5},{4,6},{5,7},{6,0},{7,1},{8,10},{9,11},{10,... | collective-permute-start | bytes 1572872 | tf_op jit(solution)/shard_map/ppermute | solution.py:563
  86.9 15.1 %collective-permute-start.4 = (bf16[256,1024]{1,0:T(8,128)(2,1)}, bf16[256,1024]{1,0:T(8,128)(2,1)}, u32[]{:S(2)}, u32[]{:S(2)}) collective-permute-start(bf16[256,1024]{1,0:T(8,128)(2,1)} %get-tuple-element.57), channel_id=1, source_target_pairs={{0,6},{1,7},{2,0},{3,1},{4,2},{5,3},{6,4},{7,5},{8,14},{9,15},{10,... | collective-permute-start | bytes 1572872 | tf_op jit(solution)/shard_map/ppermute | solution.py:563
  95.1 17.7 %copy-start.14 = (bf16[512,768]{1,0:T(8,128)(2,1)S(1)}, bf16[512,768]{1,0:T(8,128)(2,1)}, u32[]{:S(2)}) copy-start(bf16[512,768]{1,0:T(8,128)(2,1)} %copy-done.13) | copy-start | bytes 2359300
  95.1 24.8 %collective-permute-start.6 = (bf16[256,1024]{1,0:T(8,128)(2,1)}, bf16[256,1024]{1,0:T(8,128)(2,1)}, u32[]{:S(2)}, u32[]{:S(2)}) collective-permute-start(bf16[256,1024]{1,0:T(8,128)(2,1)} %get-tuple-element.63), channel_id=1, source_target_pairs={{0,6},{1,7},{2,0},{3,1},{4,2},{5,3},{6,4},{7,5},{8,14},{9,15},{10,... | collective-permute-start | bytes 1572872 | tf_op jit(solution)/shard_map/ppermute | solution.py:563
  96.6 23.3 %collective-permute-start.7 = (bf16[256,1024]{1,0:T(8,128)(2,1)}, bf16[256,1024]{1,0:T(8,128)(2,1)}, u32[]{:S(2)}, u32[]{:S(2)}) collective-permute-start(bf16[256,1024]{1,0:T(8,128)(2,1)} %get-tuple-element.64), channel_id=1, source_target_pairs={{0,2},{1,3},{2,4},{3,5},{4,6},{5,7},{6,0},{7,1},{8,10},{9,11},{10,... | collective-permute-start | bytes 1572872 | tf_op jit(solution)/shard_map/ppermute | solution.py:563
  109.2 14.2 %collective-permute-start.5 = (bf16[256,1024]{1,0:T(8,128)(2,1)}, bf16[256,1024]{1,0:T(8,128)(2,1)S(1)}, u32[]{:S(2)}, u32[]{:S(2)}) collective-permute-start(bf16[256,1024]{1,0:T(8,128)(2,1)} %copy-done.21), channel_id=1, source_target_pairs={{0,2},{1,3},{2,4},{3,5},{4,6},{5,7},{6,0},{7,1},{8,10},{9,11},{10,... | collective-permute-start | bytes 1572872 | tf_op jit(solution)/shard_map/ppermute | solution.py:563
  110.7 12.7 %collective-permute-start.8 = (bf16[256,1024]{1,0:T(8,128)(2,1)}, bf16[256,1024]{1,0:T(8,128)(2,1)S(1)}, u32[]{:S(2)}, u32[]{:S(2)}) collective-permute-start(bf16[256,1024]{1,0:T(8,128)(2,1)} %copy-done.20), channel_id=1, source_target_pairs={{0,6},{1,7},{2,0},{3,1},{4,2},{5,3},{6,4},{7,5},{8,14},{9,15},{10,... | collective-permute-start | bytes 1572872 | tf_op jit(solution)/shard_map/ppermute | solution.py:563
  129.8 16.9 %all-to-all-start.3 = ((bf16[16,16,1024]{2,1,0:T(8,128)(2,1)}), bf16[16,16,1024]{2,1,0:T(8,128)(2,1)S(1)}, u32[]{:S(2)}, u32[]{:S(2)}) async-start(bf16[16,16,1024]{2,1,0:T(8,128)(2,1)} %bitcast.17), calls=%async_computation.3 | async-start | bytes 1048576 | tf_op jit(solution)/shard_map/all_to_all | solution.py:571
  136.8 1.6 copy-start.6
  152.8 25.4 %copy-start.10 = (bf16[512,768]{1,0:T(8,128)(2,1)S(1)}, bf16[512,768]{1,0:T(8,128)(2,1)}, u32[]{:S(2)}) copy-start(bf16[512,768]{1,0:T(8,128)(2,1)} %copy-done.9) | copy-start | bytes 2359300
  (14 other events, 14.6 us)

commit v4 on v3

--- a/solution.py
+++ b/solution.py
@@ -36,6 +36,10 @@
 
 def cost(flops, nbytes):
     return pl.CostEstimate(flops=int(flops) // 10, bytes_accessed=int(nbytes) // 10, transcendentals=0)
+
+
+def in_hbm(x):
+    return pltpu.with_memory_space_constraint(x, pltpu.HBM)
 
 
 def whole(shape):
@@ -100,7 +104,7 @@
         compiler_params=params(),
         cost_estimate=cost(2 * slots * rows * channels, 2 * (2 * rows + slots) * channels),
         name="pack_kv",
-    )(route, planes, planes)
+    )(in_hbm(route), planes, planes)
 
 
 def pack_two(planes, route, first, second, slot_count, peers, tile=512):
@@ -132,7 +136,7 @@
         compiler_params=params(),
         cost_estimate=cost(4 * slots * rows * channels, 4 * (rows + slots) * channels),
         name="pack_two",
-    )(route, planes, planes)
+    )(in_hbm(route), planes, planes)
 
 
 def place_matrices(received, rows, slot_count, peers):
@@ -332,7 +336,7 @@
         compiler_params=params(),
         cost_estimate=cost(2 * slots * rows * channels, (6 * rows + 2 * slots) * channels),
         name="gate",
-    )(to_rows, received, filtered, rim, spectrum, forward, inverse, beside)
+    )(in_hbm(to_rows), in_hbm(received), filtered, rim, spectrum, forward, inverse, in_hbm(beside))
 
 
 def project(tasks, blocks, own, other, weight, other_weight, tile=512):
@@ -502,7 +506,7 @@
         compiler_params=params(),
         cost_estimate=cost(8e9, 8 * count * rows * 128),
         name="recur",
-    )(table, segs, u, keep, coef)
+    )(table, segs, in_hbm(u), keep, coef)
 
 
 def carry_in(table, ends, li, unbroken, coef, back, peers, step_blocks=4):
@@ -552,7 +556,7 @@
         compiler_params=params(),
         cost_estimate=cost(4e9, 8 * count * rows * 128),
         name="carry",
-    )(table, ends, li, unbroken, coef, back)
+    )(table, ends, li, unbroken, coef, in_hbm(back))
 
 
 def along_x(shard, dx, dcore=0):

time: 182 us -> 180 us (0.989)
  local copies, waits for them, and re-layouts: 13.5 us -> 9.59 us
  Pallas kernels: 65 us -> 67.2 us
    unnamed x50 -> x40, local copies, waits for them, and re-layouts: 13.1 us -> 9.12 us
  transfers between devices with their start and end apart: 13 -> 13, of which waited for: 6 -> 6; matrix products, arithmetic and copies ran while one was open for 1% -> 1% of each run, Pallas kernels for 26% -> 27%
where the time goes in v4:
time: 180 us; the launch traced here: 179 us
  Pallas kernels  67.2 us (37%)
  starting transfers between devices  39.2 us (22%)
  waiting for transfers between devices  37.3 us (21%)
  blocking collectives  24.7 us (14%)
  local copies, waits for them, and re-layouts  9.59 us (5%)
    all_to_all x4, waiting for transfers between devices, swap(): return lax.all_to_all(shard, 'ctx', split_axis=0, concat_axis=0, tiled=True)  28.8 us
    all_to_all x4, starting transfers between devices, swap(): return lax.all_to_all(shard, 'ctx', split_axis=0, concat_axis=0, tiled=True)  26.8 us
    all_to_all x1, blocking collectives, swap(): return lax.all_to_all(shard, 'ctx', split_axis=0, concat_axis=0, tiled=True)  24.7 us
    pallas_call x4, Pallas kernels, project(): pl.pallas_call(body, grid_spec=pltpu.PrefetchScalarGridSpec(num_scalar_pr...  21.8 us
    unnamed x40, local copies, waits for them, and re-layouts  9.12 us
    ppermute x8, starting transfers between devices, along_x(): return lax.ppermute(shard, 'tp', pairs)  8.59 us
    ppermute x8, waiting for transfers between devices, along_x(): return lax.ppermute(shard, 'tp', pairs)  8.51 us
    pallas_call x1, Pallas kernels, recur(): pl.pallas_call(body, grid_spec=pltpu.PrefetchScalarGridSpec(num_scalar_pr...  7.54 us
  transfers between devices with their start and end apart: 13, of which 6 were waited for; matrix products, arithmetic and copies ran while one was open for 1% of the time, Pallas kernels for 27%

profile of v4, /device:TPU:0, one launch (start us, length us, event | category | flops | bytes accessed | tf_op | source)
XLA Modules:
  0.0 179.2 jit_solution(2304752089106074228)
XLA Ops:
  0.0 4.1 %pack_kv.1 = bf16[768,1024]{1,0:T(8,128)(2,1)} custom-call(s32[1,512]{1,0:T(1,128)} %bitcast.35, bf16[5,512,1024]{2,1,0:T(8,128)(2,1)} %bitcast.30, bf16[5,512,1024]{2,1,0:T(8,128)(2,1)} %bitcast.31), custom_call_target="tpu_custom_call" | custom-call | flops 80530640 | bytes 367001 | tf_op jit(solution)/shard_map/pack_kv/pallas_call | solution.py:96
  4.1 8.3 %all-to-all-start = ((bf16[16,48,1024]{2,1,0:T(8,128)(2,1)}), bf16[16,48,1024]{2,1,0:T(8,128)(2,1)S(1)}, u32[]{:S(2)}, u32[]{:S(2)}) async-start(bf16[16,48,1024]{2,1,0:T(8,128)(2,1)} %bitcast.7), calls=%async_computation | async-start | bytes 3145728 | tf_op jit(solution)/shard_map/all_to_all | solution.py:575
  14.4 4.3 %pack_two.1 = (bf16[768,1024]{1,0:T(8,128)(2,1)S(1)}, bf16[768,1024]{1,0:T(8,128)(2,1)S(1)}, bf16[512,768]{1,0:T(8,128)(2,1)S(1)}) custom-call(s32[1,512]{1,0:T(1,128)} %bitcast.36, bf16[5,512,1024]{2,1,0:T(8,128)(2,1)} %bitcast.32, bf16[5,512,1024]{2,1,0:T(8,128)(2,1)} %bitcast.33), custom_call_target="tpu_custom_call" | custom-call | flops 161061280 | bytes 524288 | tf_op jit(solution)/shard_map/pack_two/pallas_call | solution.py:124
  21.3 16.4 %all-to-all-done = bf16[16,48,1024]{2,1,0:T(8,128)(2,1)S(1)} async-done(((bf16[16,48,1024]{2,1,0:T(8,128)(2,1)}), bf16[16,48,1024]{2,1,0:T(8,128)(2,1)S(1)}, u32[]{:S(2)}, u32[]{:S(2)}) %all-to-all-start) | async-done | bytes 1572896 | tf_op jit(solution)/shard_map/all_to_all | solution.py:575
  37.7 4.4 %all-to-all-start.1 = ((bf16[16,48,1024]{2,1,0:T(8,128)(2,1)}), bf16[16,48,1024]{2,1,0:T(8,128)(2,1)}, u32[]{:S(2)}, u32[]{:S(2)}) async-start(bf16[16,48,1024]{2,1,0:T(8,128)(2,1)} %bitcast.29), calls=%async_computation.1 | async-start | bytes 3145728 | tf_op jit(solution)/shard_map/all_to_all | solution.py:575
  45.8 3.8 %collective-permute-start = (bf16[128,1024]{1,0:T(8,128)(2,1)S(1)}, bf16[128,1024]{1,0:T(8,128)(2,1)S(1)}, u32[]{:S(2)}, u32[]{:S(2)}) collective-permute-start(bf16[128,1024]{1,0:T(8,128)(2,1)S(1)} %slice.4), channel_id=1, source_target_pairs={{0,8},{8,16},{16,24},{24,32},{32,40},{40,48},{48,56},{56,64},{64,7... | collective-permute-start | bytes 786440 | tf_op jit(solution)/shard_map/ppermute | solution.py:628
  49.6 4.0 %taps.1.filt_ref = f32[512,1024]{1,0:T(8,128)S(1)} custom-call(bf16[512,1024]{1,0:T(8,128)(2,1)S(1)} %unpack.2.u_ref, f32[3,128,1024]{2,1,0:T(8,128)S(1)} %spectrum.1.h_ref, bf16[512,256]{1,0:T(8,128)(2,1)S(1)} %copy-done.4, bf16[256,256]{1,0:T(8,128)(2,1)S(1)} %copy-done.13), custom_call_target="tpu_custom_call" | custom-call | flops 93952408 | bytes 419430 | tf_op jit(solution)/shard_map/taps/pallas_call | solution.py:297
  55.0 9.9 %all-to-all-done.1 = bf16[16,48,1024]{2,1,0:T(8,128)(2,1)} async-done(((bf16[16,48,1024]{2,1,0:T(8,128)(2,1)}), bf16[16,48,1024]{2,1,0:T(8,128)(2,1)}, u32[]{:S(2)}, u32[]{:S(2)}) %all-to-all-start.1) | async-done | bytes 1572896 | tf_op jit(solution)/shard_map/all_to_all | solution.py:575
  66.5 4.5 %gate.1.own_ref = bf16[512,1024]{1,0:T(8,128)(2,1)S(1)} custom-call(bf16[512,768]{1,0:T(8,128)(2,1)} %copy-done.2, bf16[768,1024]{1,0:T(8,128)(2,1)} %bitcast.14.in_ref, f32[512,1024]{1,0:T(8,128)S(1)} %copy-done.1, bf16[128,1024]{1,0:T(8,128)(2,1)S(1)} %collective-permute-done.rim_ref, f32[3,128,1024]{2,1,0:T(8,128)S(1)} %spectrum.1.h_ref, ...), custom_call_target="tpu_custom_call" | custom-call | flops 80530640 | bytes 471859 | tf_op jit(solution)/shard_map/gate/pallas_call | solution.py:321
  71.1 7.3 %all-to-all-start.2 = ((bf16[16,48,1024]{2,1,0:T(8,128)(2,1)}), bf16[16,48,1024]{2,1,0:T(8,128)(2,1)}, u32[]{:S(2)}, u32[]{:S(2)}) async-start(bf16[16,48,1024]{2,1,0:T(8,128)(2,1)} %bitcast.28), calls=%async_computation.2 | async-start | bytes 3145728 | tf_op jit(solution)/shard_map/all_to_all | solution.py:575
  78.8 5.4 %project.4 = (bf16[256,1024]{1,0:T(8,128)(2,1)}, bf16[256,1024]{1,0:T(8,128)(2,1)}) custom-call(s32[4]{0:T(128)S(1)} %pad_add_fusion.1.blocks_ref, bf16[512,1024]{1,0:T(8,128)(2,1)S(1)} %gate.1.own_ref, bf16[512,1024]{1,0:T(8,128)(2,1)S(1)} %collective-permute-done.1.other_ref, bf16[1024,8192]{1,0:T(8,128)(2,1)} %rest_0_.7, ...), custom_call_target="tpu_custom_call" | custom-call | flops 214748368 | bytes 838860 | tf_op jit(solution)/shard_map/project/pallas_call | solution.py:374
  87.7 6.1 %project.5 = (bf16[256,1024]{1,0:T(8,128)(2,1)}, bf16[256,1024]{1,0:T(8,128)(2,1)}) custom-call(s32[4]{0:T(128)S(1)} %pad_add_fusion.1.blocks_ref, bf16[512,1024]{1,0:T(8,128)(2,1)S(1)} %gate.1.own_ref, bf16[512,1024]{1,0:T(8,128)(2,1)S(1)} %collective-permute-done.1.other_ref, bf16[1024,8192]{1,0:T(8,128)(2,1)} %rest_0_.7, ...), custom_call_target="tpu_custom_call" | custom-call | flops 214748368 | bytes 1258291 | tf_op jit(solution)/shard_map/project/pallas_call | solution.py:374
  95.8 4.6 %collective-permute-done.3.rest_4_ = bf16[256,1024]{1,0:T(8,128)(2,1)} collective-permute-done((bf16[256,1024]{1,0:T(8,128)(2,1)}, bf16[256,1024]{1,0:T(8,128)(2,1)}, u32[]{:S(2)}, u32[]{:S(2)}) %collective-permute-start.3) | collective-permute-done | bytes 524320 | tf_op jit(solution)/shard_map/ppermute | solution.py:567
  100.8 5.6 %project.6 = (bf16[256,1024]{1,0:T(8,128)(2,1)S(1)}, bf16[256,1024]{1,0:T(8,128)(2,1)S(1)}) custom-call(s32[4]{0:T(128)S(1)} %pad_add_fusion.1.blocks_ref, bf16[512,1024]{1,0:T(8,128)(2,1)S(1)} %gate.1.own_ref, bf16[512,1024]{1,0:T(8,128)(2,1)S(1)} %collective-permute-done.1.other_ref, bf16[1024,8192]{1,0:T(8,128)(2,1)} %rest_0_.7, ...), custom_call_target="tpu_custom_call" | custom-call | flops 214748368 | bytes 1258291 | tf_op jit(solution)/shard_map/project/pallas_call | solution.py:374
  111.6 2.4 %unpack.3.k_ref = bf16[512,1024]{1,0:T(8,128)(2,1)S(1)} custom-call(bf16[512,768]{1,0:T(8,128)(2,1)S(1)} %copy-done.12, bf16[768,1024]{1,0:T(8,128)(2,1)} %bitcast.16.in_ref), custom_call_target="tpu_custom_call" | custom-call | flops 80530640 | bytes 262144 | tf_op jit(solution)/shard_map/unpack/pallas_call | solution.py:179
  113.9 4.7 %project.7.own_ref = bf16[512,1024]{1,0:T(8,128)(2,1)S(1)} custom-call(s32[4]{0:T(128)S(1)} %pad_add_fusion.1.blocks_ref, bf16[512,1024]{1,0:T(8,128)(2,1)S(1)} %gate.1.own_ref, bf16[512,1024]{1,0:T(8,128)(2,1)S(1)} %collective-permute-done.1.other_ref, bf16[1024,8192]{1,0:T(8,128)(2,1)} %rest_0_.7, bf16[1024,8192]{1,0:T(8,128)(2,1)} %collective-permute-done.2.rest_1_.rest_3_), custom_call_target="tpu_custom_call" | custom-call | flops 214748368 | bytes 838860 | tf_op jit(solution)/shard_map/project/pallas_call | solution.py:374
  118.7 3.6 %collective-permute-done.5.a0_ref = bf16[256,1024]{1,0:T(8,128)(2,1)S(1)} collective-permute-done((bf16[256,1024]{1,0:T(8,128)(2,1)}, bf16[256,1024]{1,0:T(8,128)(2,1)S(1)}, u32[]{:S(2)}, u32[]{:S(2)}) %collective-permute-start.5) | collective-permute-done | bytes 524320 | tf_op jit(solution)/shard_map/ppermute | solution.py:567
  122.4 6.2 %ends.1 = (f32[8,512,128]{2,1,0:T(8,128)}, f32[8,128,128]{2,1,0:T(8,128)S(1)}, bf16[256,1024]{1,0:T(8,128)(2,1)}) custom-call(s32[25]{0:T(128)S(1)} %pad_add_fusion.table_ref, bf16[512,1024]{1,0:T(8,128)(2,1)S(1)} %project.7.own_ref, bf16[256,1024]{1,0:T(8,128)(2,1)S(1)} %collective-permute-done.5.a0_ref, bf16[256,1024]{1,0:T(8,128)(2,1)} %collective-permute-done.6.a1_ref, ...), custom_call_target="tpu_custom_call" | custom-call | flops 400000000 | bytes 629145 | tf_op jit(solution)/shard_map/ends/pallas_call | solution.py:437
  128.6 6.8 %all-to-all-start.3 = ((bf16[16,16,1024]{2,1,0:T(8,128)(2,1)}), bf16[16,16,1024]{2,1,0:T(8,128)(2,1)S(1)}, u32[]{:S(2)}, u32[]{:S(2)}) async-start(bf16[16,16,1024]{2,1,0:T(8,128)(2,1)} %bitcast.17), calls=%async_computation.3 | async-start | bytes 1048576 | tf_op jit(solution)/shard_map/all_to_all | solution.py:575
  135.5 7.5 %recur.1.li_ref = f32[8,512,128]{2,1,0:T(8,128)S(1)} custom-call(s32[25]{0:T(128)S(1)} %pad_add_fusion.table_ref, f32[8,128,128]{2,1,0:T(8,128)S(1)} %get-tuple-element.70.seg_ref, f32[8,512,128]{2,1,0:T(8,128)} %get-tuple-element.71.u_ref, f32[512,128]{1,0:T(8,128)S(1)} %broadcast_in_dim.35.keep_ref, f32[4,16,1024]{2,1,0:T(8,128)S(1)} %pad_maximum_fusion.coef_ref), custom_call_target="tpu_custom_call" | custom-call | flops 800000000 | bytes 419430 | tf_op jit(solution)/shard_map/recur/pallas_call | solution.py:491
  143.1 2.4 %all-to-all-done.3.ends_ref = bf16[16,16,1024]{2,1,0:T(8,128)(2,1)S(1)} async-done(((bf16[16,16,1024]{2,1,0:T(8,128)(2,1)}), bf16[16,16,1024]{2,1,0:T(8,128)(2,1)S(1)}, u32[]{:S(2)}, u32[]{:S(2)}) %all-to-all-start.3) | async-done | bytes 524320 | tf_op jit(solution)/shard_map/all_to_all | solution.py:575
  145.6 5.9 %carry.1 = bf16[768,1024]{1,0:T(8,128)(2,1)S(1)} custom-call(s32[25]{0:T(128)S(1)} %pad_add_fusion.table_ref, bf16[16,16,1024]{2,1,0:T(8,128)(2,1)S(1)} %all-to-all-done.3.ends_ref, f32[8,512,128]{2,1,0:T(8,128)S(1)} %recur.1.li_ref, f32[512,128]{1,0:T(8,128)S(1)} %broadcast_in_dim.36.unbroken_ref, f32[4,16,1024]{2,1,0:T(8,128)S(1)} %pad_maximum_fusion.coef_ref, ...), custom_call_target="tpu_custom_call" | custom-call | flops 400000000 | bytes 419430 | tf_op jit(solution)/shard_map/carry/pallas_call | solution.py:540
  151.5 24.7 %all_to_all.56 = bf16[16,48,1024]{2,1,0:T(8,128)(2,1)S(1)} all-to-all(bf16[16,48,1024]{2,1,0:T(8,128)(2,1)S(1)} %bitcast.26), channel_id=1, replica_groups=mesh['ctx'=16,'tp'=8] {'ctx'}, dimensions={0} | all-to-all | bytes 3145728 | tf_op jit(solution)/shard_map/all_to_all | solution.py:575
  176.2 3.0 %finish.1 = bf16[512,1024]{1,0:T(8,128)(2,1)} custom-call(bf16[512,768]{1,0:T(8,128)(2,1)S(1)} %copy-done.9, bf16[5,512,1024]{2,1,0:T(8,128)(2,1)} %bitcast.34, bf16[768,1024]{1,0:T(8,128)(2,1)S(1)} %bitcast.27), custom_call_target="tpu_custom_call" | custom-call | flops 80530640 | bytes 367001 | tf_op jit(solution)/shard_map/finish/pallas_call | solution.py:198
  (82 shorter events, 22.7 us)
Async XLA Ops:
  4.1 74.7 %collective-permute-start.2 = (bf16[1024,8192]{1,0:T(8,128)(2,1)}, bf16[1024,8192]{1,0:T(8,128)(2,1)}, u32[]{:S(2)}, u32[]{:S(2)}) collective-permute-start(bf16[1024,8192]{1,0:T(8,128)(2,1)} %rest_0_.7), channel_id=1, source_target_pairs={{0,1},{1,0},{2,3},{3,2},{4,5},{5,4},{6,7},{7,6},{8,9},{9,8},{10,11... | collective-permute-start | bytes 50331656 | tf_op jit(solution)/shard_map/ppermute | solution.py:567
  4.1 8.3 %copy-start.3 = (bf16[512,256]{1,0:T(8,128)(2,1)S(1)}, bf16[512,256]{1,0:T(8,128)(2,1)}, u32[]{:S(2)}) copy-start(bf16[512,256]{1,0:T(8,128)(2,1)} %constant.117.clone.fwd_ref) | copy-start | bytes 786436
  4.1 33.6 %all-to-all-start = ((bf16[16,48,1024]{2,1,0:T(8,128)(2,1)}), bf16[16,48,1024]{2,1,0:T(8,128)(2,1)S(1)}, u32[]{:S(2)}, u32[]{:S(2)}) async-start(bf16[16,48,1024]{2,1,0:T(8,128)(2,1)} %bitcast.7), calls=%async_computation | async-start | bytes 3145728 | tf_op jit(solution)/shard_map/all_to_all | solution.py:575
  14.3 5.2 %copy-start.17 = (f32[16,1024]{1,0:T(8,128)S(1)}, f32[16,1024]{1,0:T(8,128)}, u32[]{:S(2)}) copy-start(f32[16,1024]{1,0:T(8,128)} %param.15) | copy-start | bytes 196612
  14.3 5.2 %copy-start.18 = (f32[16,1024]{1,0:T(8,128)S(1)}, f32[16,1024]{1,0:T(8,128)}, u32[]{:S(2)}) copy-start(f32[16,1024]{1,0:T(8,128)} %param.16) | copy-start | bytes 196612
  19.5 1.7 copy-start.7
  37.7 27.2 %all-to-all-start.1 = ((bf16[16,48,1024]{2,1,0:T(8,128)(2,1)}), bf16[16,48,1024]{2,1,0:T(8,128)(2,1)}, u32[]{:S(2)}, u32[]{:S(2)}) async-start(bf16[16,48,1024]{2,1,0:T(8,128)(2,1)} %bitcast.29), calls=%async_computation.1 | async-start | bytes 3145728 | tf_op jit(solution)/shard_map/all_to_all | solution.py:575
  44.3 5.2 %copy-start.4 = (bf16[512,256]{1,0:T(8,128)(2,1)S(1)}, bf16[512,256]{1,0:T(8,128)(2,1)}, u32[]{:S(2)}) copy-start(bf16[512,256]{1,0:T(8,128)(2,1)} %constant.117.clone.fwd_ref) | copy-start | bytes 786436
  44.3 5.2 %copy-start.13 = (bf16[256,256]{1,0:T(8,128)(2,1)S(1)}, bf16[256,256]{1,0:T(8,128)(2,1)}, u32[]{:S(2)}) copy-start(bf16[256,256]{1,0:T(8,128)(2,1)} %constant.118.clone.inv_ref) | copy-start | bytes 393220
  45.7 19.2 %copy-start.5 = (bf16[512,256]{1,0:T(8,128)(2,1)S(1)}, bf16[512,256]{1,0:T(8,128)(2,1)}, u32[]{:S(2)}) copy-start(bf16[512,256]{1,0:T(8,128)(2,1)} %constant.117.clone.fwd_ref) | copy-start | bytes 786436
  45.8 19.2 %collective-permute-start = (bf16[128,1024]{1,0:T(8,128)(2,1)S(1)}, bf16[128,1024]{1,0:T(8,128)(2,1)S(1)}, u32[]{:S(2)}, u32[]{:S(2)}) collective-permute-start(bf16[128,1024]{1,0:T(8,128)(2,1)S(1)} %slice.4), channel_id=1, source_target_pairs={{0,8},{8,16},{16,24},{24,32},{32,40},{40,48},{48,56},{56,64},{64,7... | collective-permute-start | bytes 786440 | tf_op jit(solution)/shard_map/ppermute | solution.py:628
  64.9 1.6 copy-start.1
  71.0 7.7 %collective-permute-start.1 = (bf16[512,1024]{1,0:T(8,128)(2,1)S(1)}, bf16[512,1024]{1,0:T(8,128)(2,1)S(1)}, u32[]{:S(2)}, u32[]{:S(2)}) collective-permute-start(bf16[512,1024]{1,0:T(8,128)(2,1)S(1)} %gate.1.own_ref), channel_id=1, source_target_pairs={{0,1},{1,0},{2,3},{3,2},{4,5},{5,4},{6,7},{7,6},{8,9},{9,8},{10,11... | collective-permute-start | bytes 3145736 | tf_op jit(solution)/shard_map/ppermute | solution.py:567
  71.1 7.5 %copy-start.19 = (s32[8]{0:T(128)S(1)}, s32[8]{0:T(128)}, u32[]{:S(2)}) copy-start(s32[8]{0:T(128)} %param.12) | copy-start | bytes 100
  71.1 36.9 %all-to-all-start.2 = ((bf16[16,48,1024]{2,1,0:T(8,128)(2,1)}), bf16[16,48,1024]{2,1,0:T(8,128)(2,1)}, u32[]{:S(2)}, u32[]{:S(2)}) async-start(bf16[16,48,1024]{2,1,0:T(8,128)(2,1)} %bitcast.28), calls=%async_computation.2 | async-start | bytes 3145728 | tf_op jit(solution)/shard_map/all_to_all | solution.py:575
  84.2 16.3 %collective-permute-start.3 = (bf16[256,1024]{1,0:T(8,128)(2,1)}, bf16[256,1024]{1,0:T(8,128)(2,1)}, u32[]{:S(2)}, u32[]{:S(2)}) collective-permute-start(bf16[256,1024]{1,0:T(8,128)(2,1)} %get-tuple-element.56), channel_id=1, source_target_pairs={{0,2},{1,3},{2,4},{3,5},{4,6},{5,7},{6,0},{7,1},{8,10},{9,11},{10,... | collective-permute-start | bytes 1572872 | tf_op jit(solution)/shard_map/ppermute | solution.py:567
  85.7 15.1 %collective-permute-start.4 = (bf16[256,1024]{1,0:T(8,128)(2,1)}, bf16[256,1024]{1,0:T(8,128)(2,1)}, u32[]{:S(2)}, u32[]{:S(2)}) collective-permute-start(bf16[256,1024]{1,0:T(8,128)(2,1)} %get-tuple-element.57), channel_id=1, source_target_pairs={{0,6},{1,7},{2,0},{3,1},{4,2},{5,3},{6,4},{7,5},{8,14},{9,15},{10,... | collective-permute-start | bytes 1572872 | tf_op jit(solution)/shard_map/ppermute | solution.py:567
  93.8 17.7 %copy-start.12 = (bf16[512,768]{1,0:T(8,128)(2,1)S(1)}, bf16[512,768]{1,0:T(8,128)(2,1)}, u32[]{:S(2)}) copy-start(bf16[512,768]{1,0:T(8,128)(2,1)} %copy-done.11) | copy-start | bytes 2359300
  93.8 24.8 %collective-permute-start.6 = (bf16[256,1024]{1,0:T(8,128)(2,1)}, bf16[256,1024]{1,0:T(8,128)(2,1)}, u32[]{:S(2)}, u32[]{:S(2)}) collective-permute-start(bf16[256,1024]{1,0:T(8,128)(2,1)} %get-tuple-element.63), channel_id=1, source_target_pairs={{0,6},{1,7},{2,0},{3,1},{4,2},{5,3},{6,4},{7,5},{8,14},{9,15},{10,... | collective-permute-start | bytes 1572872 | tf_op jit(solution)/shard_map/ppermute | solution.py:567
  95.4 23.3 %collective-permute-start.7 = (bf16[256,1024]{1,0:T(8,128)(2,1)}, bf16[256,1024]{1,0:T(8,128)(2,1)}, u32[]{:S(2)}, u32[]{:S(2)}) collective-permute-start(bf16[256,1024]{1,0:T(8,128)(2,1)} %get-tuple-element.64), channel_id=1, source_target_pairs={{0,2},{1,3},{2,4},{3,5},{4,6},{5,7},{6,0},{7,1},{8,10},{9,11},{10,... | collective-permute-start | bytes 1572872 | tf_op jit(solution)/shard_map/ppermute | solution.py:567
  108.0 14.2 %collective-permute-start.5 = (bf16[256,1024]{1,0:T(8,128)(2,1)}, bf16[256,1024]{1,0:T(8,128)(2,1)S(1)}, u32[]{:S(2)}, u32[]{:S(2)}) collective-permute-start(bf16[256,1024]{1,0:T(8,128)(2,1)} %copy-done.16), channel_id=1, source_target_pairs={{0,2},{1,3},{2,4},{3,5},{4,6},{5,7},{6,0},{7,1},{8,10},{9,11},{10,... | collective-permute-start | bytes 1572872 | tf_op jit(solution)/shard_map/ppermute | solution.py:567
  109.5 12.7 %collective-permute-start.8 = (bf16[256,1024]{1,0:T(8,128)(2,1)}, bf16[256,1024]{1,0:T(8,128)(2,1)S(1)}, u32[]{:S(2)}, u32[]{:S(2)}) collective-permute-start(bf16[256,1024]{1,0:T(8,128)(2,1)} %copy-done.15), channel_id=1, source_target_pairs={{0,6},{1,7},{2,0},{3,1},{4,2},{5,3},{6,4},{7,5},{8,14},{9,15},{10,... | collective-permute-start | bytes 1572872 | tf_op jit(solution)/shard_map/ppermute | solution.py:567
  128.6 16.9 %all-to-all-start.3 = ((bf16[16,16,1024]{2,1,0:T(8,128)(2,1)}), bf16[16,16,1024]{2,1,0:T(8,128)(2,1)S(1)}, u32[]{:S(2)}, u32[]{:S(2)}) async-start(bf16[16,16,1024]{2,1,0:T(8,128)(2,1)} %bitcast.17), calls=%async_computation.3 | async-start | bytes 1048576 | tf_op jit(solution)/shard_map/all_to_all | solution.py:575
  151.5 24.7 %copy-start.9 = (bf16[512,768]{1,0:T(8,128)(2,1)S(1)}, bf16[512,768]{1,0:T(8,128)(2,1)}, u32[]{:S(2)}) copy-start(bf16[512,768]{1,0:T(8,128)(2,1)} %copy-done.8) | copy-start | bytes 2359300
  (9 other events, 9.8 us)

commit v5 on v4

--- a/solution.py
+++ b/solution.py
@@ -336,7 +336,7 @@
         compiler_params=params(),
         cost_estimate=cost(2 * slots * rows * channels, (6 * rows + 2 * slots) * channels),
         name="gate",
-    )(in_hbm(to_rows), in_hbm(received), filtered, rim, spectrum, forward, inverse, in_hbm(beside))
+    )(in_hbm(to_rows), in_hbm(received), in_hbm(filtered), rim, spectrum, forward, inverse, in_hbm(beside))
 
 
 def project(tasks, blocks, own, other, weight, other_weight, tile=512):

time: 180 us -> 179 us (level)
    unnamed x40 -> x38, local copies, waits for them, and re-layouts: 9.12 us -> 7.49 us
where the time goes in v5:
time: 179 us; the launch traced here: 178 us
  Pallas kernels  67.5 us (38%)
  starting transfers between devices  39.2 us (22%)
  waiting for transfers between devices  37.3 us (21%)
  blocking collectives  24.7 us (14%)
  local copies, waits for them, and re-layouts  7.96 us (4%)
    all_to_all x4, waiting for transfers between devices, swap(): return lax.all_to_all(shard, 'ctx', split_axis=0, concat_axis=0, tiled=True)  28.8 us
    all_to_all x4, starting transfers between devices, swap(): return lax.all_to_all(shard, 'ctx', split_axis=0, concat_axis=0, tiled=True)  26.8 us
    all_to_all x1, blocking collectives, swap(): return lax.all_to_all(shard, 'ctx', split_axis=0, concat_axis=0, tiled=True)  24.7 us
    pallas_call x4, Pallas kernels, project(): pl.pallas_call(body, grid_spec=pltpu.PrefetchScalarGridSpec(num_scalar_pr...  21.8 us
    ppermute x8, starting transfers between devices, along_x(): return lax.ppermute(shard, 'tp', pairs)  8.59 us
    ppermute x8, waiting for transfers between devices, along_x(): return lax.ppermute(shard, 'tp', pairs)  8.54 us
    pallas_call x1, Pallas kernels, recur(): pl.pallas_call(body, grid_spec=pltpu.PrefetchScalarGridSpec(num_scalar_pr...  7.54 us
    unnamed x38, local copies, waits for them, and re-layouts  7.49 us
  transfers between devices with their start and end apart: 13, of which 6 were waited for; matrix products, arithmetic and copies ran while one was open for 1% of the time, Pallas kernels for 27%

profile of v5, /device:TPU:0, one launch (start us, length us, event | category | flops | bytes accessed | tf_op | source)
XLA Modules:
  0.0 177.9 jit_solution(17927013871419448155)
XLA Ops:
  0.0 4.1 %pack_kv.1 = bf16[768,1024]{1,0:T(8,128)(2,1)} custom-call(s32[1,512]{1,0:T(1,128)} %bitcast.35, bf16[5,512,1024]{2,1,0:T(8,128)(2,1)} %bitcast.30, bf16[5,512,1024]{2,1,0:T(8,128)(2,1)} %bitcast.31), custom_call_target="tpu_custom_call" | custom-call | flops 80530640 | bytes 367001 | tf_op jit(solution)/shard_map/pack_kv/pallas_call | solution.py:96
  4.1 8.3 %all-to-all-start = ((bf16[16,48,1024]{2,1,0:T(8,128)(2,1)}), bf16[16,48,1024]{2,1,0:T(8,128)(2,1)S(1)}, u32[]{:S(2)}, u32[]{:S(2)}) async-start(bf16[16,48,1024]{2,1,0:T(8,128)(2,1)} %bitcast.7), calls=%async_computation | async-start | bytes 3145728 | tf_op jit(solution)/shard_map/all_to_all | solution.py:575
  14.3 4.3 %pack_two.1 = (bf16[768,1024]{1,0:T(8,128)(2,1)S(1)}, bf16[768,1024]{1,0:T(8,128)(2,1)S(1)}, bf16[512,768]{1,0:T(8,128)(2,1)S(1)}) custom-call(s32[1,512]{1,0:T(1,128)} %bitcast.36, bf16[5,512,1024]{2,1,0:T(8,128)(2,1)} %bitcast.32, bf16[5,512,1024]{2,1,0:T(8,128)(2,1)} %bitcast.33), custom_call_target="tpu_custom_call" | custom-call | flops 161061280 | bytes 524288 | tf_op jit(solution)/shard_map/pack_two/pallas_call | solution.py:124
  21.3 16.4 %all-to-all-done = bf16[16,48,1024]{2,1,0:T(8,128)(2,1)S(1)} async-done(((bf16[16,48,1024]{2,1,0:T(8,128)(2,1)}), bf16[16,48,1024]{2,1,0:T(8,128)(2,1)S(1)}, u32[]{:S(2)}, u32[]{:S(2)}) %all-to-all-start) | async-done | bytes 1572896 | tf_op jit(solution)/shard_map/all_to_all | solution.py:575
  37.7 4.4 %all-to-all-start.1 = ((bf16[16,48,1024]{2,1,0:T(8,128)(2,1)}), bf16[16,48,1024]{2,1,0:T(8,128)(2,1)}, u32[]{:S(2)}, u32[]{:S(2)}) async-start(bf16[16,48,1024]{2,1,0:T(8,128)(2,1)} %bitcast.29), calls=%async_computation.1 | async-start | bytes 3145728 | tf_op jit(solution)/shard_map/all_to_all | solution.py:575
  45.7 3.8 %collective-permute-start = (bf16[128,1024]{1,0:T(8,128)(2,1)S(1)}, bf16[128,1024]{1,0:T(8,128)(2,1)S(1)}, u32[]{:S(2)}, u32[]{:S(2)}) collective-permute-start(bf16[128,1024]{1,0:T(8,128)(2,1)S(1)} %slice.4), channel_id=1, source_target_pairs={{0,8},{8,16},{16,24},{24,32},{32,40},{40,48},{48,56},{56,64},{64,7... | collective-permute-start | bytes 786440 | tf_op jit(solution)/shard_map/ppermute | solution.py:628
  49.6 4.0 %taps.1.filt_ref = f32[512,1024]{1,0:T(8,128)S(1)} custom-call(bf16[512,1024]{1,0:T(8,128)(2,1)S(1)} %unpack.2.u_ref, f32[3,128,1024]{2,1,0:T(8,128)S(1)} %spectrum.1.h_ref, bf16[512,256]{1,0:T(8,128)(2,1)S(1)} %copy-done.3, bf16[256,256]{1,0:T(8,128)(2,1)S(1)} %copy-done.12), custom_call_target="tpu_custom_call" | custom-call | flops 93952408 | bytes 419430 | tf_op jit(solution)/shard_map/taps/pallas_call | solution.py:297
  54.9 10.0 %all-to-all-done.1 = bf16[16,48,1024]{2,1,0:T(8,128)(2,1)} async-done(((bf16[16,48,1024]{2,1,0:T(8,128)(2,1)}), bf16[16,48,1024]{2,1,0:T(8,128)(2,1)}, u32[]{:S(2)}, u32[]{:S(2)}) %all-to-all-start.1) | async-done | bytes 1572896 | tf_op jit(solution)/shard_map/all_to_all | solution.py:575
  64.9 4.8 %gate.1.own_ref = bf16[512,1024]{1,0:T(8,128)(2,1)S(1)} custom-call(bf16[512,768]{1,0:T(8,128)(2,1)} %copy-done.1, bf16[768,1024]{1,0:T(8,128)(2,1)} %bitcast.14.in_ref, f32[512,1024]{1,0:T(8,128)} %copy-done, bf16[128,1024]{1,0:T(8,128)(2,1)S(1)} %collective-permute-done.rim_ref, f32[3,128,1024]{2,1,0:T(8,128)S(1)} %spectrum.1.h_ref, ...), custom_call_target="tpu_custom_call" | custom-call | flops 80530640 | bytes 471859 | tf_op jit(solution)/shard_map/gate/pallas_call | solution.py:321
  69.8 7.3 %all-to-all-start.2 = ((bf16[16,48,1024]{2,1,0:T(8,128)(2,1)}), bf16[16,48,1024]{2,1,0:T(8,128)(2,1)}, u32[]{:S(2)}, u32[]{:S(2)}) async-start(bf16[16,48,1024]{2,1,0:T(8,128)(2,1)} %bitcast.28), calls=%async_computation.2 | async-start | bytes 3145728 | tf_op jit(solution)/shard_map/all_to_all | solution.py:575
  77.5 5.4 %project.4 = (bf16[256,1024]{1,0:T(8,128)(2,1)}, bf16[256,1024]{1,0:T(8,128)(2,1)}) custom-call(s32[4]{0:T(128)S(1)} %pad_add_fusion.1.blocks_ref, bf16[512,1024]{1,0:T(8,128)(2,1)S(1)} %gate.1.own_ref, bf16[512,1024]{1,0:T(8,128)(2,1)S(1)} %collective-permute-done.1.other_ref, bf16[1024,8192]{1,0:T(8,128)(2,1)} %rest_0_.7, ...), custom_call_target="tpu_custom_call" | custom-call | flops 214748368 | bytes 838860 | tf_op jit(solution)/shard_map/project/pallas_call | solution.py:374
  86.4 6.1 %project.5 = (bf16[256,1024]{1,0:T(8,128)(2,1)}, bf16[256,1024]{1,0:T(8,128)(2,1)}) custom-call(s32[4]{0:T(128)S(1)} %pad_add_fusion.1.blocks_ref, bf16[512,1024]{1,0:T(8,128)(2,1)S(1)} %gate.1.own_ref, bf16[512,1024]{1,0:T(8,128)(2,1)S(1)} %collective-permute-done.1.other_ref, bf16[1024,8192]{1,0:T(8,128)(2,1)} %rest_0_.7, ...), custom_call_target="tpu_custom_call" | custom-call | flops 214748368 | bytes 1258291 | tf_op jit(solution)/shard_map/project/pallas_call | solution.py:374
  94.5 4.6 %collective-permute-done.3.rest_4_ = bf16[256,1024]{1,0:T(8,128)(2,1)} collective-permute-done((bf16[256,1024]{1,0:T(8,128)(2,1)}, bf16[256,1024]{1,0:T(8,128)(2,1)}, u32[]{:S(2)}, u32[]{:S(2)}) %collective-permute-start.3) | collective-permute-done | bytes 524320 | tf_op jit(solution)/shard_map/ppermute | solution.py:567
  99.5 5.6 %project.6 = (bf16[256,1024]{1,0:T(8,128)(2,1)S(1)}, bf16[256,1024]{1,0:T(8,128)(2,1)S(1)}) custom-call(s32[4]{0:T(128)S(1)} %pad_add_fusion.1.blocks_ref, bf16[512,1024]{1,0:T(8,128)(2,1)S(1)} %gate.1.own_ref, bf16[512,1024]{1,0:T(8,128)(2,1)S(1)} %collective-permute-done.1.other_ref, bf16[1024,8192]{1,0:T(8,128)(2,1)} %rest_0_.7, ...), custom_call_target="tpu_custom_call" | custom-call | flops 214748368 | bytes 1258291 | tf_op jit(solution)/shard_map/project/pallas_call | solution.py:374
  110.2 2.4 %unpack.3.k_ref = bf16[512,1024]{1,0:T(8,128)(2,1)S(1)} custom-call(bf16[512,768]{1,0:T(8,128)(2,1)S(1)} %copy-done.11, bf16[768,1024]{1,0:T(8,128)(2,1)} %bitcast.16.in_ref), custom_call_target="tpu_custom_call" | custom-call | flops 80530640 | bytes 262144 | tf_op jit(solution)/shard_map/unpack/pallas_call | solution.py:179
  112.6 4.7 %project.7.own_ref = bf16[512,1024]{1,0:T(8,128)(2,1)S(1)} custom-call(s32[4]{0:T(128)S(1)} %pad_add_fusion.1.blocks_ref, bf16[512,1024]{1,0:T(8,128)(2,1)S(1)} %gate.1.own_ref, bf16[512,1024]{1,0:T(8,128)(2,1)S(1)} %collective-permute-done.1.other_ref, bf16[1024,8192]{1,0:T(8,128)(2,1)} %rest_0_.7, bf16[1024,8192]{1,0:T(8,128)(2,1)} %collective-permute-done.2.rest_1_.rest_3_), custom_call_target="tpu_custom_call" | custom-call | flops 214748368 | bytes 838860 | tf_op jit(solution)/shard_map/project/pallas_call | solution.py:374
  117.3 3.6 %collective-permute-done.5.a0_ref = bf16[256,1024]{1,0:T(8,128)(2,1)S(1)} collective-permute-done((bf16[256,1024]{1,0:T(8,128)(2,1)}, bf16[256,1024]{1,0:T(8,128)(2,1)S(1)}, u32[]{:S(2)}, u32[]{:S(2)}) %collective-permute-start.5) | collective-permute-done | bytes 524320 | tf_op jit(solution)/shard_map/ppermute | solution.py:567
  121.1 6.2 %ends.1 = (f32[8,512,128]{2,1,0:T(8,128)}, f32[8,128,128]{2,1,0:T(8,128)S(1)}, bf16[256,1024]{1,0:T(8,128)(2,1)}) custom-call(s32[25]{0:T(128)S(1)} %pad_add_fusion.table_ref, bf16[512,1024]{1,0:T(8,128)(2,1)S(1)} %project.7.own_ref, bf16[256,1024]{1,0:T(8,128)(2,1)S(1)} %collective-permute-done.5.a0_ref, bf16[256,1024]{1,0:T(8,128)(2,1)} %collective-permute-done.6.a1_ref, ...), custom_call_target="tpu_custom_call" | custom-call | flops 400000000 | bytes 629145 | tf_op jit(solution)/shard_map/ends/pallas_call | solution.py:437
  127.2 6.8 %all-to-all-start.3 = ((bf16[16,16,1024]{2,1,0:T(8,128)(2,1)}), bf16[16,16,1024]{2,1,0:T(8,128)(2,1)S(1)}, u32[]{:S(2)}, u32[]{:S(2)}) async-start(bf16[16,16,1024]{2,1,0:T(8,128)(2,1)} %bitcast.17), calls=%async_computation.3 | async-start | bytes 1048576 | tf_op jit(solution)/shard_map/all_to_all | solution.py:575
  134.2 7.5 %recur.1.li_ref = f32[8,512,128]{2,1,0:T(8,128)S(1)} custom-call(s32[25]{0:T(128)S(1)} %pad_add_fusion.table_ref, f32[8,128,128]{2,1,0:T(8,128)S(1)} %get-tuple-element.70.seg_ref, f32[8,512,128]{2,1,0:T(8,128)} %get-tuple-element.71.u_ref, f32[512,128]{1,0:T(8,128)S(1)} %broadcast_in_dim.35.keep_ref, f32[4,16,1024]{2,1,0:T(8,128)S(1)} %pad_maximum_fusion.coef_ref), custom_call_target="tpu_custom_call" | custom-call | flops 800000000 | bytes 419430 | tf_op jit(solution)/shard_map/recur/pallas_call | solution.py:491
  141.8 2.4 %all-to-all-done.3.ends_ref = bf16[16,16,1024]{2,1,0:T(8,128)(2,1)S(1)} async-done(((bf16[16,16,1024]{2,1,0:T(8,128)(2,1)}), bf16[16,16,1024]{2,1,0:T(8,128)(2,1)S(1)}, u32[]{:S(2)}, u32[]{:S(2)}) %all-to-all-start.3) | async-done | bytes 524320 | tf_op jit(solution)/shard_map/all_to_all | solution.py:575
  144.3 5.9 %carry.1 = bf16[768,1024]{1,0:T(8,128)(2,1)S(1)} custom-call(s32[25]{0:T(128)S(1)} %pad_add_fusion.table_ref, bf16[16,16,1024]{2,1,0:T(8,128)(2,1)S(1)} %all-to-all-done.3.ends_ref, f32[8,512,128]{2,1,0:T(8,128)S(1)} %recur.1.li_ref, f32[512,128]{1,0:T(8,128)S(1)} %broadcast_in_dim.36.unbroken_ref, f32[4,16,1024]{2,1,0:T(8,128)S(1)} %pad_maximum_fusion.coef_ref, ...), custom_call_target="tpu_custom_call" | custom-call | flops 400000000 | bytes 419430 | tf_op jit(solution)/shard_map/carry/pallas_call | solution.py:540
  150.2 24.7 %all_to_all.56 = bf16[16,48,1024]{2,1,0:T(8,128)(2,1)S(1)} all-to-all(bf16[16,48,1024]{2,1,0:T(8,128)(2,1)S(1)} %bitcast.26), channel_id=1, replica_groups=mesh['ctx'=16,'tp'=8] {'ctx'}, dimensions={0} | all-to-all | bytes 3145728 | tf_op jit(solution)/shard_map/all_to_all | solution.py:575
  174.9 3.0 %finish.1 = bf16[512,1024]{1,0:T(8,128)(2,1)} custom-call(bf16[512,768]{1,0:T(8,128)(2,1)S(1)} %copy-done.8, bf16[5,512,1024]{2,1,0:T(8,128)(2,1)} %bitcast.34, bf16[768,1024]{1,0:T(8,128)(2,1)S(1)} %bitcast.27), custom_call_target="tpu_custom_call" | custom-call | flops 80530640 | bytes 367001 | tf_op jit(solution)/shard_map/finish/pallas_call | solution.py:198
  (80 shorter events, 21.1 us)
Async XLA Ops:
  4.1 73.4 %collective-permute-start.2 = (bf16[1024,8192]{1,0:T(8,128)(2,1)}, bf16[1024,8192]{1,0:T(8,128)(2,1)}, u32[]{:S(2)}, u32[]{:S(2)}) collective-permute-start(bf16[1024,8192]{1,0:T(8,128)(2,1)} %rest_0_.7), channel_id=1, source_target_pairs={{0,1},{1,0},{2,3},{3,2},{4,5},{5,4},{6,7},{7,6},{8,9},{9,8},{10,11... | collective-permute-start | bytes 50331656 | tf_op jit(solution)/shard_map/ppermute | solution.py:567
  4.1 8.3 %copy-start.2 = (bf16[512,256]{1,0:T(8,128)(2,1)S(1)}, bf16[512,256]{1,0:T(8,128)(2,1)}, u32[]{:S(2)}) copy-start(bf16[512,256]{1,0:T(8,128)(2,1)} %constant.117.clone.fwd_ref) | copy-start | bytes 786436
  4.1 33.6 %all-to-all-start = ((bf16[16,48,1024]{2,1,0:T(8,128)(2,1)}), bf16[16,48,1024]{2,1,0:T(8,128)(2,1)S(1)}, u32[]{:S(2)}, u32[]{:S(2)}) async-start(bf16[16,48,1024]{2,1,0:T(8,128)(2,1)} %bitcast.7), calls=%async_computation | async-start | bytes 3145728 | tf_op jit(solution)/shard_map/all_to_all | solution.py:575
  14.3 5.2 %copy-start.16 = (f32[16,1024]{1,0:T(8,128)S(1)}, f32[16,1024]{1,0:T(8,128)}, u32[]{:S(2)}) copy-start(f32[16,1024]{1,0:T(8,128)} %param.15) | copy-start | bytes 196612
  14.3 5.2 %copy-start.17 = (f32[16,1024]{1,0:T(8,128)S(1)}, f32[16,1024]{1,0:T(8,128)}, u32[]{:S(2)}) copy-start(f32[16,1024]{1,0:T(8,128)} %param.16) | copy-start | bytes 196612
  19.5 1.7 copy-start.6
  37.7 27.2 %all-to-all-start.1 = ((bf16[16,48,1024]{2,1,0:T(8,128)(2,1)}), bf16[16,48,1024]{2,1,0:T(8,128)(2,1)}, u32[]{:S(2)}, u32[]{:S(2)}) async-start(bf16[16,48,1024]{2,1,0:T(8,128)(2,1)} %bitcast.29), calls=%async_computation.1 | async-start | bytes 3145728 | tf_op jit(solution)/shard_map/all_to_all | solution.py:575
  44.3 1.4 copy-start.9
  44.3 5.2 %copy-start.3 = (bf16[512,256]{1,0:T(8,128)(2,1)S(1)}, bf16[512,256]{1,0:T(8,128)(2,1)}, u32[]{:S(2)}) copy-start(bf16[512,256]{1,0:T(8,128)(2,1)} %constant.117.clone.fwd_ref) | copy-start | bytes 786436
  44.3 5.2 %copy-start.12 = (bf16[256,256]{1,0:T(8,128)(2,1)S(1)}, bf16[256,256]{1,0:T(8,128)(2,1)}, u32[]{:S(2)}) copy-start(bf16[256,256]{1,0:T(8,128)(2,1)} %constant.118.clone.inv_ref) | copy-start | bytes 393220
  45.7 19.2 %copy-start.4 = (bf16[512,256]{1,0:T(8,128)(2,1)S(1)}, bf16[512,256]{1,0:T(8,128)(2,1)}, u32[]{:S(2)}) copy-start(bf16[512,256]{1,0:T(8,128)(2,1)} %constant.117.clone.fwd_ref) | copy-start | bytes 786436
  45.7 19.2 %collective-permute-start = (bf16[128,1024]{1,0:T(8,128)(2,1)S(1)}, bf16[128,1024]{1,0:T(8,128)(2,1)S(1)}, u32[]{:S(2)}, u32[]{:S(2)}) collective-permute-start(bf16[128,1024]{1,0:T(8,128)(2,1)S(1)} %slice.4), channel_id=1, source_target_pairs={{0,8},{8,16},{16,24},{24,32},{32,40},{40,48},{48,56},{56,64},{64,7... | collective-permute-start | bytes 786440 | tf_op jit(solution)/shard_map/ppermute | solution.py:628
  69.7 7.7 %collective-permute-start.1 = (bf16[512,1024]{1,0:T(8,128)(2,1)S(1)}, bf16[512,1024]{1,0:T(8,128)(2,1)S(1)}, u32[]{:S(2)}, u32[]{:S(2)}) collective-permute-start(bf16[512,1024]{1,0:T(8,128)(2,1)S(1)} %gate.1.own_ref), channel_id=1, source_target_pairs={{0,1},{1,0},{2,3},{3,2},{4,5},{5,4},{6,7},{7,6},{8,9},{9,8},{10,11... | collective-permute-start | bytes 3145736 | tf_op jit(solution)/shard_map/ppermute | solution.py:567
  69.8 7.5 %copy-start.18 = (s32[8]{0:T(128)S(1)}, s32[8]{0:T(128)}, u32[]{:S(2)}) copy-start(s32[8]{0:T(128)} %param.12) | copy-start | bytes 100
  69.8 36.9 %all-to-all-start.2 = ((bf16[16,48,1024]{2,1,0:T(8,128)(2,1)}), bf16[16,48,1024]{2,1,0:T(8,128)(2,1)}, u32[]{:S(2)}, u32[]{:S(2)}) async-start(bf16[16,48,1024]{2,1,0:T(8,128)(2,1)} %bitcast.28), calls=%async_computation.2 | async-start | bytes 3145728 | tf_op jit(solution)/shard_map/all_to_all | solution.py:575
  82.9 16.3 %collective-permute-start.3 = (bf16[256,1024]{1,0:T(8,128)(2,1)}, bf16[256,1024]{1,0:T(8,128)(2,1)}, u32[]{:S(2)}, u32[]{:S(2)}) collective-permute-start(bf16[256,1024]{1,0:T(8,128)(2,1)} %get-tuple-element.56), channel_id=1, source_target_pairs={{0,2},{1,3},{2,4},{3,5},{4,6},{5,7},{6,0},{7,1},{8,10},{9,11},{10,... | collective-permute-start | bytes 1572872 | tf_op jit(solution)/shard_map/ppermute | solution.py:567
  84.4 15.1 %collective-permute-start.4 = (bf16[256,1024]{1,0:T(8,128)(2,1)}, bf16[256,1024]{1,0:T(8,128)(2,1)}, u32[]{:S(2)}, u32[]{:S(2)}) collective-permute-start(bf16[256,1024]{1,0:T(8,128)(2,1)} %get-tuple-element.57), channel_id=1, source_target_pairs={{0,6},{1,7},{2,0},{3,1},{4,2},{5,3},{6,4},{7,5},{8,14},{9,15},{10,... | collective-permute-start | bytes 1572872 | tf_op jit(solution)/shard_map/ppermute | solution.py:567
  92.5 17.7 %copy-start.11 = (bf16[512,768]{1,0:T(8,128)(2,1)S(1)}, bf16[512,768]{1,0:T(8,128)(2,1)}, u32[]{:S(2)}) copy-start(bf16[512,768]{1,0:T(8,128)(2,1)} %copy-done.10) | copy-start | bytes 2359300
  92.5 24.8 %collective-permute-start.6 = (bf16[256,1024]{1,0:T(8,128)(2,1)}, bf16[256,1024]{1,0:T(8,128)(2,1)}, u32[]{:S(2)}, u32[]{:S(2)}) collective-permute-start(bf16[256,1024]{1,0:T(8,128)(2,1)} %get-tuple-element.63), channel_id=1, source_target_pairs={{0,6},{1,7},{2,0},{3,1},{4,2},{5,3},{6,4},{7,5},{8,14},{9,15},{10,... | collective-permute-start | bytes 1572872 | tf_op jit(solution)/shard_map/ppermute | solution.py:567
  94.1 23.3 %collective-permute-start.7 = (bf16[256,1024]{1,0:T(8,128)(2,1)}, bf16[256,1024]{1,0:T(8,128)(2,1)}, u32[]{:S(2)}, u32[]{:S(2)}) collective-permute-start(bf16[256,1024]{1,0:T(8,128)(2,1)} %get-tuple-element.64), channel_id=1, source_target_pairs={{0,2},{1,3},{2,4},{3,5},{4,6},{5,7},{6,0},{7,1},{8,10},{9,11},{10,... | collective-permute-start | bytes 1572872 | tf_op jit(solution)/shard_map/ppermute | solution.py:567
  106.7 14.2 %collective-permute-start.5 = (bf16[256,1024]{1,0:T(8,128)(2,1)}, bf16[256,1024]{1,0:T(8,128)(2,1)S(1)}, u32[]{:S(2)}, u32[]{:S(2)}) collective-permute-start(bf16[256,1024]{1,0:T(8,128)(2,1)} %copy-done.15), channel_id=1, source_target_pairs={{0,2},{1,3},{2,4},{3,5},{4,6},{5,7},{6,0},{7,1},{8,10},{9,11},{10,... | collective-permute-start | bytes 1572872 | tf_op jit(solution)/shard_map/ppermute | solution.py:567
  108.2 12.7 %collective-permute-start.8 = (bf16[256,1024]{1,0:T(8,128)(2,1)}, bf16[256,1024]{1,0:T(8,128)(2,1)S(1)}, u32[]{:S(2)}, u32[]{:S(2)}) collective-permute-start(bf16[256,1024]{1,0:T(8,128)(2,1)} %copy-done.14), channel_id=1, source_target_pairs={{0,6},{1,7},{2,0},{3,1},{4,2},{5,3},{6,4},{7,5},{8,14},{9,15},{10,... | collective-permute-start | bytes 1572872 | tf_op jit(solution)/shard_map/ppermute | solution.py:567
  127.2 16.9 %all-to-all-start.3 = ((bf16[16,16,1024]{2,1,0:T(8,128)(2,1)}), bf16[16,16,1024]{2,1,0:T(8,128)(2,1)S(1)}, u32[]{:S(2)}, u32[]{:S(2)}) async-start(bf16[16,16,1024]{2,1,0:T(8,128)(2,1)} %bitcast.17), calls=%async_computation.3 | async-start | bytes 1048576 | tf_op jit(solution)/shard_map/all_to_all | solution.py:575
  150.2 24.8 %copy-start.8 = (bf16[512,768]{1,0:T(8,128)(2,1)S(1)}, bf16[512,768]{1,0:T(8,128)(2,1)}, u32[]{:S(2)}) copy-start(bf16[512,768]{1,0:T(8,128)(2,1)} %copy-done.7) | copy-start | bytes 2359300
  (8 other events, 8.3 us)
